TPU v7x, 256 devices: a whole 4x4x8 slice. The times are simulated.
256 devices in a mesh: gx: 16 (over x, y), gy: 8 (over z), gz: 2 (over core).
Axes of the slice: x: 4, y: 4, z: 8, core: 2. Of those that a mesh axis runs over, the one named last changes fastest.
Arguments:
- right_side: float32 [16, 256, 2048], P('gz', 'gx', 'gy'), may hold values from -5 to 5
- conductivity: float32 [16, 256, 2048], P('gz', 'gx', 'gy'), may hold values from 0.1 to 10
- storage: float32 [16, 256, 2048], P('gz', 'gx', 'gy'), may hold values from 0.05 to 0.5
- basis: bfloat16 [8, 16, 256, 2048], P(None, 'gz', 'gx', 'gy'), may hold values from -1.25 to 1.25
Outputs:
- solution_field: float32 [16, 256, 2048], P('gz', 'gx', 'gy')
- residual: float32 [16, 256, 2048], P('gz', 'gx', 'gy')
- direction: float32 [16, 256, 2048], P('gz', 'gx', 'gy')
All inputs are finite; a program needn't handle non-finite values.
Results may differ from a plain program's by a relative error of at most 0.0003.
Values may be sent and summed in bfloat16 or wider, within the bound.
No kernel may reach another device: no remote copies, remote signals or barrier semaphores. Data moves between devices by JAX's collectives and lax.ppermute only.
A program may use at most 64 MiB of HBM per device.

v0:
```python
import jax
import jax.numpy as jnp
from jax import lax
from jax.sharding import PartitionSpec as P

KITERS = 6


HIGHEST = lax.Precision.HIGHEST
RELAXATION = 0.6


def with_halo(block, sides, width):
    for axis, dim in sides:
        count = lax.axis_size(axis)
        forward = [(i, i + 1) for i in range(count - 1)]
        backward = [(target, source) for source, target in forward]
        low = lax.ppermute(
            lax.slice_in_dim(block, block.shape[dim] - width, None, axis=dim), axis, forward
        )
        high = lax.ppermute(lax.slice_in_dim(block, 0, width, axis=dim), axis, backward)
        block = jnp.concatenate([low, block, high], axis=dim)
    return block


def neighbours(padded):
    return [
        padded[..., :-2, 1:-1, 1:-1],
        padded[..., 2:, 1:-1, 1:-1],
        padded[..., 1:-1, :-2, 1:-1],
        padded[..., 1:-1, 2:, 1:-1],
        padded[..., 1:-1, 1:-1, :-2],
        padded[..., 1:-1, 1:-1, 2:],
    ]


def pad_cells(field):
    widths = [(0, 0)] * (field.ndim - 3) + [(1, 1)] * 3
    return jnp.pad(field, widths)


def harmonic(conductivity, padded):
    return [2.0 * conductivity * other / (conductivity + other) for other in neighbours(padded)]


def stencil(field, padded, weights, diagonal):
    total = diagonal * field
    for weight, other in zip(weights, neighbours(padded)):
        total = total - weight * other
    return total


def operate(field, weights, diagonal):
    padded = with_halo(field, (("gx", 1), ("gy", 2), ("gz", 0)), 1)
    return stencil(field, padded, weights, diagonal)


def face_tile(weight_face, own_face, other_face):
    return -jnp.einsum(
        "ij,aij,bij->ab",
        weight_face,
        own_face.astype(jnp.float32),
        other_face.astype(jnp.float32),
        precision=HIGHEST,
    )


def local_tiles(basis, outer_basis, weights, diagonal):
    basis_float = basis.astype(jnp.float32)
    image = stencil(basis_float, pad_cells(basis_float), weights, diagonal)
    tiles = [jnp.einsum("aijk,bijk->ab", basis_float, image, precision=HIGHEST)]
    tiles.append(face_tile(weights[0][0], basis[:, 0], outer_basis[:, 0, 1:-1, 1:-1]))
    tiles.append(face_tile(weights[1][-1], basis[:, -1], outer_basis[:, -1, 1:-1, 1:-1]))
    tiles.append(face_tile(weights[2][:, 0], basis[:, :, 0], outer_basis[:, 1:-1, 0, 1:-1]))
    tiles.append(face_tile(weights[3][:, -1], basis[:, :, -1], outer_basis[:, 1:-1, -1, 1:-1]))
    tiles.append(face_tile(weights[4][:, :, 0], basis[:, :, :, 0], outer_basis[:, 1:-1, 1:-1, 0]))
    tiles.append(
        face_tile(weights[5][:, :, -1], basis[:, :, :, -1], outer_basis[:, 1:-1, 1:-1, -1])
    )
    return jnp.stack(tiles)


def spread_apply(tiles, values):
    beside_all = with_halo(
        values.reshape(1, 1, 1, values.shape[0]), (("gx", 1), ("gy", 2), ("gz", 0)), 1
    )
    stacked = jnp.stack(
        [
            values,
            beside_all[0, 1, 1],
            beside_all[2, 1, 1],
            beside_all[1, 0, 1],
            beside_all[1, 2, 1],
            beside_all[1, 1, 0],
            beside_all[1, 1, 2],
        ]
    )
    return jnp.einsum("oab,ob->a", tiles, stacked, precision=HIGHEST)


def global_total(values):
    return lax.psum(jnp.sum(values), ("gx", "gy", "gz"))


def coarse_iterate(apply_fn, total_fn, source):
    solution = jnp.zeros_like(source)
    remainder = source
    search = source
    current = total_fn(remainder * remainder)
    for iteration in range(KITERS):
        image = apply_fn(search)
        step_size = current / total_fn(search * image)
        solution = solution + step_size * search
        remainder = remainder - step_size * image
        updated = total_fn(remainder * remainder)
        search = remainder + updated / current * search
        current = updated
    return solution


def coarse_values(coarse_tiles, source):
    return coarse_iterate(lambda values: spread_apply(coarse_tiles, values), global_total, source)


def precondition(field, weights, diagonal, basis_float, coarse_tiles):
    first = RELAXATION * field / diagonal
    second = first + RELAXATION * (field - operate(first, weights, diagonal)) / diagonal
    source = jnp.einsum("aijk,ijk->a", basis_float, field, precision=HIGHEST)
    coarse = coarse_values(coarse_tiles, source)
    return second + jnp.einsum("aijk,a->ijk", basis_float, coarse, precision=HIGHEST)


def inner_total(left, right):
    return lax.psum(jnp.sum(left * right), ("gx", "gy", "gz"))


def local(right_side, conductivity, storage, basis):
    padded_cond = with_halo(conductivity, (("gx", 1), ("gy", 2), ("gz", 0)), 1)
    weights = harmonic(conductivity, padded_cond)
    diagonal = storage + sum(weights)
    outer_basis = with_halo(basis, (("gx", 2), ("gy", 3), ("gz", 1)), 1)
    tiles = local_tiles(basis, outer_basis, weights, diagonal)
    basis_float = basis.astype(jnp.float32)
    preconditioned = precondition(right_side, weights, diagonal, basis_float, tiles)
    inner_first = inner_total(right_side, preconditioned)
    image = operate(preconditioned, weights, diagonal)
    curvature = lax.psum(jnp.sum(preconditioned * image), ("gx", "gy", "gz"))
    step_size = inner_first / curvature
    solution_field = step_size * preconditioned
    residual = right_side - step_size * image
    refined = precondition(residual, weights, diagonal, basis_float, tiles)
    growth = inner_total(residual, refined) / inner_first
    direction = refined + growth * preconditioned
    return (solution_field, residual, direction)


def solution(mesh):
    return jax.shard_map(
        local,
        mesh=mesh,
        in_specs=(
            P("gz", "gx", "gy"),
            P("gz", "gx", "gy"),
            P("gz", "gx", "gy"),
            P(None, "gz", "gx", "gy"),
        ),
        out_specs=(P("gz", "gx", "gy"), P("gz", "gx", "gy"), P("gz", "gx", "gy")),
        check_vma=False,
    )
```

profile of v0, /device:TPU:1, one launch (start us, length us, event | category | flops | bytes accessed | tf_op | source)
XLA Modules:
  0.0 2261.2 jit_solution(8455379297949303143)
XLA Ops:
  89.1 85.1 %all-reduce.3 = (f32[]{:T(128)}, f32[]{:T(128)}) all-reduce(f32[]{:T(128)} %get-tuple-element.14, f32[]{:T(128)} %get-tuple-element.13), channel_id=1, replica_groups=mesh['gx'=16,'gy'=8,'gz'=2] {'gx','gy','gz'}, use_global_device_ids=true, to_apply=%region_1.2 | all-reduce | flops 2 | bytes 16 | tf_op jit(solution)/shard_map/psum | solution.py:102
  176.2 73.4 %psum.191 = f32[]{:T(128)} all-reduce(f32[]{:T(128)} %get-tuple-element.40), channel_id=1, replica_groups=mesh['gx'=16,'gy'=8,'gz'=2] {'gx','gy','gz'}, use_global_device_ids=true, to_apply=%region_5.6 | all-reduce | flops 1 | bytes 8 | tf_op jit(solution)/shard_map/psum | solution.py:102
  266.0 5.4 collective-permute-start.29
  275.3 77.2 %psum.192 = f32[]{:T(128)} all-reduce(f32[]{:T(128)} %get-tuple-element.87), channel_id=1, replica_groups=mesh['gx'=16,'gy'=8,'gz'=2] {'gx','gy','gz'}, use_global_device_ids=true, to_apply=%region_7.8 | all-reduce | flops 1 | bytes 8 | tf_op jit(solution)/shard_map/psum | solution.py:102
  354.4 73.4 %psum.193 = f32[]{:T(128)} all-reduce(f32[]{:T(128)} %get-tuple-element.38), channel_id=1, replica_groups=mesh['gx'=16,'gy'=8,'gz'=2] {'gx','gy','gz'}, use_global_device_ids=true, to_apply=%region_9.10 | all-reduce | flops 1 | bytes 8 | tf_op jit(solution)/shard_map/psum | solution.py:102
  444.5 5.4 collective-permute-start.35
  453.7 76.7 %psum.194 = f32[]{:T(128)} all-reduce(f32[]{:T(128)} %get-tuple-element.89), channel_id=1, replica_groups=mesh['gx'=16,'gy'=8,'gz'=2] {'gx','gy','gz'}, use_global_device_ids=true, to_apply=%region_11.12 | all-reduce | flops 1 | bytes 8 | tf_op jit(solution)/shard_map/psum | solution.py:102
  532.4 73.4 %psum.195 = f32[]{:T(128)} all-reduce(f32[]{:T(128)} %get-tuple-element.36), channel_id=1, replica_groups=mesh['gx'=16,'gy'=8,'gz'=2] {'gx','gy','gz'}, use_global_device_ids=true, to_apply=%region_13.14 | all-reduce | flops 1 | bytes 8 | tf_op jit(solution)/shard_map/psum | solution.py:102
  622.5 5.4 collective-permute-start.41
  631.7 76.7 %psum.196 = f32[]{:T(128)} all-reduce(f32[]{:T(128)} %get-tuple-element.91), channel_id=1, replica_groups=mesh['gx'=16,'gy'=8,'gz'=2] {'gx','gy','gz'}, use_global_device_ids=true, to_apply=%region_15.16 | all-reduce | flops 1 | bytes 8 | tf_op jit(solution)/shard_map/psum | solution.py:102
  710.4 73.4 %psum.197 = f32[]{:T(128)} all-reduce(f32[]{:T(128)} %get-tuple-element.34), channel_id=1, replica_groups=mesh['gx'=16,'gy'=8,'gz'=2] {'gx','gy','gz'}, use_global_device_ids=true, to_apply=%region_17.18 | all-reduce | flops 1 | bytes 8 | tf_op jit(solution)/shard_map/psum | solution.py:102
  800.5 5.4 collective-permute-start.47
  809.7 76.7 %psum.198 = f32[]{:T(128)} all-reduce(f32[]{:T(128)} %get-tuple-element.93), channel_id=1, replica_groups=mesh['gx'=16,'gy'=8,'gz'=2] {'gx','gy','gz'}, use_global_device_ids=true, to_apply=%region_19.20 | all-reduce | flops 1 | bytes 8 | tf_op jit(solution)/shard_map/psum | solution.py:102
  889.7 73.9 %psum.199 = f32[]{:T(128)} all-reduce(f32[]{:T(128)} %multiply_reduce_fusion.12), channel_id=1, replica_groups=mesh['gx'=16,'gy'=8,'gz'=2] {'gx','gy','gz'}, use_global_device_ids=true, to_apply=%region_21.22 | all-reduce | flops 1 | bytes 8 | tf_op jit(solution)/shard_map/psum | solution.py:102
  979.8 5.4 collective-permute-start.53
  991.1 76.8 %psum.200 = f32[]{:T(128)} all-reduce(f32[]{:T(128)} %fusion.34), channel_id=1, replica_groups=mesh['gx'=16,'gy'=8,'gz'=2] {'gx','gy','gz'}, use_global_device_ids=true, to_apply=%region_23.24 | all-reduce | flops 1 | bytes 8 | tf_op jit(solution)/shard_map/psum | solution.py:102
  1087.0 5.4 collective-permute-start.59
  1094.1 78.1 %all-reduce.2 = (f32[]{:T(128)}, f32[]{:T(128)}) all-reduce(f32[]{:T(128)} %get-tuple-element.10, f32[]{:T(128)} %get-tuple-element.9), channel_id=1, replica_groups=mesh['gx'=16,'gy'=8,'gz'=2] {'gx','gy','gz'}, use_global_device_ids=true, to_apply=%region_25.26 | all-reduce | flops 2 | bytes 16 | tf_op jit(solution)/shard_map/psum | solution.py:134
  1197.9 79.3 %all-reduce.1 = (f32[]{:T(128)}, f32[]{:T(128)}) all-reduce(f32[]{:T(128)} %get-tuple-element.12, f32[]{:T(128)} %get-tuple-element.11), channel_id=1, replica_groups=mesh['gx'=16,'gy'=8,'gz'=2] {'gx','gy','gz'}, use_global_device_ids=true, to_apply=%region_29.30 | all-reduce | flops 2 | bytes 16 | tf_op jit(solution)/shard_map/psum | solution.py:102
  1279.1 73.5 %psum.205 = f32[]{:T(128)} all-reduce(f32[]{:T(128)} %get-tuple-element.29), channel_id=1, replica_groups=mesh['gx'=16,'gy'=8,'gz'=2] {'gx','gy','gz'}, use_global_device_ids=true, to_apply=%region_33.34 | all-reduce | flops 1 | bytes 8 | tf_op jit(solution)/shard_map/psum | solution.py:102
  1369.3 5.4 collective-permute-start.77
  1378.6 76.7 %psum.206 = f32[]{:T(128)} all-reduce(f32[]{:T(128)} %get-tuple-element.96), channel_id=1, replica_groups=mesh['gx'=16,'gy'=8,'gz'=2] {'gx','gy','gz'}, use_global_device_ids=true, to_apply=%region_35.36 | all-reduce | flops 1 | bytes 8 | tf_op jit(solution)/shard_map/psum | solution.py:102
  1457.2 73.4 %psum.207 = f32[]{:T(128)} all-reduce(f32[]{:T(128)} %get-tuple-element.27), channel_id=1, replica_groups=mesh['gx'=16,'gy'=8,'gz'=2] {'gx','gy','gz'}, use_global_device_ids=true, to_apply=%region_37.38 | all-reduce | flops 1 | bytes 8 | tf_op jit(solution)/shard_map/psum | solution.py:102
  1547.3 5.4 collective-permute-start.83
  1556.5 76.7 %psum.208 = f32[]{:T(128)} all-reduce(f32[]{:T(128)} %get-tuple-element.98), channel_id=1, replica_groups=mesh['gx'=16,'gy'=8,'gz'=2] {'gx','gy','gz'}, use_global_device_ids=true, to_apply=%region_39.40 | all-reduce | flops 1 | bytes 8 | tf_op jit(solution)/shard_map/psum | solution.py:102
  1635.2 73.4 %psum.209 = f32[]{:T(128)} all-reduce(f32[]{:T(128)} %get-tuple-element.25), channel_id=1, replica_groups=mesh['gx'=16,'gy'=8,'gz'=2] {'gx','gy','gz'}, use_global_device_ids=true, to_apply=%region_41.42 | all-reduce | flops 1 | bytes 8 | tf_op jit(solution)/shard_map/psum | solution.py:102
  1734.5 76.7 %psum.210 = f32[]{:T(128)} all-reduce(f32[]{:T(128)} %get-tuple-element.100), channel_id=1, replica_groups=mesh['gx'=16,'gy'=8,'gz'=2] {'gx','gy','gz'}, use_global_device_ids=true, to_apply=%region_43.44 | all-reduce | flops 1 | bytes 8 | tf_op jit(solution)/shard_map/psum | solution.py:102
  1813.2 73.4 %psum.211 = f32[]{:T(128)} all-reduce(f32[]{:T(128)} %get-tuple-element.23), channel_id=1, replica_groups=mesh['gx'=16,'gy'=8,'gz'=2] {'gx','gy','gz'}, use_global_device_ids=true, to_apply=%region_45.46 | all-reduce | flops 1 | bytes 8 | tf_op jit(solution)/shard_map/psum | solution.py:102
  1912.5 76.7 %psum.212 = f32[]{:T(128)} all-reduce(f32[]{:T(128)} %get-tuple-element.102), channel_id=1, replica_groups=mesh['gx'=16,'gy'=8,'gz'=2] {'gx','gy','gz'}, use_global_device_ids=true, to_apply=%region_47.48 | all-reduce | flops 1 | bytes 8 | tf_op jit(solution)/shard_map/psum | solution.py:102
  1992.5 75.8 %psum.213 = f32[]{:T(128)} all-reduce(f32[]{:T(128)} %multiply_reduce_fusion.3), channel_id=1, replica_groups=mesh['gx'=16,'gy'=8,'gz'=2] {'gx','gy','gz'}, use_global_device_ids=true, to_apply=%region_49.50 | all-reduce | flops 1 | bytes 8 | tf_op jit(solution)/shard_map/psum | solution.py:102
  2097.0 79.6 %psum.214 = f32[]{:T(128)} all-reduce(f32[]{:T(128)} %fusion.33), channel_id=1, replica_groups=mesh['gx'=16,'gy'=8,'gz'=2] {'gx','gy','gz'}, use_global_device_ids=true, to_apply=%region_51.52 | all-reduce | flops 1 | bytes 8 | tf_op jit(solution)/shard_map/psum | solution.py:102
  2184.3 73.9 %psum.215 = f32[]{:T(128)} all-reduce(f32[]{:T(128)} %get-tuple-element.21), channel_id=1, replica_groups=mesh['gx'=16,'gy'=8,'gz'=2] {'gx','gy','gz'}, use_global_device_ids=true, to_apply=%region_53.54 | all-reduce | flops 1 | bytes 8 | tf_op jit(solution)/shard_map/psum | solution.py:134
  (404 shorter events, 359.6 us)
Async XLA Ops:
  3.2 17.1 collective-permute-start.18
  7.2 13.1 collective-permute-start.19
  8.7 25.0 %collective-permute-start = (f32[8,1,256]{2,0,1:T(8,128)S(1)}, f32[8,1,256]{2,0,1:T(8,128)S(1)}, u32[]{:S(2)}, u32[]{:S(2)}) collective-permute-start(f32[8,1,256]{2,0,1:T(8,128)S(1)} %get-tuple-element.85), channel_id=1, source_target_pairs={{0,16},{16,32},{32,48},{48,64},{64,80},{80,96},{96,112},{112,128},... | collective-permute-start | bytes 24584 | tf_op jit(solution)/shard_map/ppermute | solution.py:18
  12.6 22.4 collective-permute-start.1
  15.1 47.4 %collective-permute-start.12 = (bf16[8,8,1,256]{3,0,2,1:T(8,128)(2,1)}, bf16[8,8,1,256]{3,0,2,1:T(8,128)(2,1)S(1)}, u32[]{:S(2)}, u32[]{:S(2)}) collective-permute-start(bf16[8,8,1,256]{3,0,2,1:T(8,128)(2,1)} %get-tuple-element.59), channel_id=1, source_target_pairs={{0,16},{16,32},{32,48},{48,64},{64,80},{80,96},{96,112},{112,128},... | collective-permute-start | bytes 98312 | tf_op jit(solution)/shard_map/ppermute | solution.py:18
  25.2 37.6 %collective-permute-start.13 = (bf16[8,8,1,256]{3,0,2,1:T(8,128)(2,1)}, bf16[8,8,1,256]{3,0,2,1:T(8,128)(2,1)}, u32[]{:S(2)}, u32[]{:S(2)}) collective-permute-start(bf16[8,8,1,256]{3,0,2,1:T(8,128)(2,1)} %get-tuple-element.58), channel_id=1, source_target_pairs={{16,0},{32,16},{48,32},{64,48},{80,64},{96,80},{112,96},{128,112},... | collective-permute-start | bytes 98312 | tf_op jit(solution)/shard_map/ppermute | solution.py:21
  28.4 10.3 collective-permute-start.23
  33.7 17.8 collective-permute-start.22
  57.2 12.6 collective-permute-start.6
  60.5 9.4 collective-permute-start.7
  63.7 12.5 collective-permute-start.14
  68.5 10.4 collective-permute-start.15
  70.6 14.6 collective-permute-start.8
  74.9 10.3 collective-permute-start.9
  266.0 6.7 collective-permute-start.29
  444.5 6.7 collective-permute-start.35
  622.5 6.7 collective-permute-start.41
  800.5 6.7 collective-permute-start.47
  888.4 181.5 %collective-permute-start.10 = (f32[1,18,258]{2,0,1:T(1,128)S(1)}, f32[1,18,258]{2,0,1:T(1,128)S(1)}, u32[]{:S(2)}, u32[]{:S(2)}) collective-permute-start(f32[1,18,258]{2,0,1:T(1,128)S(1)} %get-tuple-element.64), channel_id=1, source_target_pairs={{0,1},{2,3},{4,5},{6,7},{8,9},{10,11},{12,13},{14,15},{16,17},{18,... | collective-permute-start | bytes 55736 | tf_op jit(solution)/shard_map/ppermute | solution.py:18
  979.8 6.7 collective-permute-start.53
  989.0 80.9 %collective-permute-start.11 = (f32[1,18,258]{2,0,1:T(1,128)S(1)}, f32[1,18,258]{2,0,1:T(1,128)S(1)}, u32[]{:S(2)}, u32[]{:S(2)}) collective-permute-start(f32[1,18,258]{2,0,1:T(1,128)S(1)} %get-tuple-element.65), channel_id=1, source_target_pairs={{1,0},{3,2},{5,4},{7,6},{9,8},{11,10},{13,12},{15,14},{17,16},{19,... | collective-permute-start | bytes 55736 | tf_op jit(solution)/shard_map/ppermute | solution.py:21
  1085.7 6.7 collective-permute-start.58
  1175.2 8.5 collective-permute-start.66
  1179.7 912.8 %collective-permute-start.60 = (f32[8,1,256]{2,0,1:T(8,128)S(1)}, f32[8,1,256]{2,0,1:T(8,128)S(1)}, u32[]{:S(2)}, u32[]{:S(2)}) collective-permute-start(f32[8,1,256]{2,0,1:T(8,128)S(1)} %get-tuple-element.78), channel_id=1, source_target_pairs={{0,16},{16,32},{32,48},{48,64},{64,80},{80,96},{96,112},{112,128},... | collective-permute-start | bytes 24584 | tf_op jit(solution)/shard_map/ppermute | solution.py:18
  1369.3 6.7 collective-permute-start.77
  1547.3 6.7 collective-permute-start.83
  1725.3 6.7 collective-permute-start.89
  1903.3 6.7 collective-permute-start.95
  1991.2 101.3 %collective-permute-start.61 = (f32[8,1,256]{2,0,1:T(8,128)S(1)}, f32[8,1,256]{2,0,1:T(8,128)S(1)}, u32[]{:S(2)}, u32[]{:S(2)}) collective-permute-start(f32[8,1,256]{2,0,1:T(8,128)S(1)} %get-tuple-element.79), channel_id=1, source_target_pairs={{16,0},{32,16},{48,32},{64,48},{80,64},{96,80},{112,96},{128,112},... | collective-permute-start | bytes 24584 | tf_op jit(solution)/shard_map/ppermute | solution.py:21
  2083.9 6.7 collective-permute-start.101
  2092.5 85.4 %collective-permute-start.62 = (f32[8,18,1]{2,0,1:T(8,128)S(1)}, f32[8,18,1]{2,0,1:T(8,128)S(1)}, u32[]{:S(2)}, u32[]{:S(2)}) collective-permute-start(f32[8,18,1]{2,0,1:T(8,128)S(1)} %get-tuple-element.68), channel_id=1, source_target_pairs={{0,2},{2,4},{4,6},{6,8},{8,10},{10,12},{12,14},{1,3},{3,5},{5,7},{... | collective-permute-start | bytes 1736 | tf_op jit(solution)/shard_map/ppermute | solution.py:18
  2094.2 83.7 %collective-permute-start.63 = (f32[8,18,1]{2,0,1:T(8,128)S(1)}, f32[8,18,1]{2,0,1:T(8,128)S(1)}, u32[]{:S(2)}, u32[]{:S(2)}) collective-permute-start(f32[8,18,1]{2,0,1:T(8,128)S(1)} %get-tuple-element.69), channel_id=1, source_target_pairs={{2,0},{4,2},{6,4},{8,6},{10,8},{12,10},{14,12},{3,1},{5,3},{7,5},{... | collective-permute-start | bytes 1736 | tf_op jit(solution)/shard_map/ppermute | solution.py:21
  (78 other events, 402.2 us)
where the time goes:
time: 2280 us; the launch traced here: 2260 us
  blocking collectives  1820 us (80%)
  starting transfers between devices  260 us (11%)
  waiting for transfers between devices  99.5 us (4%)
  between operations  35 us (2%)
    psum x22, blocking collectives, global_total(): return lax.psum(jnp.sum(values), ('gx', 'gy', 'gz'))  1670 us
    psum x2, blocking collectives, inner_total(): return lax.psum(jnp.sum(left * right), ('gx', 'gy', 'gz'))  152 us
    ppermute x51, starting transfers between devices, with_halo(): lax.ppermute(lax.slice_in_dim(block, block.shape[dim] - width, None, axis...  134 us
    ppermute x51, starting transfers between devices, with_halo(): lax.ppermute(lax.slice_in_dim(block, 0, width, axis=dim), axis, backward)  126 us
    ppermute x51, waiting for transfers between devices, with_halo(): lax.ppermute(lax.slice_in_dim(block, 0, width, axis=dim), axis, backward)  80.3 us
  transfers between devices with their start and end apart: 102, of which 41 were waited for; matrix products, arithmetic and copies ran while one was open for 1% of the time, Pallas kernels for 0%

commit v1 on v0

v1 whole, which is shorter than its diff:
```python
import functools

import jax
import jax.numpy as jnp
from jax import lax
from jax.experimental import pallas as pl
from jax.experimental.pallas import tpu as pltpu
from jax.sharding import PartitionSpec as P

KITERS = 6
RELAXATION = 0.6
HIGHEST = lax.Precision.HIGHEST
AXES = ("gx", "gy", "gz")
CZ, CX, CY = 8, 16, 256
EZ, EX, EY = 12, 24, 384
NDEV = 256
PAIRS = [(a, b) for a in range(8) for b in range(a, 8)]
ROW_Z, ROW_Y, ROW_X, ROW_OWN, ROW_RS, ROW_SAS, ROW_G, ROW_H = 0, 64, 128, 192, 228, 229, 232, 240
VMEM_LIMIT = 48 * 1024 * 1024


def harmonic(k, other):
    return 2.0 * k * other / jnp.maximum(k + other, 1e-30)


def y_next(v):
    return pltpu.roll(v, v.shape[1] - 1, 1)


def y_prev(v):
    return pltpu.roll(v, 1, 1)


def x_next(v):
    return pltpu.roll(v, v.shape[0] - 1, 0)


def x_prev(v):
    return pltpu.roll(v, 1, 0)


def apply_at(z, v, v_up, v_down, diag, wx, wy, wz_up, wz_down):
    total = diag * v - wy * y_next(v) - y_prev(wy * v) - wx * x_next(v) - x_prev(wx * v)
    if v_up is not None:
        total = total - wz_up * v_up
    if v_down is not None:
        total = total - wz_down * v_down
    return total


def fold(v):
    return (v[:8, :128] + v[8:, :128]) + (v[:8, 128:] + v[8:, 128:])


def prepare_kernel(f_ref, b_ref, xa_ref, xb_ref, ya_ref, yb_ref, kx_ref, ky_ref,
                   pay_ref, wx_ref, wy_ref, wz_ref, dg_ref, iv_ref, s_ref, u_ref,
                   first_ref, acc_ref):
    acc_ref[...] = jnp.zeros_like(acc_ref)
    for z in range(11):
        k = f_ref[0, z]
        wy_ref[z] = harmonic(k, y_next(k))
        wx_ref[z] = harmonic(k, x_next(k))
        wz_ref[z] = harmonic(k, f_ref[0, z + 1])
    for z in range(11):
        wy, wx = wy_ref[z], wx_ref[z]
        diag = f_ref[1, z] + wy + y_prev(wy) + wx + x_prev(wx) + wz_ref[z]
        if z:
            diag = diag + wz_ref[z - 1]
        inverse = RELAXATION / jnp.maximum(diag, 1e-3)
        dg_ref[z] = diag
        iv_ref[z] = inverse
        first_ref[z] = inverse * f_ref[2, z]

    def at(z, ref):
        return apply_at(z, ref[z], ref[z + 1], ref[z - 1] if z else None, dg_ref[z], wx_ref[z],
                        wy_ref[z], wz_ref[z], wz_ref[z - 1] if z else None)

    for z in range(10):
        s_ref[z] = first_ref[z] + iv_ref[z] * (f_ref[2, z] - at(z, first_ref))
    for z in range(9):
        u_ref[z] = at(z, s_ref)

    rows = lax.broadcasted_iota(jnp.int32, (CX, CY), 0)
    lanes = lax.broadcasted_iota(jnp.int32, (CX, CY), 1)

    def add(row, value):
        acc_ref[8 * row:8 * row + 8, :] += value

    def own(ref, *lead):
        return ref[lead + (slice(0, CX), slice(0, CY))]

    def body(z, carry):
        r, s, u = own(f_ref, 2, z), own(s_ref, z), own(u_ref, z)
        diag = own(dg_ref, z)
        wy = jnp.where(lanes == CY - 1, 0.0, own(wy_ref, z))
        wx = jnp.where(rows == CX - 1, 0.0, own(wx_ref, z))
        up = jnp.minimum(z + 1, CZ - 1)
        down = jnp.maximum(z - 1, 0)
        wz_up = jnp.where(z < CZ - 1, own(wz_ref, z), 0.0)
        wz_down = jnp.where(z > 0, own(wz_ref, down), 0.0)
        add(ROW_RS, fold(r * s))
        add(ROW_SAS, fold(s * u))
        basis = [own(b_ref, a, z) for a in range(8)]
        for b in range(8):
            add(ROW_G + b, fold(basis[b] * r))
            add(ROW_H + b, fold(basis[b] * u))
            image = apply_at(z, basis[b], own(b_ref, b, up), own(b_ref, b, down), diag, wx, wy,
                             wz_up, wz_down)
            for a in range(b + 1):
                add(ROW_OWN + PAIRS.index((a, b)), fold(basis[a] * image))
        return carry

    lax.fori_loop(0, CZ, body, 0)

    wz_face = -own(wz_ref, CZ - 1)
    wx_face = -harmonic(kx_ref[0], kx_ref[1])
    wy_face = -harmonic(ky_ref[0], ky_ref[1])
    for a in range(8):
        za = wz_face * own(b_ref, a, CZ - 1)
        xa = wx_face * xa_ref[a]
        ya = wy_face * ya_ref[a]
        for b in range(8):
            row = 8 * b + a
            add(ROW_Z + row, fold(za * own(b_ref, b, CZ)))
            x = xa * xb_ref[b]
            add(ROW_X + row, x[:, :128] + x[:, 128:])
            acc_ref[8 * (ROW_Y + row):8 * (ROW_Y + row) + 8, 0:CX] = ya * yb_ref[b]

    total = acc_ref[pl.ds(0, 256, stride=8), :]
    for sub in range(1, 8):
        total = total + acc_ref[pl.ds(sub, 256, stride=8), :]
    summed = lax.dot_general(jnp.ones((8, 128), jnp.float32), total, (((1,), (1,)), ((), ())),
                             precision=HIGHEST, preferred_element_type=jnp.float32)
    pay_ref[...] = summed[0:1]


def total_of(v):
    return jnp.sum(jnp.sum(v, axis=1, keepdims=True), axis=0, keepdims=True)


def coarse_solve(tile_ref, lane_even):
    def partner(c):
        return jnp.where(lane_even, pltpu.roll(c, NDEV - 1, 1), pltpu.roll(c, 1, 1))

    def apply_e(c):
        shifted = [c, partner(c), pltpu.roll(c, NDEV - 2, 1), pltpu.roll(c, NDEV - 16, 1),
                   pltpu.roll(c, 2, 1), pltpu.roll(c, 16, 1)]
        total = None
        for o, v in enumerate(shifted):
            part = None
            for b in range(8):
                tile = (tile_ref[8 * (8 * o + b):8 * (8 * o + b) + 8, :])
                term = tile * v[b:b + 1, :]
                part = term if part is None else part + term
            total = part if total is None else total + part
        return total

    def solve(g):
        remainder, search, current = g, g, total_of(g * g)
        solution = jnp.zeros_like(g)
        for _ in range(KITERS):
            image = apply_e(search)
            step = current / total_of(search * image)
            solution = solution + step * search
            remainder = remainder - step * image
            updated = total_of(remainder * remainder)
            search = remainder + (updated / current) * search
            current = updated
        return solution

    return apply_e, solve


def coarse_kernel(dev_ref, gath_ref, f_ref, b_ref, wx_ref, wy_ref, wz_ref, dg_ref, iv_ref, s_ref, u_ref,
                  sol_ref, res_ref, pre_ref, refined_ref, part_ref, scal_ref,
                  t_ref, tile_ref, pc_ref, q_ref):
    dev = dev_ref[0]
    gz = lax.rem(dev, 2)
    turned = gath_ref[...].T
    t_ref[0] = turned[:, :128]
    t_ref[1] = turned[:, 128:]

    def rows_at(index):
        return jnp.concatenate([t_ref[0, index, :], t_ref[1, index, :]], axis=1)

    for b in range(8):
        for a in range(8):
            row = ROW_OWN + PAIRS.index((min(a, b), max(a, b)))
            tile_ref[8 * b + a:8 * b + a + 1, :] = turned[row:row + 1, :]
    tile_ref[64:256, :] = turned[0:192, :]
    for b in range(8):
        tile_ref[256 + 8 * b:264 + 8 * b, :] = pltpu.roll(rows_at(pl.ds(ROW_Y + b, 8, stride=8)), 2, 1)
        tile_ref[320 + 8 * b:328 + 8 * b, :] = pltpu.roll(rows_at(pl.ds(ROW_X + b, 8, stride=8)), 16, 1)
    lane = lax.broadcasted_iota(jnp.int32, (8, NDEV), 1)
    apply_e, solve = coarse_solve(tile_ref, lax.rem(lane, 2) == 0)
    g = turned[ROW_G:ROW_G + 8]
    h = turned[ROW_H:ROW_H + 8]
    rs = turned[ROW_RS:ROW_RS + 1]
    sas = turned[ROW_SAS:ROW_SAS + 1]
    c1 = solve(g)
    ec1 = apply_e(c1)
    rz = total_of(rs) + total_of(g * c1)
    curvature = total_of(sas) + total_of((2.0 * h + ec1) * c1)
    step = rz / curvature
    g2 = g - step * (h + ec1)
    c2 = solve(g2)
    g2c2 = total_of(g2 * c2)

    own_c = pltpu.roll(c1, lax.rem(NDEV - dev, NDEV), 1)
    other = dev + 1 - 2 * gz
    other_c = pltpu.roll(c1, lax.rem(NDEV - other, NDEV), 1)
    row = lax.broadcasted_iota(jnp.int32, (EX, EY), 0)
    col = lax.broadcasted_iota(jnp.int32, (EX, EY), 1)
    col_own, col_high = col < CY, col < CY + 64
    row_own, row_high = row < CX, row < CX + 4

    def field_of(c, b):
        def at(lane_index):
            lane_index %= NDEV
            return c[b:b + 1, lane_index:lane_index + 1]

        def along_y(base):
            return jnp.where(col_own, at(base), jnp.where(col_high, at(base + 2), at(base - 2)))

        return jnp.where(row_own, along_y(0), jnp.where(row_high, along_y(16), along_y(-16)))

    for b in range(8):
        mine = field_of(own_c, b)
        theirs = field_of(other_c, b)
        for z in range(10):
            value = b_ref[b, z] * (mine if z < CZ else theirs)
            if b:
                value = value + pc_ref[z]
            pc_ref[z] = value

    def at(z, ref):
        return apply_at(z, ref[z], ref[z + 1], ref[z - 1] if z else None, dg_ref[z], wx_ref[z],
                        wy_ref[z], wz_ref[z], wz_ref[z - 1] if z else None)

    def out_z(z):
        return z + gz * (CZ - 1 - 2 * z)

    def keep(ref, z, value):
        ref[pl.ds(out_z(z), 1)] = value[None, :CX, :CY]

    for z in range(9):
        image = u_ref[z] + at(z, pc_ref)
        residual = f_ref[2, z] - step * image
        q_ref[z] = iv_ref[z] * residual
        if z < CZ:
            keep(res_ref, z, residual)
            pre = s_ref[z, :CX, :CY] + pc_ref[z, :CX, :CY]
            keep(pre_ref, z, pre)
            keep(sol_ref, z, step * pre)
    own_c2 = pltpu.roll(c2, lax.rem(NDEV - dev, NDEV), 1)
    partial = jnp.zeros((8, 128), jnp.float32)
    for z in range(CZ):
        residual = res_ref[pl.ds(out_z(z), 1)][0]
        second = q_ref[z, :CX, :CY] + iv_ref[z, :CX, :CY] * (residual - at(z, q_ref)[:CX, :CY])
        partial = partial + fold(residual * second)
        for b in range(8):
            second = second + b_ref[b, z, :CX, :CY] * own_c2[b:b + 1, 0:1]
        keep(refined_ref, z, second)
    part_ref[...] = jnp.sum(partial, axis=0, keepdims=True)
    spot = lax.broadcasted_iota(jnp.int32, (1, 128), 1)
    scal_ref[...] = jnp.where(spot == 0, g2c2, rz)


def finish_kernel(parts_ref, scal_ref, refined_ref, pre_ref, out_ref):
    growth = (total_of(parts_ref[...]) + scal_ref[:, 0:1]) / scal_ref[:, 1:2]
    for z in range(CZ):
        out_ref[z] = refined_ref[z] + growth * pre_ref[z]


def call(kernel, out_shapes, scratch, n_args, smem_first=False):
    whole = pl.BlockSpec(memory_space=pltpu.VMEM)
    specs = [whole] * n_args
    if smem_first:
        specs[0] = pl.BlockSpec(memory_space=pltpu.SMEM)
    return pl.pallas_call(
        kernel,
        out_shape=[jax.ShapeDtypeStruct(s, jnp.float32) for s in out_shapes],
        in_specs=specs,
        out_specs=[whole] * len(out_shapes),
        scratch_shapes=[pltpu.VMEM(s, jnp.float32) for s in scratch],
        compiler_params=pltpu.CompilerParams(vmem_limit_bytes=VMEM_LIMIT),
    )


def ring(axis, to):
    n = lax.axis_size(axis)
    return [(i, (i + to) % n) for i in range(n)]


def gather_rows(row):
    rows = jnp.broadcast_to(row[None], (NDEV,) + row.shape)
    return lax.all_to_all(rows, AXES, 0, 0, tiled=False).reshape(NDEV, row.shape[-1])


def local(right_side, conductivity, storage, basis):
    gx, gy, gz = (lax.axis_index(a) for a in AXES)
    dev = (gx * 8 + gy) * 2 + gz
    fields = jnp.stack([conductivity, storage, right_side])
    fields = jnp.where(gz == 0, fields, fields[:, ::-1])
    basis = jnp.where(gz == 0, basis, basis[:, ::-1])
    only_k = (jnp.arange(3) == 0)[:, None, None, None]

    def halo(v, axis, dim, width):
        low = lax.ppermute(lax.slice_in_dim(v, v.shape[dim] - width, None, axis=dim), axis, ring(axis, 1))
        high = lax.ppermute(lax.slice_in_dim(v, 0, width, axis=dim), axis, ring(axis, -1))
        return low, high

    def clear(low, high, index, count):
        low = jnp.where(only_k & (index == 0), 0.0, low)
        high = jnp.where(only_k & (index == count - 1), 0.0, high)
        return low, high

    fx_low, fx_high = clear(*halo(fields, "gx", 2, 4), gx, 16)
    bx_low, bx_high = halo(basis, "gx", 2, 2)
    xa = basis[:, :, CX - 1].astype(jnp.float32)
    xb = bx_high[:, :, 0].astype(jnp.float32)
    kx = jnp.stack([fields[0, :, CX - 1], fx_high[0, :, 0]])
    fields_x = jnp.concatenate([fields, fx_high, fx_low], axis=2)
    gap = jnp.zeros(basis.shape[:2] + (4,) + basis.shape[3:], basis.dtype)
    basis_x = jnp.concatenate([basis, bx_high, gap, bx_low], axis=2)

    fy_low, fy_high = clear(*halo(fields_x, "gy", 3, 4), gy, 8)
    by_low, by_high = halo(basis_x, "gy", 3, 2)
    ya = basis[:, :, :, CY - 1].astype(jnp.float32)
    yb = by_high[:, :, :CX, 0].astype(jnp.float32)
    ky = jnp.stack([fields[0, :, :, CY - 1], fy_high[0, :, :CX, 0]])
    fields_y = jnp.concatenate([fields_x, fy_high, jnp.ones((3, CZ, EX, EY - CY - 8), jnp.float32), fy_low], axis=3)
    basis_y = jnp.concatenate(
        [basis_x, by_high, jnp.zeros((8, CZ, EX, EY - CY - 4), basis.dtype), by_low], axis=3)

    swap = [(0, 1), (1, 0)]
    fz = lax.ppermute(fields_y[:, 4:], "gz", swap)
    bz = lax.ppermute(basis_y[:, 6:], "gz", swap)
    fields_e = jnp.concatenate([fields_y, fz[:, ::-1]], axis=1)
    basis_e = jnp.concatenate([basis_y, bz[:, ::-1]], axis=1).astype(jnp.float32)

    ext = (EZ, EX, EY)
    pay, wx, wy, wz, dg, iv, s, u = call(
        prepare_kernel, [(1, 256)] + [ext] * 7, [ext, (2048, 128)], 8
    )(fields_e, basis_e, xa, xb, ya, yb, kx, ky)
    gathered = gather_rows(pay)
    box = (CZ, CX, CY)
    sol, res, pre, refined, part, scal = call(
        coarse_kernel, [box] * 4 + [(1, 128)] * 2,
        [(2, 256, 128), (384, 256), ext, ext], 11, True,
    )(dev.astype(jnp.int32).reshape(1), gathered, fields_e, basis_e, wx, wy, wz, dg, iv, s, u)
    parts = gather_rows(part)
    direction, = call(finish_kernel, [box], [], 4)(parts, scal, refined, pre)
    return sol, res, direction


def solution(mesh):
    spec = P("gz", "gx", "gy")
    return jax.shard_map(
        local,
        mesh=mesh,
        in_specs=(spec, spec, spec, P(None, "gz", "gx", "gy")),
        out_specs=(spec, spec, spec),
        check_vma=False,
    )
```

time: 2280 us -> 114 us (0.05)
  blocking collectives: 1820 us -> 18.2 us
  starting transfers between devices: 260 us -> 26.6 us
  waiting for transfers between devices: 99.5 us -> 35.1 us
  between operations: 35 us -> 0.97 us
    psum x24 -> x0, blocking collectives: 1820 us -> none  [the longest x22 1670 us: global_total(): return lax.psum(jnp.sum(values), ('gx', 'gy', 'gz'))]
    ppermute x102 -> x10, starting transfers between devices: 260 us -> 19.8 us  [the longest x4 11 us: halo(): lax.ppermute(lax.slice_in_dim(v, 0, width, axis=dim), axis, ring(axis, -1))]
    ppermute x102 -> x10, waiting for transfers between devices: 99.5 us -> 20.1 us  [the longest x4 12.1 us: halo(): lax.ppermute(lax.slice_in_dim(v, 0, width, axis=dim), axis, ring(axis, -1))]
  transfers between devices with their start and end apart: 102 -> 11, of which waited for: 41 -> 6; matrix products, arithmetic and copies ran while one was open for 1% -> 11% of each run, Pallas kernels for 0% -> 0%
where the time goes in v1:
time: 114 us
  waiting for transfers between devices  35.1 us (31%)
  starting transfers between devices  26.6 us (23%)
  blocking collectives  18.2 us (16%)
  Pallas kernels  12.2 us (11%)
  local copies, waits for them, and re-layouts  10.9 us (10%)
  other arithmetic  9.8 us (9%)
    all_to_all x1, blocking collectives, gather_rows(): lax.all_to_all(rows, AXES, 0, 0, tiled=False).reshape(NDEV, row.shape[-1])  18.2 us
    all_to_all x1, waiting for transfers between devices, gather_rows(): lax.all_to_all(rows, AXES, 0, 0, tiled=False).reshape(NDEV, row.shape[-1])  15.1 us
    ppermute x4, waiting for transfers between devices, halo(): lax.ppermute(lax.slice_in_dim(v, 0, width, axis=dim), axis, ring(axis, -1))  12.1 us
    ppermute x4, starting transfers between devices, halo(): lax.ppermute(lax.slice_in_dim(v, 0, width, axis=dim), axis, ring(axis, -1))  11 us
    ppermute x4, waiting for transfers between devices, halo(): lax.ppermute(lax.slice_in_dim(v, v.shape[dim] - width, None, axis=dim), a...  8 us
    all_to_all x1, starting transfers between devices, gather_rows(): lax.all_to_all(rows, AXES, 0, 0, tiled=False).reshape(NDEV, row.shape[-1])  6.76 us
    unnamed x28, local copies, waits for them, and re-layouts  6.5 us
    pallas_call x1, Pallas kernels, local(): call(coarse_kernel, [box] * 4 + [(1, 128)] * 2, [(2, 256, 128), (384, 256...  6.4 us
  transfers between devices with their start and end apart: 11, of which 6 were waited for; matrix products, arithmetic and copies ran while one was open for 11% of the time, Pallas kernels for 0%

profile of v1, /device:TPU:1, one launch (start us, length us, event | category | flops | bytes accessed | tf_op | source)
XLA Modules:
  0.0 113.8 jit_solution(12752896542211878106)
XLA Ops:
  0.6 1.1 pad_maximum_fusion.8
  1.8 2.2 %collective-permute-start.1 = (f32[3,8,4,256]{3,2,1,0:T(4,128)S(1)}, f32[3,8,4,256]{3,2,1,0:T(4,128)}, u32[]{:S(2)}, u32[]{:S(2)}) collective-permute-start(f32[3,8,4,256]{3,2,1,0:T(4,128)S(1)} %get-tuple-element.38), channel_id=1, source_target_pairs={{0,16},{16,32},{32,48},{48,64},{64,80},{80,96},{96,112},{112,128},... | collective-permute-start | bytes 294920 | tf_op jit(solution)/shard_map/ppermute | solution.py:309
  4.1 3.7 %collective-permute-start = (f32[3,8,4,256]{3,0,2,1:T(4,128)S(1)}, f32[3,8,4,256]{3,0,2,1:T(4,128)S(1)}, u32[]{:S(2)}, u32[]{:S(2)}) collective-permute-start(f32[3,8,4,256]{3,0,2,1:T(4,128)S(1)} %copy.22), channel_id=1, source_target_pairs={{0,240},{16,0},{32,16},{48,32},{64,48},{80,64},{96,80},{112,96},{1... | collective-permute-start | bytes 294920 | tf_op jit(solution)/shard_map/ppermute | solution.py:310
  8.1 1.5 %collective-permute-start.5 = (bf16[8,8,2,256]{3,2,1,0:T(2,128)(2,1)S(1)}, bf16[8,8,2,256]{3,2,1,0:T(2,128)(2,1)S(1)}, u32[]{:S(2)}, u32[]{:S(2)}) collective-permute-start(bf16[8,8,2,256]{3,2,1,0:T(2,128)(2,1)S(1)} %get-tuple-element.35), channel_id=1, source_target_pairs={{0,240},{16,0},{32,16},{48,32},{64,48},{80,64},{96,80},{112,96},{1... | collective-permute-start | bytes 196616 | tf_op jit(solution)/shard_map/ppermute | solution.py:310
  10.5 0.9 convert_reduce_fusion.1.ya_ref
  12.2 3.9 %collective-permute-done.6 = bf16[8,8,2,256]{3,2,1,0:T(2,128)(2,1)S(1)} collective-permute-done((bf16[8,8,2,256]{3,2,1,0:T(2,128)(2,1)S(1)}, bf16[8,8,2,256]{3,2,1,0:T(2,128)(2,1)S(1)}, u32[]{:S(2)}, u32[]{:S(2)}) %collective-permute-start.6) | collective-permute-done | bytes 65568 | tf_op jit(solution)/shard_map/ppermute | solution.py:309
  16.7 5.7 %collective-permute-start.7 = (bf16[8,8,24,2]{3,2,1,0:T(8,128)(2,1)S(1)}, bf16[8,8,24,2]{3,2,1,0:T(8,128)(2,1)S(1)}, u32[]{:S(2)}, u32[]{:S(2)}) collective-permute-start(bf16[8,8,24,2]{3,2,1,0:T(8,128)(2,1)S(1)} %get-tuple-element.31), channel_id=1, source_target_pairs={{0,14},{2,0},{4,2},{6,4},{8,6},{10,8},{12,10},{14,12},{1,15},{3,1}... | collective-permute-start | bytes 18440 | tf_op jit(solution)/shard_map/ppermute | solution.py:310
  23.0 5.0 %collective-permute-done.7 = bf16[8,8,24,2]{3,2,1,0:T(8,128)(2,1)S(1)} collective-permute-done((bf16[8,8,24,2]{3,2,1,0:T(8,128)(2,1)S(1)}, bf16[8,8,24,2]{3,2,1,0:T(8,128)(2,1)S(1)}, u32[]{:S(2)}, u32[]{:S(2)}) %collective-permute-start.7) | collective-permute-done | bytes 6176 | tf_op jit(solution)/shard_map/ppermute | solution.py:310
  28.0 3.1 %collective-permute-done.8 = bf16[8,8,24,2]{3,2,1,0:T(8,128)(2,1)S(1)} collective-permute-done((bf16[8,8,24,2]{3,2,1,0:T(8,128)(2,1)S(1)}, bf16[8,8,24,2]{3,2,1,0:T(8,128)(2,1)S(1)}, u32[]{:S(2)}, u32[]{:S(2)}) %collective-permute-start.8) | collective-permute-done | bytes 6176 | tf_op jit(solution)/shard_map/ppermute | solution.py:309
  31.4 4.0 %collective-permute-start.9 = (bf16[8,2,24,384]{3,2,1,0:T(8,128)(2,1)S(1)}, bf16[8,2,24,384]{3,2,1,0:T(8,128)(2,1)}, u32[]{:S(2)}, u32[]{:S(2)}) collective-permute-start(bf16[8,2,24,384]{3,2,1,0:T(8,128)(2,1)S(1)} %pad_maximum_fusion.9), channel_id=1, source_target_pairs={{0,1},{1,0},{2,3},{3,2},{4,5},{5,4},{6,7},{7,6},{8,9},{9,8},{10,11... | collective-permute-start | bytes 884744 | tf_op jit(solution)/shard_map/ppermute | solution.py:338
  35.4 0.8 convert_reduce_fusion.yb_ref
  36.4 1.0 broadcast_select_fusion.3
  37.7 1.5 %collective-permute-start.3 = (f32[3,8,24,4]{3,2,1,0:T(8,128)S(1)}, f32[3,8,24,4]{3,2,1,0:T(8,128)S(1)}, u32[]{:S(2)}, u32[]{:S(2)}) collective-permute-start(f32[3,8,24,4]{3,2,1,0:T(8,128)S(1)} %get-tuple-element.34), channel_id=1, source_target_pairs={{0,2},{2,4},{4,6},{6,8},{8,10},{10,12},{12,14},{14,0},{1,3},{3,5},... | collective-permute-start | bytes 27656 | tf_op jit(solution)/shard_map/ppermute | solution.py:309
  39.2 7.0 %collective-permute-done.2 = f32[3,8,24,4]{3,2,1,0:T(8,128)S(1)} collective-permute-done((f32[3,8,24,4]{3,2,1,0:T(8,128)S(1)}, f32[3,8,24,4]{3,2,1,0:T(8,128)S(1)}, u32[]{:S(2)}, u32[]{:S(2)}) %collective-permute-start.2) | collective-permute-done | bytes 9248 | tf_op jit(solution)/shard_map/ppermute | solution.py:310
  46.3 0.9 collective-permute-done.3
  47.4 0.9 pad_maximum_fusion.3
  48.3 1.1 collective-permute-start.4
  50.1 1.0 rev.15
  51.1 3.1 %maximum_convert_fusion.b_ref = f32[8,10,24,384]{3,2,1,0:T(8,128)} fusion(bf16[8,2,24,384]{3,2,1,0:T(8,128)(2,1)S(1)} %rev.15, bf16[8,8,24,2]{3,2,1,0:T(8,128)(2,1)} %copy-done.9, bf16[8,8,24,124]{3,2,1,0:T(8,128)(2,1)S(1)} %broadcast_in_dim.70, bf16[8,8,24,2]{3,2,1,0:T(8,128)(2,1)S(1)} %collective-permute-done.7, ...), kind=kLoop, calls=%fused_computation | loop fusion | flops 11796480 | bytes 4423680 | tf_op jit(solution)/shard_map/convert_element_type | solution.py:340
  54.2 1.0 rev.13
  56.1 4.9 %shard_map.67 = (f32[1,256]{1,0:T(1,128)S(1)}, f32[12,24,384]{2,1,0:T(8,128)S(1)}, f32[12,24,384]{2,1,0:T(8,128)S(1)}, f32[12,24,384]{2,1,0:T(8,128)S(1)}, f32[1...) custom-call(f32[3,12,24,384]{3,2,1,0:T(8,128)S(1)} %pad_maximum_fusi, ...), custom_call_target="tpu_custom_call" | custom-call | tf_op jit(solution)/shard_map/pallas_call | solution.py:343
  61.0 0.8 copy-done
  61.8 0.8 copy-done.2
  62.6 0.8 broadcast_in_dim.72
  63.4 6.8 %all-to-all-start = ((f32[256,1,256]{2,1,0:T(1,128)}), f32[256,1,256]{2,1,0:T(1,128)}, u32[]{:S(2)}, u32[]{:S(2)}) async-start(f32[256,1,256]{2,1,0:T(1,128)} %broadcast_in_dim.72), calls=%async_computation | async-start | bytes 524288 | tf_op jit(solution)/shard_map/all_to_all | solution.py:297
  70.2 15.1 %all-to-all-done = f32[256,1,256]{2,1,0:T(1,128)} async-done(((f32[256,1,256]{2,1,0:T(1,128)}), f32[256,1,256]{2,1,0:T(1,128)}, u32[]{:S(2)}, u32[]{:S(2)}) %all-to-all-start) | async-done | bytes 262176 | tf_op jit(solution)/shard_map/all_to_all | solution.py:297
  85.2 1.0 copy.26
  86.2 1.0 copy-done.1
  87.2 1.0 copy-done.3
  88.2 6.4 %shard_map.68 = (f32[8,16,256]{2,1,0:T(8,128)}, f32[8,16,256]{2,1,0:T(8,128)}, f32[8,16,256]{2,1,0:T(8,128)S(1)}, f32[8,16,256]{2,1,0:T(8,128)S(1)}, f32[1,128]{1,0:T(1,128)S(1)}, /*index=5*/f32[1,128]{1,0:T(1,128)S(1)}) custom-call(s32[1]{0:T(128)} %bitcast.dev_ref, f32[256,256]{1,0:T(8,128)S(1)} %bitcast.22, f32[3,12,24,384]{3,2,1,0:T(8,128)S(1)} %pad_maximum_fusion.f_ref, ...), custom_call_target="tpu_custom_call" | custom-call | tf_op jit(solution)/shard_map/pallas_call | solution.py:348
  94.7 18.2 %all_to_all.10 = f32[256,1,128]{2,1,0:T(1,128)S(1)} all-to-all(f32[256,1,128]{2,1,0:T(1,128)S(1)} %broadcast_in_dim.74), channel_id=1, replica_groups=mesh['gx'=16,'gy'=8,'gz'=2] {'gx','gy','gz'}, dimensions={0} | all-to-all | bytes 262144 | tf_op jit(solution)/shard_map/all_to_all | solution.py:297
  113.0 0.9 shard_map.69
  (62 shorter events, 5.6 us)
Async XLA Ops:
  0.6 7.2 %copy-start.10 = (bf16[8,8,16,256]{3,2,1,0:T(8,128)(2,1)S(1)}, bf16[8,8,16,256]{3,2,1,0:T(8,128)(2,1)}, u32[]{:S(2)}) copy-start(bf16[8,8,16,256]{3,2,1,0:T(8,128)(2,1)} %param.7) | copy-start | bytes 1572868
  1.8 34.5 %collective-permute-start.1 = (f32[3,8,4,256]{3,2,1,0:T(4,128)S(1)}, f32[3,8,4,256]{3,2,1,0:T(4,128)}, u32[]{:S(2)}, u32[]{:S(2)}) collective-permute-start(f32[3,8,4,256]{3,2,1,0:T(4,128)S(1)} %get-tuple-element.38), channel_id=1, source_target_pairs={{0,16},{16,32},{32,48},{48,64},{64,80},{80,96},{96,112},{112,128},... | collective-permute-start | bytes 294920 | tf_op jit(solution)/shard_map/ppermute | solution.py:309
  4.1 32.1 %collective-permute-start = (f32[3,8,4,256]{3,0,2,1:T(4,128)S(1)}, f32[3,8,4,256]{3,0,2,1:T(4,128)S(1)}, u32[]{:S(2)}, u32[]{:S(2)}) collective-permute-start(f32[3,8,4,256]{3,0,2,1:T(4,128)S(1)} %copy.22), channel_id=1, source_target_pairs={{0,240},{16,0},{32,16},{48,32},{64,48},{80,64},{96,80},{112,96},{1... | collective-permute-start | bytes 294920 | tf_op jit(solution)/shard_map/ppermute | solution.py:310
  8.1 4.0 %collective-permute-start.5 = (bf16[8,8,2,256]{3,2,1,0:T(2,128)(2,1)S(1)}, bf16[8,8,2,256]{3,2,1,0:T(2,128)(2,1)S(1)}, u32[]{:S(2)}, u32[]{:S(2)}) collective-permute-start(bf16[8,8,2,256]{3,2,1,0:T(2,128)(2,1)S(1)} %get-tuple-element.35), channel_id=1, source_target_pairs={{0,240},{16,0},{32,16},{48,32},{64,48},{80,64},{96,80},{112,96},{1... | collective-permute-start | bytes 196616 | tf_op jit(solution)/shard_map/ppermute | solution.py:310
  9.7 6.4 %collective-permute-start.6 = (bf16[8,8,2,256]{3,2,1,0:T(2,128)(2,1)S(1)}, bf16[8,8,2,256]{3,2,1,0:T(2,128)(2,1)S(1)}, u32[]{:S(2)}, u32[]{:S(2)}) collective-permute-start(bf16[8,8,2,256]{3,2,1,0:T(2,128)(2,1)S(1)} %get-tuple-element.36), channel_id=1, source_target_pairs={{0,16},{16,32},{32,48},{48,64},{64,80},{80,96},{96,112},{112,128},... | collective-permute-start | bytes 196616 | tf_op jit(solution)/shard_map/ppermute | solution.py:309
  16.7 11.4 %collective-permute-start.7 = (bf16[8,8,24,2]{3,2,1,0:T(8,128)(2,1)S(1)}, bf16[8,8,24,2]{3,2,1,0:T(8,128)(2,1)S(1)}, u32[]{:S(2)}, u32[]{:S(2)}) collective-permute-start(bf16[8,8,24,2]{3,2,1,0:T(8,128)(2,1)S(1)} %get-tuple-element.31), channel_id=1, source_target_pairs={{0,14},{2,0},{4,2},{6,4},{8,6},{10,8},{12,10},{14,12},{1,15},{3,1}... | collective-permute-start | bytes 18440 | tf_op jit(solution)/shard_map/ppermute | solution.py:310
  22.3 8.9 %collective-permute-start.8 = (bf16[8,8,24,2]{3,2,1,0:T(8,128)(2,1)S(1)}, bf16[8,8,24,2]{3,2,1,0:T(8,128)(2,1)S(1)}, u32[]{:S(2)}, u32[]{:S(2)}) collective-permute-start(bf16[8,8,24,2]{3,2,1,0:T(8,128)(2,1)S(1)} %get-tuple-element.32), channel_id=1, source_target_pairs={{0,2},{2,4},{4,6},{6,8},{8,10},{10,12},{12,14},{14,0},{1,3},{3,5},... | collective-permute-start | bytes 18440 | tf_op jit(solution)/shard_map/ppermute | solution.py:309
  31.2 8.0 %copy-start.9 = (bf16[8,8,24,2]{3,2,1,0:T(8,128)(2,1)}, bf16[8,8,24,2]{3,2,1,0:T(8,128)(2,1)S(1)}, u32[]{:S(2)}) copy-start(bf16[8,8,24,2]{3,2,1,0:T(8,128)(2,1)S(1)} %collective-permute-done.8) | copy-start | bytes 18436
  31.4 18.7 %collective-permute-start.9 = (bf16[8,2,24,384]{3,2,1,0:T(8,128)(2,1)S(1)}, bf16[8,2,24,384]{3,2,1,0:T(8,128)(2,1)}, u32[]{:S(2)}, u32[]{:S(2)}) collective-permute-start(bf16[8,2,24,384]{3,2,1,0:T(8,128)(2,1)S(1)} %pad_maximum_fusion.9), channel_id=1, source_target_pairs={{0,1},{1,0},{2,3},{3,2},{4,5},{5,4},{6,7},{7,6},{8,9},{9,8},{10,11... | collective-permute-start | bytes 884744 | tf_op jit(solution)/shard_map/ppermute | solution.py:338
  37.5 8.7 %collective-permute-start.2 = (f32[3,8,24,4]{3,2,1,0:T(8,128)S(1)}, f32[3,8,24,4]{3,2,1,0:T(8,128)S(1)}, u32[]{:S(2)}, u32[]{:S(2)}) collective-permute-start(f32[3,8,24,4]{3,2,1,0:T(8,128)S(1)} %get-tuple-element.33), channel_id=1, source_target_pairs={{0,14},{2,0},{4,2},{6,4},{8,6},{10,8},{12,10},{14,12},{1,15},{3,1}... | collective-permute-start | bytes 27656 | tf_op jit(solution)/shard_map/ppermute | solution.py:310
  37.7 9.6 %collective-permute-start.3 = (f32[3,8,24,4]{3,2,1,0:T(8,128)S(1)}, f32[3,8,24,4]{3,2,1,0:T(8,128)S(1)}, u32[]{:S(2)}, u32[]{:S(2)}) collective-permute-start(f32[3,8,24,4]{3,2,1,0:T(8,128)S(1)} %get-tuple-element.34), channel_id=1, source_target_pairs={{0,2},{2,4},{4,6},{6,8},{8,10},{10,12},{12,14},{14,0},{1,3},{3,5},... | collective-permute-start | bytes 27656 | tf_op jit(solution)/shard_map/ppermute | solution.py:309
  46.3 3.2 %copy-start.11 = (f32[8,16]{1,0:T(8,128)S(1)}, f32[8,16]{1,0:T(8,128)}, u32[]{:S(2)}) copy-start(f32[8,16]{1,0:T(8,128)} %slice_reduce_fusion.1) | copy-start | bytes 1540
  48.3 5.9 %collective-permute-start.4 = (f32[3,4,24,384]{3,2,1,0:T(8,128)}, f32[3,4,24,384]{3,2,1,0:T(8,128)}, u32[]{:S(2)}, u32[]{:S(2)}) collective-permute-start(f32[3,4,24,384]{3,2,1,0:T(8,128)} %pad_maximum_fusion.3), channel_id=1, source_target_pairs={{0,1},{1,0},{2,3},{3,2},{4,5},{5,4},{6,7},{7,6},{8,9},{9,8},{10,11... | collective-permute-start | bytes 1327112 | tf_op jit(solution)/shard_map/ppermute | solution.py:337
  55.2 0.8 copy-start.4
  55.2 0.9 copy-start.5
  55.2 0.9 copy-start.6
  55.3 0.8 copy-start.7
  55.3 0.8 copy-start.8
  61.0 0.8 copy-start
  61.8 0.8 copy-start.2
  63.4 21.8 %all-to-all-start = ((f32[256,1,256]{2,1,0:T(1,128)}), f32[256,1,256]{2,1,0:T(1,128)}, u32[]{:S(2)}, u32[]{:S(2)}) async-start(f32[256,1,256]{2,1,0:T(1,128)} %broadcast_in_dim.72), calls=%async_computation | async-start | bytes 524288 | tf_op jit(solution)/shard_map/all_to_all | solution.py:297
  86.2 1.0 copy-start.1
  87.2 1.0 copy-start.3

commit v2 on v1

--- a/solution.py
+++ b/solution.py
@@ -16,7 +16,9 @@
 NDEV = 256
 PAIRS = [(a, b) for a in range(8) for b in range(a, 8)]
 ROW_Z, ROW_Y, ROW_X, ROW_OWN, ROW_RS, ROW_SAS, ROW_G, ROW_H = 0, 64, 128, 192, 228, 229, 232, 240
-VMEM_LIMIT = 48 * 1024 * 1024
+X_ROWS = 26
+ST_LANE, R_LANE, FACE_LANE = 32, 56, 80
+VMEM_LIMIT = 24 * 1024 * 1024
 
 
 def harmonic(k, other):
@@ -52,31 +54,147 @@
     return (v[:8, :128] + v[8:, :128]) + (v[:8, 128:] + v[8:, 128:])
 
 
-def prepare_kernel(f_ref, b_ref, xa_ref, xb_ref, ya_ref, yb_ref, kx_ref, ky_ref,
-                   pay_ref, wx_ref, wy_ref, wz_ref, dg_ref, iv_ref, s_ref, u_ref,
-                   first_ref, acc_ref):
+def pack_x_kernel(pos_ref, k_ref, st_ref, r_ref, b_ref, hi_ref, lo_ref, q_ref):
+    gz = pos_ref[2]
+    for z in range(CZ):
+        src = z + gz * (CZ - 1 - 2 * z)
+        base, j = X_ROWS * z, CZ - 1 - z
+        k, st, r = (ref[pl.ds(src, 1)][0] for ref in (k_ref, st_ref, r_ref))
+        hi_ref[base:base + 4, :] = k[12:16]
+        lo_ref[base:base + 4, :] = k[0:4]
+        hi_ref[base + 4:base + 7, :] = st[13:16]
+        lo_ref[base + 4:base + 7, :] = st[0:3]
+        hi_ref[base + 7:base + 10, :] = r[13:16]
+        lo_ref[base + 7:base + 10, :] = r[0:3]
+        if j < 4:
+            q_ref[j] = k
+        if j < 3:
+            q_ref[4 + j] = st
+            q_ref[7 + j] = r
+        for a in range(8):
+            v = b_ref[a, pl.ds(src, 1)][0].astype(jnp.float32)
+            row = base + 10 + 2 * a
+            hi_ref[row:row + 2, :] = v[14:16]
+            lo_ref[row:row + 2, :] = v[0:2]
+            if j < 2:
+                q_ref[10 + 2 * a + j] = v
+
+
+def flag(inside):
+    return jnp.where(inside, 1.0, 0.0).astype(jnp.float32)
+
+
+def pack_y_kernel(pos_ref, k_ref, st_ref, r_ref, b_ref, xh_ref, xl_ref, hi_ref, lo_ref, edge_ref):
+    gx, gz = pos_ref[0], pos_ref[2]
+    x_high, x_low = flag(gx < 15), flag(gx > 0)
+    lane = lax.broadcasted_iota(jnp.int32, (EX, 128), 1)
+    edge_ref[...] = jnp.ones_like(edge_ref)
+    out = {}
+
+    def put(side, half, tile, source, width, offset):
+        rolled = pltpu.roll(tile, (offset - source) % 128, 1)
+        mask = (lane >= offset) & (lane < offset + width)
+        old = out.get((side, half), 0.0)
+        out[side, half] = jnp.where(mask, rolled, old)
+
+    def both(slot, main, half, base, width, offset, mul_h=None, mul_l=None):
+        xh, xl = xh_ref[base:base + width, :], xl_ref[base:base + width, :]
+        if mul_h is not None:
+            xh, xl = xh * mul_h, xl * mul_l
+        edge_ref[slot, 0:width, :] = xh
+        edge_ref[slot, 8 - width:8, :] = xl
+        full = jnp.concatenate([main, edge_ref[slot]], axis=0)
+        put("hi", half, full[:, 128:], 128 - width, width, offset)
+        put("lo", half, full[:, :128], 0, width, offset)
+        return full
+
+    for z in range(CZ):
+        src = z + gz * (CZ - 1 - 2 * z)
+        base = X_ROWS * z
+        k, st, r = (ref[pl.ds(src, 1)][0] for ref in (k_ref, st_ref, r_ref))
+        full = both(z, k, 0, base, 4, 4 * z, x_high, x_low)
+        put("hi", 0, full[:, 128:], 127, 1, FACE_LANE + 2 * z + 1)
+        put("lo", 0, full[:, :128], 0, 1, FACE_LANE + 2 * z + 1)
+        both(8 + z, st, 0, base + 4, 3, ST_LANE + 3 * z)
+        both(16 + z, r, 0, base + 7, 3, R_LANE + 3 * z)
+        for a in range(8):
+            v = b_ref[a, pl.ds(src, 1)][0].astype(jnp.float32)
+            both(24 + 8 * a + z, v, 1, base + 10 + 2 * a, 2, 16 * a + 2 * z)
+    for half in range(2):
+        hi_ref[:, 128 * half:128 * half + 128] = out["hi", half]
+        lo_ref[:, 128 * half:128 * half + 128] = out["lo", half]
+
+
+def prepare_kernel(pos_ref, k_in, st_in, r_in, b_in, q_ref, xh_ref, xl_ref, xhq_ref, xlq_ref,
+                   ys_ref, yh_ref, yl_ref, yhq_ref, ylq_ref,
+                   pay_ref, r_ref, b_ref, wx_ref, wy_ref, wz_ref, dg_ref, iv_ref, s_ref, u_ref,
+                   k_ref, st_ref, first_ref, acc_ref, xa_ref, xb_ref, wf_ref):
+    gx, gy, gz = pos_ref[0], pos_ref[1], pos_ref[2]
+    x_high, x_low = flag(gx < 15), flag(gx > 0)
+    y_high, y_low = flag(gy < 7), flag(gy > 0)
+    lane = lax.broadcasted_iota(jnp.int32, (EX, 128), 1)
+
+    def assemble(ref, index, main, halos, base, width, half, offset, masked=False):
+        xh, xl, yh, yl = halos
+        xh, xl = xh[base:base + width, :], xl[base:base + width, :]
+        columns = slice(128 * half, 128 * half + 128)
+        yh = pltpu.roll(yh[:, columns], -offset % 128, 1)
+        yl = pltpu.roll(yl[:, columns], (128 - width - offset) % 128, 1)
+        if masked:
+            xh, xl, yh, yl = xh * x_high, xl * x_low, yh * y_high, yl * y_low
+        ref[index + (slice(0, CX), slice(0, CY))] = main
+        if width < 4:
+            ref[index + (slice(CX, EX), slice(0, CY))] = jnp.ones((8, CY), jnp.float32)
+        ref[index + (slice(CX, CX + width), slice(0, CY))] = xh
+        ref[index + (slice(EX - width, EX), slice(0, CY))] = xl
+        ref[index + (slice(0, EX), slice(CY, EY))] = jnp.where(
+            lane < width, yh, jnp.where(lane >= 128 - width, yl, 1.0))
+
+    own_halos = (xh_ref, xl_ref, yh_ref, yl_ref)
+    for z in range(CZ):
+        src = z + gz * (CZ - 1 - 2 * z)
+        base = X_ROWS * z
+        assemble(k_ref, (z,), k_in[pl.ds(src, 1)][0], own_halos, base, 4, 0, 4 * z, True)
+        assemble(st_ref, (z,), st_in[pl.ds(src, 1)][0], own_halos, base + 4, 3, 0, ST_LANE + 3 * z)
+        assemble(r_ref, (z,), r_in[pl.ds(src, 1)][0], own_halos, base + 7, 3, 0, R_LANE + 3 * z)
+        for a in range(8):
+            v = b_in[a, pl.ds(src, 1)][0].astype(jnp.float32)
+            assemble(b_ref, (a, z), v, own_halos, base + 10 + 2 * a, 2, 1, 16 * a + 2 * z)
+    other_halos = (xhq_ref, xlq_ref, yhq_ref, ylq_ref)
+    for j in range(4):
+        z, theirs = CZ + j, CZ - 1 - j
+        base = X_ROWS * (theirs - 4)
+        assemble(k_ref, (z,), q_ref[j], other_halos, base, 4, 0, 4 * theirs, True)
+        if j < 3:
+            assemble(st_ref, (z,), q_ref[4 + j], other_halos, base + 4, 3, 0, ST_LANE + 3 * theirs)
+            assemble(r_ref, (z,), q_ref[7 + j], other_halos, base + 7, 3, 0, R_LANE + 3 * theirs)
+        if j < 2:
+            for a in range(8):
+                assemble(b_ref, (a, z), q_ref[10 + 2 * a + j], other_halos, base + 10 + 2 * a, 2, 1,
+                         16 * a + 2 * theirs)
+
     acc_ref[...] = jnp.zeros_like(acc_ref)
     for z in range(11):
-        k = f_ref[0, z]
+        k = k_ref[z]
         wy_ref[z] = harmonic(k, y_next(k))
         wx_ref[z] = harmonic(k, x_next(k))
-        wz_ref[z] = harmonic(k, f_ref[0, z + 1])
+        wz_ref[z] = harmonic(k, k_ref[z + 1])
     for z in range(11):
         wy, wx = wy_ref[z], wx_ref[z]
-        diag = f_ref[1, z] + wy + y_prev(wy) + wx + x_prev(wx) + wz_ref[z]
+        diag = st_ref[z] + wy + y_prev(wy) + wx + x_prev(wx) + wz_ref[z]
         if z:
             diag = diag + wz_ref[z - 1]
         inverse = RELAXATION / jnp.maximum(diag, 1e-3)
         dg_ref[z] = diag
         iv_ref[z] = inverse
-        first_ref[z] = inverse * f_ref[2, z]
+        first_ref[z] = inverse * r_ref[z]
 
     def at(z, ref):
         return apply_at(z, ref[z], ref[z + 1], ref[z - 1] if z else None, dg_ref[z], wx_ref[z],
                         wy_ref[z], wz_ref[z], wz_ref[z - 1] if z else None)
 
     for z in range(10):
-        s_ref[z] = first_ref[z] + iv_ref[z] * (f_ref[2, z] - at(z, first_ref))
+        s_ref[z] = first_ref[z] + iv_ref[z] * (r_ref[z] - at(z, first_ref))
     for z in range(9):
         u_ref[z] = at(z, s_ref)
 
@@ -90,7 +208,7 @@
         return ref[lead + (slice(0, CX), slice(0, CY))]
 
     def body(z, carry):
-        r, s, u = own(f_ref, 2, z), own(s_ref, z), own(u_ref, z)
+        r, s, u = own(r_ref, z), own(s_ref, z), own(u_ref, z)
         diag = own(dg_ref, z)
         wy = jnp.where(lanes == CY - 1, 0.0, own(wy_ref, z))
         wx = jnp.where(rows == CX - 1, 0.0, own(wx_ref, z))
@@ -112,26 +230,45 @@
 
     lax.fori_loop(0, CZ, body, 0)
 
+    for z in range(CZ):
+        wf_ref[z:z + 1, :] = -wx_ref[z, CX - 1:CX, 0:CY]
+        for a in range(8):
+            xa_ref[a, z:z + 1, :] = b_ref[a, z, CX - 1:CX, 0:CY]
+            xb_ref[a, z:z + 1, :] = b_ref[a, z, CX:CX + 1, 0:CY]
     wz_face = -own(wz_ref, CZ - 1)
-    wx_face = -harmonic(kx_ref[0], kx_ref[1])
-    wy_face = -harmonic(ky_ref[0], ky_ref[1])
+    wx_face = wf_ref[...]
     for a in range(8):
         za = wz_face * own(b_ref, a, CZ - 1)
         xa = wx_face * xa_ref[a]
-        ya = wy_face * ya_ref[a]
         for b in range(8):
             row = 8 * b + a
             add(ROW_Z + row, fold(za * own(b_ref, b, CZ)))
             x = xa * xb_ref[b]
             add(ROW_X + row, x[:, :128] + x[:, 128:])
-            acc_ref[8 * (ROW_Y + row):8 * (ROW_Y + row) + 8, 0:CX] = ya * yb_ref[b]
+
+    lane = lax.broadcasted_iota(jnp.int32, (CX, 128), 1)
+    weight = harmonic(ys_ref[0:CX, 0:128], yh_ref[0:CX, 0:128] * y_high)
+    weight = pltpu.roll(weight, 128 - FACE_LANE, 1)
+    weight = jnp.where((lane < 16) & (lax.rem(lane, 2) == 1), -weight, 0.0)
+    for shift in (16, 32, 64):
+        weight = weight + pltpu.roll(weight, shift, 1)
+    mine = weight * ys_ref[0:CX, 128:256]
+    theirs = pltpu.roll(yh_ref[0:CX, 128:256], 1, 1)
+    group = lax.broadcasted_iota(jnp.int32, (8, 128), 1) // 16
+    for d in range(8):
+        product = mine * (pltpu.roll(theirs, 128 - 16 * d, 1) if d else theirs)
+        product = product[:8] + product[8:]
+        for a in range(8):
+            row = 8 * (ROW_Y + 8 * ((a + d) % 8) + a)
+            acc_ref[row:row + 8, :] = jnp.where(group == a, product, 0.0)
 
     total = acc_ref[pl.ds(0, 256, stride=8), :]
     for sub in range(1, 8):
         total = total + acc_ref[pl.ds(sub, 256, stride=8), :]
     summed = lax.dot_general(jnp.ones((8, 128), jnp.float32), total, (((1,), (1,)), ((), ())),
                              precision=HIGHEST, preferred_element_type=jnp.float32)
-    pay_ref[...] = summed[0:1]
+    pay_ref[0:1, :] = summed[0:1, :128]
+    pay_ref[1:2, :] = summed[0:1, 128:]
 
 
 def total_of(v):
@@ -171,11 +308,11 @@
     return apply_e, solve
 
 
-def coarse_kernel(dev_ref, gath_ref, f_ref, b_ref, wx_ref, wy_ref, wz_ref, dg_ref, iv_ref, s_ref, u_ref,
+def coarse_kernel(pos_ref, gath_ref, r_ref, b_ref, wx_ref, wy_ref, wz_ref, dg_ref, iv_ref, s_ref, u_ref,
                   sol_ref, res_ref, pre_ref, refined_ref, part_ref, scal_ref,
                   t_ref, tile_ref, pc_ref, q_ref):
-    dev = dev_ref[0]
-    gz = lax.rem(dev, 2)
+    gz = pos_ref[2]
+    dev = (pos_ref[0] * 8 + pos_ref[1]) * 2 + gz
     turned = gath_ref[...].T
     t_ref[0] = turned[:, :128]
     t_ref[1] = turned[:, 128:]
@@ -245,7 +382,7 @@
 
     for z in range(9):
         image = u_ref[z] + at(z, pc_ref)
-        residual = f_ref[2, z] - step * image
+        residual = r_ref[z] - step * image
         q_ref[z] = iv_ref[z] * residual
         if z < CZ:
             keep(res_ref, z, residual)
@@ -294,62 +431,42 @@
 
 def gather_rows(row):
     rows = jnp.broadcast_to(row[None], (NDEV,) + row.shape)
-    return lax.all_to_all(rows, AXES, 0, 0, tiled=False).reshape(NDEV, row.shape[-1])
+    return lax.all_to_all(rows, AXES, 0, 0, tiled=False)
 
 
 def local(right_side, conductivity, storage, basis):
-    gx, gy, gz = (lax.axis_index(a) for a in AXES)
-    dev = (gx * 8 + gy) * 2 + gz
-    fields = jnp.stack([conductivity, storage, right_side])
-    fields = jnp.where(gz == 0, fields, fields[:, ::-1])
-    basis = jnp.where(gz == 0, basis, basis[:, ::-1])
-    only_k = (jnp.arange(3) == 0)[:, None, None, None]
-
-    def halo(v, axis, dim, width):
-        low = lax.ppermute(lax.slice_in_dim(v, v.shape[dim] - width, None, axis=dim), axis, ring(axis, 1))
-        high = lax.ppermute(lax.slice_in_dim(v, 0, width, axis=dim), axis, ring(axis, -1))
-        return low, high
-
-    def clear(low, high, index, count):
-        low = jnp.where(only_k & (index == 0), 0.0, low)
-        high = jnp.where(only_k & (index == count - 1), 0.0, high)
-        return low, high
-
-    fx_low, fx_high = clear(*halo(fields, "gx", 2, 4), gx, 16)
-    bx_low, bx_high = halo(basis, "gx", 2, 2)
-    xa = basis[:, :, CX - 1].astype(jnp.float32)
-    xb = bx_high[:, :, 0].astype(jnp.float32)
-    kx = jnp.stack([fields[0, :, CX - 1], fx_high[0, :, 0]])
-    fields_x = jnp.concatenate([fields, fx_high, fx_low], axis=2)
-    gap = jnp.zeros(basis.shape[:2] + (4,) + basis.shape[3:], basis.dtype)
-    basis_x = jnp.concatenate([basis, bx_high, gap, bx_low], axis=2)
-
-    fy_low, fy_high = clear(*halo(fields_x, "gy", 3, 4), gy, 8)
-    by_low, by_high = halo(basis_x, "gy", 3, 2)
-    ya = basis[:, :, :, CY - 1].astype(jnp.float32)
-    yb = by_high[:, :, :CX, 0].astype(jnp.float32)
-    ky = jnp.stack([fields[0, :, :, CY - 1], fy_high[0, :, :CX, 0]])
-    fields_y = jnp.concatenate([fields_x, fy_high, jnp.ones((3, CZ, EX, EY - CY - 8), jnp.float32), fy_low], axis=3)
-    basis_y = jnp.concatenate(
-        [basis_x, by_high, jnp.zeros((8, CZ, EX, EY - CY - 4), basis.dtype), by_low], axis=3)
-
+    pos = jnp.stack([lax.axis_index(a) for a in AXES]).astype(jnp.int32)
+    fields = (conductivity, storage, right_side, basis)
     swap = [(0, 1), (1, 0)]
-    fz = lax.ppermute(fields_y[:, 4:], "gz", swap)
-    bz = lax.ppermute(basis_y[:, 6:], "gz", swap)
-    fields_e = jnp.concatenate([fields_y, fz[:, ::-1]], axis=1)
-    basis_e = jnp.concatenate([basis_y, bz[:, ::-1]], axis=1).astype(jnp.float32)
+
+    def exchange(axis, hi, lo):
+        return lax.ppermute(lo, axis, ring(axis, -1)), lax.ppermute(hi, axis, ring(axis, 1))
+
+    faces = (X_ROWS * CZ, CY)
+    hi, lo, layers = call(pack_x_kernel, [faces, faces, (X_ROWS, CX, CY)], [], 5, True)(pos, *fields)
+    x_high, x_low = exchange("gx", hi, lo)
+    other_layers = lax.ppermute(layers, "gz", swap)
+    other_xh = lax.ppermute(x_high[X_ROWS * 4:], "gz", swap)
+    other_xl = lax.ppermute(x_low[X_ROWS * 4:], "gz", swap)
+    columns = (EX, 256)
+    hi, lo = call(pack_y_kernel, [columns, columns], [(88, 8, CY)], 7, True)(pos, *fields, x_high, x_low)
+    y_high, y_low = exchange("gy", hi, lo)
+    other_yh = lax.ppermute(y_high, "gz", swap)
+    other_yl = lax.ppermute(y_low, "gz", swap)
 
     ext = (EZ, EX, EY)
-    pay, wx, wy, wz, dg, iv, s, u = call(
-        prepare_kernel, [(1, 256)] + [ext] * 7, [ext, (2048, 128)], 8
-    )(fields_e, basis_e, xa, xb, ya, yb, kx, ky)
-    gathered = gather_rows(pay)
+    pay, r, b, wx, wy, wz, dg, iv, s, u = call(
+        prepare_kernel,
+        [(2, 128), ext, (8, 10, EX, EY)] + [ext] * 7,
+        [ext, ext, ext, (2048, 128), (8, CZ, CY), (8, CZ, CY), (CZ, CY)], 15, True,
+    )(pos, *fields, other_layers, x_high, x_low, other_xh, other_xl, hi, y_high, y_low, other_yh, other_yl)
+    gathered = gather_rows(pay).reshape(NDEV, 256)
     box = (CZ, CX, CY)
     sol, res, pre, refined, part, scal = call(
         coarse_kernel, [box] * 4 + [(1, 128)] * 2,
         [(2, 256, 128), (384, 256), ext, ext], 11, True,
-    )(dev.astype(jnp.int32).reshape(1), gathered, fields_e, basis_e, wx, wy, wz, dg, iv, s, u)
-    parts = gather_rows(part)
+    )(pos, gathered, r, b, wx, wy, wz, dg, iv, s, u)
+    parts = gather_rows(part).reshape(NDEV, 128)
     direction, = call(finish_kernel, [box], [], 4)(parts, scal, refined, pre)
     return sol, res, direction
 

time: 114 us -> 86.6 us (0.76)
  waiting for transfers between devices: 35.1 us -> 12.7 us
  blocking collectives: 18.2 us -> 39.4 us
  starting transfers between devices: 26.6 us -> 16.7 us
  other arithmetic: 9.8 us -> 0.08 us
  local copies, waits for them, and re-layouts: 10.9 us -> 3.96 us
    all_to_all x1 -> x2, blocking collectives: 18.2 us -> 39.4 us  [gather_rows(): return lax.all_to_all(rows, AXES, 0, 0, tiled=False)]
    all_to_all x1 -> x0, waiting for transfers between devices: 15.1 us -> none  [gather_rows(): lax.all_to_all(rows, AXES, 0, 0, tiled=False).reshape(NDEV, row.shape[-1])]
    ppermute x10 -> x9, waiting for transfers between devices: 20.1 us -> 12.7 us  [the longest x2 6.32 us: exchange(): lax.ppermute(hi, axis, ring(axis, 1))]
    all_to_all x1 -> x0, starting transfers between devices: 6.76 us -> none  [gather_rows(): lax.all_to_all(rows, AXES, 0, 0, tiled=False).reshape(NDEV, row.shape[-1])]
    convert_element_type x5 -> x0, other arithmetic: 4.93 us -> none  [the longest x1 3.06 us: local(): jnp.concatenate([basis_y, bz[:, ::-1]], axis=1).astype(jnp.float32)]
    ppermute x10 -> x9, starting transfers between devices: 19.8 us -> 16.7 us  [the longest x2 8.86 us: exchange(): lax.ppermute(lo, axis, ring(axis, -1))]
    unnamed x28 -> x9, local copies, waits for them, and re-layouts: 6.5 us -> 3.77 us
    rev x2 -> x0, local copies, waits for them, and re-layouts: 2.03 us -> none  [the longest x1 1.04 us: local(): fields_e = jnp.concatenate([fields_y, fz[:, ::-1]], axis=1)]
  transfers between devices with their start and end apart: 11 -> 9, of which waited for: 6 -> 5; matrix products, arithmetic and copies ran while one was open for 11% -> 0% of each run, Pallas kernels for 0% -> 1%
where the time goes in v2:
time: 86.6 us; the launch traced here: 86.3 us
  blocking collectives  39.4 us (45%)
  starting transfers between devices  16.7 us (19%)
  Pallas kernels  12.8 us (15%)
  waiting for transfers between devices  12.7 us (15%)
  local copies, waits for them, and re-layouts  3.96 us (5%)
    all_to_all x2, blocking collectives, gather_rows(): return lax.all_to_all(rows, AXES, 0, 0, tiled=False)  39.4 us
    ppermute x2, starting transfers between devices, exchange(): lax.ppermute(lo, axis, ring(axis, -1))  8.86 us
    ppermute x2, waiting for transfers between devices, exchange(): lax.ppermute(hi, axis, ring(axis, 1))  6.32 us
    ppermute x2, waiting for transfers between devices, exchange(): lax.ppermute(lo, axis, ring(axis, -1))  5.54 us
    pallas_call x1, Pallas kernels, local(): call(coarse_kernel, [box] * 4 + [(1, 128)] * 2, [(2, 256, 128), (384, 256...  5.16 us
    pallas_call x1, Pallas kernels, local(): call(prepare_kernel, [(2, 128), ext, (8, 10, EX, EY)] + [ext] * 7, [ext,...  4.9 us
    unnamed x9, local copies, waits for them, and re-layouts  3.77 us
    ppermute x1, starting transfers between devices, local(): other_layers = lax.ppermute(layers, 'gz', swap)  3.33 us
  transfers between devices with their start and end apart: 9, of which 5 were waited for; matrix products, arithmetic and copies ran while one was open for 0% of the time, Pallas kernels for 1%

profile of v2, /device:TPU:1, one launch (start us, length us, event | category | flops | bytes accessed | tf_op | source)
XLA Modules:
  0.0 86.3 jit_solution(17080131800075879159)
XLA Ops:
  0.6 0.1 pad_add_fusion.pos_ref
  0.7 1.0 %copy-done = bf16[8,8,16,256]{3,2,1,0:T(8,128)(2,1)S(1)} copy-done((bf16[8,8,16,256]{3,2,1,0:T(8,128)(2,1)S(1)}, bf16[8,8,16,256]{3,2,1,0:T(8,128)(2,1)}, u32[]{:S(2)}) %copy-start) | copy-done | bytes 524312
  1.8 0.9 %copy-done.1 = f32[8,16,256]{2,1,0:T(8,128)S(1)} copy-done((f32[8,16,256]{2,1,0:T(8,128)S(1)}, f32[8,16,256]{2,1,0:T(8,128)}, u32[]{:S(2)}) %copy-start.1) | copy-done | bytes 131096
  2.7 0.9 %copy-done.2 = f32[8,16,256]{2,1,0:T(8,128)S(1)} copy-done((f32[8,16,256]{2,1,0:T(8,128)S(1)}, f32[8,16,256]{2,1,0:T(8,128)}, u32[]{:S(2)}) %copy-start.2) | copy-done | bytes 131096
  3.6 0.9 %copy-done.3 = f32[8,16,256]{2,1,0:T(8,128)S(1)} copy-done((f32[8,16,256]{2,1,0:T(8,128)S(1)}, f32[8,16,256]{2,1,0:T(8,128)}, u32[]{:S(2)}) %copy-start.3) | copy-done | bytes 131096
  4.5 0.7 shard_map.67
  5.2 3.3 %collective-permute-start = (f32[26,16,256]{2,1,0:T(8,128)S(1)}, f32[26,16,256]{2,1,0:T(8,128)S(1)}, u32[]{:S(2)}, u32[]{:S(2)}) collective-permute-start(f32[26,16,256]{2,1,0:T(8,128)S(1)} %get-tuple-element.24), channel_id=1, source_target_pairs={{0,1},{1,0},{2,3},{3,2},{4,5},{5,4},{6,7},{7,6},{8,9},{9,8},{10,11... | collective-permute-start | bytes 1277960 | tf_op jit(solution)/shard_map/ppermute | solution.py:448
  8.5 3.2 %collective-permute-start.1 = (f32[208,256]{1,0:T(8,128)S(1)}, f32[208,256]{1,0:T(8,128)S(1)}, u32[]{:S(2)}, u32[]{:S(2)}) collective-permute-start(f32[208,256]{1,0:T(8,128)S(1)} %get-tuple-element.25), channel_id=1, source_target_pairs={{0,240},{16,0},{32,16},{48,32},{64,48},{80,64},{96,80},{112,96},{1... | collective-permute-start | bytes 638984 | tf_op jit(solution)/shard_map/ppermute | solution.py:443
  11.7 0.0 collective-permute-start.2
  11.7 4.6 %collective-permute-done.1.xh_ref = f32[208,256]{1,0:T(8,128)S(1)} collective-permute-done((f32[208,256]{1,0:T(8,128)S(1)}, f32[208,256]{1,0:T(8,128)S(1)}, u32[]{:S(2)}, u32[]{:S(2)}) %collective-permute-start.1) | collective-permute-done | bytes 213024 | tf_op jit(solution)/shard_map/ppermute | solution.py:443
  16.3 0.9 %collective-permute-start.3 = (f32[104,256]{1,0:T(8,128)S(1)}, f32[104,256]{1,0:T(8,128)S(1)}, u32[]{:S(2)}, u32[]{:S(2)}) collective-permute-start(f32[104,256]{1,0:T(8,128)S(1)} %slice.8), channel_id=1, source_target_pairs={{0,1},{1,0},{2,3},{3,2},{4,5},{5,4},{6,7},{7,6},{8,9},{9,8},{10,11... | collective-permute-start | bytes 319496 | tf_op jit(solution)/shard_map/ppermute | solution.py:449
  17.2 4.2 %collective-permute-done.2.xl_ref = f32[208,256]{1,0:T(8,128)S(1)} collective-permute-done((f32[208,256]{1,0:T(8,128)S(1)}, f32[208,256]{1,0:T(8,128)S(1)}, u32[]{:S(2)}, u32[]{:S(2)}) %collective-permute-start.2) | collective-permute-done | bytes 213024 | tf_op jit(solution)/shard_map/ppermute | solution.py:443
  21.5 1.3 %collective-permute-start.4 = (f32[104,256]{1,0:T(8,128)S(1)}, f32[104,256]{1,0:T(8,128)S(1)}, u32[]{:S(2)}, u32[]{:S(2)}) collective-permute-start(f32[104,256]{1,0:T(8,128)S(1)} %slice.9), channel_id=1, source_target_pairs={{0,1},{1,0},{2,3},{3,2},{4,5},{5,4},{6,7},{7,6},{8,9},{9,8},{10,11... | collective-permute-start | bytes 319496 | tf_op jit(solution)/shard_map/ppermute | solution.py:450
  22.8 1.2 %shard_map.68 = (f32[24,256]{1,0:T(8,128)S(1)}, f32[24,256]{1,0:T(8,128)S(1)}) custom-call(s32[3]{0:T(128)S(1)} %pad_add_fusion.pos_ref, f32[8,16,256]{2,1,0:T(8,128)S(1)} %copy-done.1, f32[8,16,256]{2,1,0:T(8,128)S(1)} %copy-done.2, f32[8,16,256]{2,1,0:T(8,128)S(1)} %copy-done.3, bf16[8,8,16,256]{3,2,1,0:T(8,128)(2,1)S(1)} %copy-done, ...), custom_call_target="tpu_custom_call" | custom-call | tf_op jit(solution)/shard_map/pallas_call | solution.py:452
  23.9 5.7 %collective-permute-start.5 = (f32[24,256]{1,0:T(8,128)S(1)}, f32[24,256]{1,0:T(8,128)S(1)}, u32[]{:S(2)}, u32[]{:S(2)}) collective-permute-start(f32[24,256]{1,0:T(8,128)S(1)} %get-tuple-element.28), channel_id=1, source_target_pairs={{0,14},{2,0},{4,2},{6,4},{8,6},{10,8},{12,10},{14,12},{1,15},{3,1}... | collective-permute-start | bytes 73736 | tf_op jit(solution)/shard_map/ppermute | solution.py:443
  29.6 0.0 collective-permute-start.6
  29.6 0.9 %collective-permute-done.5.yh_ref = f32[24,256]{1,0:T(8,128)S(1)} collective-permute-done((f32[24,256]{1,0:T(8,128)S(1)}, f32[24,256]{1,0:T(8,128)S(1)}, u32[]{:S(2)}, u32[]{:S(2)}) %collective-permute-start.5) | collective-permute-done | bytes 24608 | tf_op jit(solution)/shard_map/ppermute | solution.py:443
  30.5 0.9 %collective-permute-start.7 = (f32[24,256]{1,0:T(8,128)S(1)}, f32[24,256]{1,0:T(8,128)S(1)}, u32[]{:S(2)}, u32[]{:S(2)}) collective-permute-start(f32[24,256]{1,0:T(8,128)S(1)} %collective-permute-done.5.yh_ref), channel_id=1, source_target_pairs={{0,1},{1,0},{2,3},{3,2},{4,5},{5,4},{6,7},{7,6},{8,9},{9,8},{10,11... | collective-permute-start | bytes 73736 | tf_op jit(solution)/shard_map/ppermute | solution.py:454
  31.4 2.1 %collective-permute-done.6.yl_ref = f32[24,256]{1,0:T(8,128)S(1)} collective-permute-done((f32[24,256]{1,0:T(8,128)S(1)}, f32[24,256]{1,0:T(8,128)S(1)}, u32[]{:S(2)}, u32[]{:S(2)}) %collective-permute-start.6) | collective-permute-done | bytes 24608 | tf_op jit(solution)/shard_map/ppermute | solution.py:443
  33.5 1.4 %collective-permute-start.8 = (f32[24,256]{1,0:T(8,128)S(1)}, f32[24,256]{1,0:T(8,128)S(1)}, u32[]{:S(2)}, u32[]{:S(2)}) collective-permute-start(f32[24,256]{1,0:T(8,128)S(1)} %collective-permute-done.6.yl_ref), channel_id=1, source_target_pairs={{0,1},{1,0},{2,3},{3,2},{4,5},{5,4},{6,7},{7,6},{8,9},{9,8},{10,11... | collective-permute-start | bytes 73736 | tf_op jit(solution)/shard_map/ppermute | solution.py:455
  34.9 0.0 collective-permute-done.7.yhq_ref
  34.9 0.8 collective-permute-done.8.ylq_ref
  35.8 0.0 collective-permute-done.3.xhq_ref
  35.8 0.0 collective-permute-done.4.xlq_ref
  35.8 0.0 collective-permute-done.q_ref
  35.8 4.9 %shard_map.69 = (f32[2,128]{1,0:T(2,128)S(1)}, f32[12,24,384]{2,1,0:T(8,128)S(1)}, f32[8,10,24,384]{3,2,1,0:T(8,128)S(1)}, f32[12,24,384]{2,1,0:T(8,128)S(1)}, f...) custom-call(s32[3]{0:T(128)S(1)} %pad_add_fusion.pos_ref, ...), custom_call_target="tpu_custom_call" | custom-call | tf_op jit(solution)/shard_map/pallas_call | solution.py:458
  40.7 0.1 broadcast_in_dim.6
  40.8 21.2 %all_to_all.10 = f32[256,2,128]{2,1,0:T(2,128)S(1)} all-to-all(f32[256,2,128]{2,1,0:T(2,128)S(1)} %broadcast_in_dim.6), channel_id=1, replica_groups=mesh['gx'=16,'gy'=8,'gz'=2] {'gx','gy','gz'}, dimensions={0} | all-to-all | bytes 524288 | tf_op jit(solution)/shard_map/all_to_all | solution.py:434
  62.0 5.2 %shard_map.70 = (f32[8,16,256]{2,1,0:T(8,128)}, f32[8,16,256]{2,1,0:T(8,128)}, f32[8,16,256]{2,1,0:T(8,128)S(1)}, f32[8,16,256]{2,1,0:T(8,128)S(1)}, f32[1,128]{1,0:T(1,128)S(1)}, /*index=5*/f32[1,128]{1,0:T(1,128)S(1)}) custom-call(s32[3]{0:T(128)S(1)} %pad_add_fusion.pos_ref, f32[256,256]{1,0:T(8,128)S(1)} %bitcast.9, ...), custom_call_target="tpu_custom_call" | custom-call | tf_op jit(solution)/shard_map/pallas_call | solution.py:465
  67.2 0.1 broadcast_in_dim.16
  67.2 18.2 %all_to_all.11 = f32[256,1,128]{2,1,0:T(1,128)S(1)} all-to-all(f32[256,1,128]{2,1,0:T(1,128)S(1)} %broadcast_in_dim.16), channel_id=1, replica_groups=mesh['gx'=16,'gy'=8,'gz'=2] {'gx','gy','gz'}, dimensions={0} | all-to-all | bytes 262144 | tf_op jit(solution)/shard_map/all_to_all | solution.py:434
  85.5 0.9 %shard_map.71 = f32[8,16,256]{2,1,0:T(8,128)} custom-call(f32[256,128]{1,0:T(8,128)S(1)} %bitcast.10, f32[1,128]{1,0:T(1,128)S(1)} %get-tuple-element.42.scal_ref, f32[8,16,256]{2,1,0:T(8,128)S(1)} %get-tuple-element.43.refined_ref, f32[8,16,256]{2,1,0:T(8,128)S(1)} %get-tuple-element.44.pre_ref), custom_call_target="tpu_custom_call" | custom-call | tf_op jit(solution)/shard_map/pallas_call | solution.py:470
  (7 shorter events, 0.0 us)
Async XLA Ops:
  0.7 1.0 %copy-start = (bf16[8,8,16,256]{3,2,1,0:T(8,128)(2,1)S(1)}, bf16[8,8,16,256]{3,2,1,0:T(8,128)(2,1)}, u32[]{:S(2)}) copy-start(bf16[8,8,16,256]{3,2,1,0:T(8,128)(2,1)} %b_in.1) | copy-start | bytes 1572868
  1.8 0.9 %copy-start.1 = (f32[8,16,256]{2,1,0:T(8,128)S(1)}, f32[8,16,256]{2,1,0:T(8,128)}, u32[]{:S(2)}) copy-start(f32[8,16,256]{2,1,0:T(8,128)} %k_in.1) | copy-start | bytes 393220
  2.7 0.9 %copy-start.2 = (f32[8,16,256]{2,1,0:T(8,128)S(1)}, f32[8,16,256]{2,1,0:T(8,128)}, u32[]{:S(2)}) copy-start(f32[8,16,256]{2,1,0:T(8,128)} %st_in.1) | copy-start | bytes 393220
  3.6 0.9 %copy-start.3 = (f32[8,16,256]{2,1,0:T(8,128)S(1)}, f32[8,16,256]{2,1,0:T(8,128)}, u32[]{:S(2)}) copy-start(f32[8,16,256]{2,1,0:T(8,128)} %r_in.1) | copy-start | bytes 393220
  5.2 30.6 %collective-permute-start = (f32[26,16,256]{2,1,0:T(8,128)S(1)}, f32[26,16,256]{2,1,0:T(8,128)S(1)}, u32[]{:S(2)}, u32[]{:S(2)}) collective-permute-start(f32[26,16,256]{2,1,0:T(8,128)S(1)} %get-tuple-element.24), channel_id=1, source_target_pairs={{0,1},{1,0},{2,3},{3,2},{4,5},{5,4},{6,7},{7,6},{8,9},{9,8},{10,11... | collective-permute-start | bytes 1277960 | tf_op jit(solution)/shard_map/ppermute | solution.py:448
  8.5 7.8 %collective-permute-start.1 = (f32[208,256]{1,0:T(8,128)S(1)}, f32[208,256]{1,0:T(8,128)S(1)}, u32[]{:S(2)}, u32[]{:S(2)}) collective-permute-start(f32[208,256]{1,0:T(8,128)S(1)} %get-tuple-element.25), channel_id=1, source_target_pairs={{0,240},{16,0},{32,16},{48,32},{64,48},{80,64},{96,80},{112,96},{1... | collective-permute-start | bytes 638984 | tf_op jit(solution)/shard_map/ppermute | solution.py:443
  11.7 9.8 %collective-permute-start.2 = (f32[208,256]{1,0:T(8,128)S(1)}, f32[208,256]{1,0:T(8,128)S(1)}, u32[]{:S(2)}, u32[]{:S(2)}) collective-permute-start(f32[208,256]{1,0:T(8,128)S(1)} %get-tuple-element.26), channel_id=1, source_target_pairs={{0,16},{16,32},{32,48},{48,64},{64,80},{80,96},{96,112},{112,128},... | collective-permute-start | bytes 638984 | tf_op jit(solution)/shard_map/ppermute | solution.py:443
  16.3 19.5 %collective-permute-start.3 = (f32[104,256]{1,0:T(8,128)S(1)}, f32[104,256]{1,0:T(8,128)S(1)}, u32[]{:S(2)}, u32[]{:S(2)}) collective-permute-start(f32[104,256]{1,0:T(8,128)S(1)} %slice.8), channel_id=1, source_target_pairs={{0,1},{1,0},{2,3},{3,2},{4,5},{5,4},{6,7},{7,6},{8,9},{9,8},{10,11... | collective-permute-start | bytes 319496 | tf_op jit(solution)/shard_map/ppermute | solution.py:449
  21.5 14.3 %collective-permute-start.4 = (f32[104,256]{1,0:T(8,128)S(1)}, f32[104,256]{1,0:T(8,128)S(1)}, u32[]{:S(2)}, u32[]{:S(2)}) collective-permute-start(f32[104,256]{1,0:T(8,128)S(1)} %slice.9), channel_id=1, source_target_pairs={{0,1},{1,0},{2,3},{3,2},{4,5},{5,4},{6,7},{7,6},{8,9},{9,8},{10,11... | collective-permute-start | bytes 319496 | tf_op jit(solution)/shard_map/ppermute | solution.py:450
  23.9 6.6 %collective-permute-start.5 = (f32[24,256]{1,0:T(8,128)S(1)}, f32[24,256]{1,0:T(8,128)S(1)}, u32[]{:S(2)}, u32[]{:S(2)}) collective-permute-start(f32[24,256]{1,0:T(8,128)S(1)} %get-tuple-element.28), channel_id=1, source_target_pairs={{0,14},{2,0},{4,2},{6,4},{8,6},{10,8},{12,10},{14,12},{1,15},{3,1}... | collective-permute-start | bytes 73736 | tf_op jit(solution)/shard_map/ppermute | solution.py:443
  29.6 3.9 %collective-permute-start.6 = (f32[24,256]{1,0:T(8,128)S(1)}, f32[24,256]{1,0:T(8,128)S(1)}, u32[]{:S(2)}, u32[]{:S(2)}) collective-permute-start(f32[24,256]{1,0:T(8,128)S(1)} %get-tuple-element.27.ys_ref), channel_id=1, source_target_pairs={{0,2},{2,4},{4,6},{6,8},{8,10},{10,12},{12,14},{14,0},{1,3},{3,5},... | collective-permute-start | bytes 73736 | tf_op jit(solution)/shard_map/ppermute | solution.py:443
  30.5 4.4 %collective-permute-start.7 = (f32[24,256]{1,0:T(8,128)S(1)}, f32[24,256]{1,0:T(8,128)S(1)}, u32[]{:S(2)}, u32[]{:S(2)}) collective-permute-start(f32[24,256]{1,0:T(8,128)S(1)} %collective-permute-done.5.yh_ref), channel_id=1, source_target_pairs={{0,1},{1,0},{2,3},{3,2},{4,5},{5,4},{6,7},{7,6},{8,9},{9,8},{10,11... | collective-permute-start | bytes 73736 | tf_op jit(solution)/shard_map/ppermute | solution.py:454
  33.5 2.3 %collective-permute-start.8 = (f32[24,256]{1,0:T(8,128)S(1)}, f32[24,256]{1,0:T(8,128)S(1)}, u32[]{:S(2)}, u32[]{:S(2)}) collective-permute-start(f32[24,256]{1,0:T(8,128)S(1)} %collective-permute-done.6.yl_ref), channel_id=1, source_target_pairs={{0,1},{1,0},{2,3},{3,2},{4,5},{5,4},{6,7},{7,6},{8,9},{9,8},{10,11... | collective-permute-start | bytes 73736 | tf_op jit(solution)/shard_map/ppermute | solution.py:455

commit v3 on v1

v3 whole, which is shorter than its diff:
```python
import functools

import jax
import jax.numpy as jnp
from jax import lax
from jax.experimental import pallas as pl
from jax.experimental.pallas import tpu as pltpu
from jax.sharding import PartitionSpec as P

KITERS = 6
RELAXATION = 0.6
HIGHEST = lax.Precision.HIGHEST
AXES = ("gx", "gy", "gz")
CZ, CX, CY = 8, 16, 256
EZ, EX, EY = 12, 24, 384
NDEV = 256
PAIRS = [(a, b) for a in range(8) for b in range(a, 8)]
ROW_Z, ROW_Y, ROW_X, ROW_OWN, ROW_RS, ROW_SAS, ROW_G, ROW_H = 0, 64, 128, 192, 228, 229, 232, 240
DEPTHS = (4, 3, 3)
STEPS = [(f, d) for f in range(3) for d in range(DEPTHS[f])]
FIELD_ROW, LAST_ROW, FACE_ROWS = 128, 208, 216
FACE_LANE, CORNER_LANE = 96, 40
VMEM_LIMIT = 24 * 1024 * 1024


def harmonic(k, other):
    return 2.0 * k * other / jnp.maximum(k + other, 1e-30)


def y_next(v):
    return pltpu.roll(v, v.shape[1] - 1, 1)


def y_prev(v):
    return pltpu.roll(v, 1, 1)


def x_next(v):
    return pltpu.roll(v, v.shape[0] - 1, 0)


def x_prev(v):
    return pltpu.roll(v, 1, 0)


def apply_at(z, v, v_up, v_down, diag, wx, wy, wz_up, wz_down):
    total = diag * v - wy * y_next(v) - y_prev(wy * v) - wx * x_next(v) - x_prev(wx * v)
    if v_up is not None:
        total = total - wz_up * v_up
    if v_down is not None:
        total = total - wz_down * v_down
    return total


def fold(v):
    return (v[:8, :128] + v[8:, :128]) + (v[:8, 128:] + v[8:, 128:])


def flag(inside):
    return jnp.where(inside, 1.0, 0.0).astype(jnp.float32)


def source_of(z, gz):
    return z + gz * (CZ - 1 - 2 * z)


def pack_x_kernel(pos_ref, f_ref, b_ref, hi_ref, lo_ref, small_hi_ref, small_lo_ref, q_ref):
    gz = pos_ref[2]
    for z in range(CZ):
        src, j = source_of(z, gz), CZ - 1 - z
        fields = [f_ref[f, pl.ds(src, 1)][0] for f in range(3)]
        for t, (f, d) in enumerate(STEPS):
            row = FIELD_ROW + 8 * t + z
            hi_ref[row:row + 1, :] = fields[f][CX - 1 - d:CX - d]
            lo_ref[row:row + 1, :] = fields[f][d:d + 1]
        if j < 4:
            q_ref[j] = fields[0]
        if j < 3:
            q_ref[4 + j] = fields[1]
            q_ref[7 + j] = fields[2]
        for a in range(8):
            v = b_ref[a, pl.ds(src, 1)][0]
            for d in range(2):
                row = 16 * a + 8 * d + z
                hi_ref[row:row + 1, :] = v[CX - 1 - d:CX - d]
                lo_ref[row:row + 1, :] = v[d:d + 1]
            if j == 0:
                hi_ref[LAST_ROW + a:LAST_ROW + a + 1, :] = v[CX - 1:CX]
                lo_ref[LAST_ROW + a:LAST_ROW + a + 1, :] = v[0:1]
            if j < 2:
                q_ref[10 + 2 * a + j] = v
    lane = lax.broadcasted_iota(jnp.int32, (8, 128), 1)
    rows = [FIELD_ROW + 8 * t for t in range(10)] + [16 * a for a in range(8)]
    for ref, small_ref in ((hi_ref, small_hi_ref), (lo_ref, small_lo_ref)):
        first = last = jnp.zeros((8, 128), jnp.float32)
        for i, row in enumerate(rows):
            mask = (lane >= 4 * i) & (lane < 4 * i + 4)
            first = jnp.where(mask, pltpu.roll(ref[row:row + 8, :128], 4 * i, 1), first)
            last = jnp.where(mask, pltpu.roll(ref[row:row + 8, 128:], 4 * i + 4, 1), last)
        small_ref[:, :128] = first
        small_ref[:, 128:] = last


def pack_y_kernel(pos_ref, f_ref, b_ref, hi_ref, lo_ref):
    gz = pos_ref[2]
    lane = lax.broadcasted_iota(jnp.int32, (CX, 128), 1)
    hi = [jnp.zeros((CX, 128), jnp.float32)] * 2
    lo = [jnp.zeros((CX, 128), jnp.float32)] * 2

    def put(half, v, width, offset):
        mask = (lane >= offset) & (lane < offset + width)
        hi[half] = jnp.where(mask, pltpu.roll(v[:, 128:], (offset + width) % 128, 1), hi[half])
        lo[half] = jnp.where(mask, pltpu.roll(v[:, :128], offset, 1), lo[half])

    for z in range(CZ):
        src = source_of(z, gz)
        for f in range(3):
            v = f_ref[f, pl.ds(src, 1)][0]
            put(0, v, 4, 32 * f + 4 * z)
            if f == 0:
                put(0, v, 1, FACE_LANE + 2 * z + 1)
        for a in range(8):
            put(1, b_ref[a, pl.ds(src, 1)][0], 2, 16 * a + 2 * z)
    for half in range(2):
        hi_ref[:, 128 * half:128 * half + 128] = hi[half]
        lo_ref[:, 128 * half:128 * half + 128] = lo[half]


def gram_kernel(pos_ref, f_ref, b_ref, part_ref):
    gz = pos_ref[2]
    part_ref[...] = jnp.zeros_like(part_ref)
    rows = lax.broadcasted_iota(jnp.int32, (CX, CY), 0)
    lanes = lax.broadcasted_iota(jnp.int32, (CX, CY), 1)

    def add(row, value):
        part_ref[8 * row:8 * row + 8, :] += value

    def body(z, carry):
        src, up, down = source_of(z, gz), jnp.minimum(z + 1, CZ - 1), jnp.maximum(z - 1, 0)
        k, st, r = (f_ref[f, pl.ds(src, 1)][0] for f in range(3))
        src_up, src_down = source_of(up, gz), source_of(down, gz)
        wy = jnp.where(lanes == CY - 1, 0.0, harmonic(k, y_next(k)))
        wx = jnp.where(rows == CX - 1, 0.0, harmonic(k, x_next(k)))
        wz_up = jnp.where(z < CZ - 1, harmonic(k, f_ref[0, pl.ds(src_up, 1)][0]), 0.0)
        wz_down = jnp.where(z > 0, harmonic(k, f_ref[0, pl.ds(src_down, 1)][0]), 0.0)
        diag = st + wy + y_prev(wy) + wx + x_prev(wx) + wz_up + wz_down
        basis = [b_ref[a, pl.ds(src, 1)][0] for a in range(8)]
        for b in range(8):
            add(36 + b, fold(basis[b] * r))
            image = apply_at(z, basis[b], b_ref[b, pl.ds(src_up, 1)][0],
                             b_ref[b, pl.ds(src_down, 1)][0], diag,
                             wx, wy, wz_up, wz_down)
            for a in range(b + 1):
                add(PAIRS.index((a, b)), fold(basis[a] * image))
        return carry

    lax.fori_loop(0, CZ, body, 0)


def prepare_kernel(pos_ref, f_in, part_ref, b_ref, q_ref, hi_ref, lo_ref, xh_ref, xl_ref, xhq_ref,
                   xlq_ref, ys_hi_ref, ys_lo_ref, yh_ref, yl_ref, yhq_ref, ylq_ref,
                   pay_ref, r_ref, wx_ref, wy_ref, wz_ref, dg_ref, iv_ref, s_ref, u_ref,
                   k_ref, st_ref, first_ref, acc_ref):
    gx, gy, gz = pos_ref[0], pos_ref[1], pos_ref[2]
    x_high, x_low = flag(gx < 15), flag(gx > 0)
    y_high, y_low = flag(gy < 7), flag(gy > 0)
    lane16 = lax.broadcasted_iota(jnp.int32, (CX, 128), 1)
    lane8 = lax.broadcasted_iota(jnp.int32, (8, 128), 1)
    outs = (k_ref, st_ref, r_ref)

    def beside(lane, high, low, offset, f):
        high = pltpu.roll(high, -offset % 128, 1)
        low = pltpu.roll(low, (124 - offset) % 128, 1)
        if f == 0:
            high, low = high * y_high, low * y_low
        return jnp.where(lane < 4, high, jnp.where(lane >= 124, low, 1.0))

    def main(f, z, value, high, low, layer):
        ref = outs[f]
        ref[z, :CX, :CY] = value
        ref[z, :CX, CY:] = beside(lane16, high[:CX, :128], low[:CX, :128], 32 * f + 4 * layer, f)
        if f:
            ref[z, CX:, :] = jnp.ones((EX - CX, EY), jnp.float32)

    def edges(t, sides, high, low, places):
        f, d = STEPS[t]
        for side, (ref, inside, row) in enumerate(sides):
            wide = ref[row + 8 * t:row + 8 * t + 8, :]
            columns = slice(128 * side, 128 * side + 128)
            corner = beside(lane8, high[CX:, columns], low[CX:, columns], 4 * t, f)
            if f == 0:
                wide, corner = wide * inside, corner * inside
            to = EX - 1 - d if side else CX + d
            for z, layer in places:
                outs[f][z, to:to + 1, :CY] = wide[layer:layer + 1]
                outs[f][z, to:to + 1, CY:] = corner[layer:layer + 1]

    high, low = yh_ref[...], yl_ref[...]
    for z in range(CZ):
        src = source_of(z, gz)
        for f in range(3):
            main(f, z, f_in[f, pl.ds(src, 1)][0], high, low, z)
    sides = ((xh_ref, x_high, FIELD_ROW), (xl_ref, x_low, FIELD_ROW))
    for t in range(len(STEPS)):
        edges(t, sides, high, low, [(z, z) for z in range(CZ)])
    high, low = yhq_ref[...], ylq_ref[...]
    first_layer = (0, 4, 7)
    for f in range(3):
        for j in range(DEPTHS[f]):
            main(f, CZ + j, q_ref[first_layer[f] + j], high, low, CZ - 1 - j)
    sides = ((xhq_ref, x_high, 0), (xlq_ref, x_low, 0))
    for t, (f, d) in enumerate(STEPS):
        edges(t, sides, high, low, [(CZ + j, CZ - 1 - j) for j in range(DEPTHS[f])])

    for z in range(11):
        k = k_ref[z]
        wy_ref[z] = harmonic(k, y_next(k))
        wx_ref[z] = harmonic(k, x_next(k))
        wz_ref[z] = harmonic(k, k_ref[z + 1])
    for z in range(11):
        wy, wx = wy_ref[z], wx_ref[z]
        diag = st_ref[z] + wy + y_prev(wy) + wx + x_prev(wx) + wz_ref[z]
        if z:
            diag = diag + wz_ref[z - 1]
        inverse = RELAXATION / jnp.maximum(diag, 1e-3)
        dg_ref[z] = diag
        iv_ref[z] = inverse
        first_ref[z] = inverse * r_ref[z]

    def at(z, ref):
        return apply_at(z, ref[z], ref[z + 1], ref[z - 1] if z else None, dg_ref[z], wx_ref[z],
                        wy_ref[z], wz_ref[z], wz_ref[z - 1] if z else None)

    for z in range(10):
        s_ref[z] = first_ref[z] + iv_ref[z] * (r_ref[z] - at(z, first_ref))
    for z in range(9):
        u_ref[z] = at(z, s_ref)

    def set_row(row, value):
        acc_ref[8 * row:8 * row + 8, :] = value

    def layers(products):
        total = None
        for z in range(CZ):
            total = products(z) if total is None else total + products(z)
        return fold(total)

    def own(ref, z):
        return ref[z, :CX, :CY]

    def basis(a, z):
        return b_ref[a, pl.ds(source_of(z, gz), 1)][0]

    acc_ref[8 * ROW_RS:8 * ROW_G, :] = jnp.zeros((8 * (ROW_G - ROW_RS), 128), jnp.float32)
    acc_ref[8 * (ROW_H + 8):2048, :] = jnp.zeros((2048 - 8 * (ROW_H + 8), 128), jnp.float32)
    set_row(ROW_RS, layers(lambda z: own(r_ref, z) * own(s_ref, z)))
    set_row(ROW_SAS, layers(lambda z: own(u_ref, z) * own(s_ref, z)))
    for a in range(8):
        set_row(ROW_H + a, layers(lambda z: basis(a, z) * own(u_ref, z)))
    acc_ref[8 * ROW_G:8 * (ROW_G + 8), :] = part_ref[8 * 36:8 * 44, :]

    odd = (lane16 < 16) & (lax.rem(lane16, 2) == 1)
    group = lane8 // 16

    def y_weight(own_ref, beside_ref, inside):
        weight = harmonic(own_ref[...][:CX, :128], beside_ref[...][:CX, :128] * inside)
        weight = jnp.where(odd, pltpu.roll(weight, 128 - FACE_LANE, 1), 0.0)
        for shift in (16, 32, 64):
            weight = weight + pltpu.roll(weight, shift, 1)
        return weight

    def turned(v, d):
        return pltpu.roll(v, 128 - 16 * d, 1) if d else v

    mine = ys_hi_ref[...][:CX, 128:]
    first_mine = pltpu.roll(ys_lo_ref[...][:CX, 128:], 1, 1)
    theirs = pltpu.roll(yh_ref[...][:CX, 128:], 1, 1)
    weighted = y_weight(ys_hi_ref, yh_ref, y_high) * mine
    first_weighted = y_weight(ys_lo_ref, yl_ref, y_low) * first_mine
    face_y = {}
    for d in range(8):
        product = -weighted * turned(theirs, d)
        product = product[:8] + product[8:]
        for a in range(8):
            set_row(ROW_Y + 8 * ((a + d) % 8) + a, jnp.where(group == a, product, 0.0))
        if d < 5:
            inner = weighted * turned(mine, d) + first_weighted * turned(first_mine, d)
            face_y[d] = inner[:8] + inner[8:]

    wz_face = own(wz_ref, CZ - 1)
    wx_face = harmonic(hi_ref[FIELD_ROW:FIELD_ROW + 8, :], xh_ref[FIELD_ROW:FIELD_ROW + 8, :] * x_high)
    wx_first = harmonic(lo_ref[FIELD_ROW:FIELD_ROW + 8, :], xl_ref[FIELD_ROW:FIELD_ROW + 8, :] * x_low)
    for a in range(8):
        za = wz_face * basis(a, CZ - 1)
        xa = wx_face * hi_ref[16 * a:16 * a + 8, :]
        xa_first = wx_first * lo_ref[16 * a:16 * a + 8, :]
        for b in range(8):
            row = 8 * b + a
            set_row(ROW_Z + row, -fold(za * q_ref[10 + 2 * b]))
            x = xa * xh_ref[16 * b:16 * b + 8, :]
            set_row(ROW_X + row, -(x[:, :128] + x[:, 128:]))
            if b < a:
                continue
            x = xa * hi_ref[16 * b:16 * b + 8, :] + xa_first * lo_ref[16 * b:16 * b + 8, :]
            pair = PAIRS.index((a, b))
            value = part_ref[8 * pair:8 * pair + 8, :] + fold(za * basis(b, CZ - 1)) + x[:, :128] + x[:, 128:]
            d, place = (b - a, a) if b - a < 5 else (a - b + 8, b)
            set_row(ROW_OWN + pair, value + jnp.where(group == place, face_y[d], 0.0))

    total = acc_ref[pl.ds(0, 256, stride=8), :]
    for sub in range(1, 8):
        total = total + acc_ref[pl.ds(sub, 256, stride=8), :]
    summed = lax.dot_general(jnp.ones((8, 128), jnp.float32), total, (((1,), (1,)), ((), ())),
                             precision=HIGHEST, preferred_element_type=jnp.float32)
    pay_ref[0:1, :] = summed[0:1, :128]
    pay_ref[1:2, :] = summed[0:1, 128:]


def total_of(v):
    v = jnp.sum(v, axis=0, keepdims=True)
    if v.shape[1] == 256:
        v = v[:, :128] + v[:, 128:]
    return jnp.sum(v, axis=1, keepdims=True)


def dot(left, right):
    v = left * right
    return total_of(v[:, :128] + v[:, 128:])


def coarse_solve(tile_ref, lane_even):
    def partner(c):
        return jnp.where(lane_even, pltpu.roll(c, NDEV - 1, 1), pltpu.roll(c, 1, 1))

    def apply_e(c):
        shifted = [c, partner(c), pltpu.roll(c, NDEV - 2, 1), pltpu.roll(c, NDEV - 16, 1),
                   pltpu.roll(c, 2, 1), pltpu.roll(c, 16, 1)]
        total = None
        for o, v in enumerate(shifted):
            part = None
            for b in range(8):
                tile = (tile_ref[8 * (8 * o + b):8 * (8 * o + b) + 8, :])
                term = tile * v[b:b + 1, :]
                part = term if part is None else part + term
            total = part if total is None else total + part
        return total

    def solve(g):
        remainder, search, image = g, g, apply_e(g)
        current, along = dot(g, g), dot(g, image)
        solution = jnp.zeros_like(g)
        for iteration in range(KITERS):
            step = current / along
            solution = solution + step * search
            remainder = remainder - step * image
            if iteration == KITERS - 1:
                break
            applied = apply_e(remainder)
            updated = dot(remainder, remainder)
            ratio = updated / current
            along = dot(remainder, applied) + ratio * (2.0 * dot(remainder, image) + ratio * along)
            search = remainder + ratio * search
            image = applied + ratio * image
            current = updated
        return solution, g - remainder

    return solve


def coarse_kernel(pos_ref, gath_ref, r_ref, b_ref, q_in, xh_ref, xl_ref, xhq_ref, xlq_ref,
                  yh_ref, yl_ref, yhq_ref, ylq_ref, wx_ref, wy_ref, wz_ref, dg_ref, iv_ref, s_ref, u_ref,
                  sol_ref, res_ref, pre_ref, refined_ref, part_ref, scal_ref,
                  t_ref, tile_ref, pc_ref, q_ref):
    gz = pos_ref[2]
    dev = (pos_ref[0] * 8 + pos_ref[1]) * 2 + gz
    turned = gath_ref[...].T
    t_ref[0] = turned[:, :128]
    t_ref[1] = turned[:, 128:]

    def rows_at(index):
        return jnp.concatenate([t_ref[0, index, :], t_ref[1, index, :]], axis=1)

    for b in range(8):
        for a in range(8):
            row = ROW_OWN + PAIRS.index((min(a, b), max(a, b)))
            tile_ref[8 * b + a:8 * b + a + 1, :] = turned[row:row + 1, :]
    tile_ref[64:256, :] = turned[0:192, :]
    for b in range(8):
        tile_ref[256 + 8 * b:264 + 8 * b, :] = pltpu.roll(rows_at(pl.ds(ROW_Y + b, 8, stride=8)), 2, 1)
        tile_ref[320 + 8 * b:328 + 8 * b, :] = pltpu.roll(rows_at(pl.ds(ROW_X + b, 8, stride=8)), 16, 1)
    lane = lax.broadcasted_iota(jnp.int32, (8, NDEV), 1)
    solve = coarse_solve(tile_ref, lax.rem(lane, 2) == 0)
    g = turned[ROW_G:ROW_G + 8]
    h = turned[ROW_H:ROW_H + 8]
    rs = turned[ROW_RS:ROW_RS + 1]
    sas = turned[ROW_SAS:ROW_SAS + 1]
    c1, ec1 = solve(g)
    rz = total_of(rs) + dot(g, c1)
    curvature = total_of(sas) + dot(2.0 * h + ec1, c1)
    step = rz / curvature
    g2 = g - step * (h + ec1)
    c2, _ = solve(g2)
    g2c2 = dot(g2, c2)

    own_c = pltpu.roll(c1, lax.rem(NDEV - dev, NDEV), 1)
    other = dev + 1 - 2 * gz
    other_c = pltpu.roll(c1, lax.rem(NDEV - other, NDEV), 1)

    def at_lane(c, index):
        return c[:, index % NDEV:index % NDEV + 1]

    def spread(vectors, c):
        total = None
        for a, v in enumerate(vectors):
            term = v * c[a:a + 1, :]
            total = term if total is None else total + term
        return total

    mine, theirs = at_lane(own_c, 0), at_lane(other_c, 0)
    for z in range(CZ):
        pc_ref[z, :CX, :CY] = spread([b_ref[a, pl.ds(source_of(z, gz), 1)][0] for a in range(8)], mine)
    for j in range(2):
        pc_ref[CZ + j, :CX, :CY] = spread([q_in[10 + 2 * a + j] for a in range(8)], theirs)
    for z in range(10):
        pc_ref[z, CX:, :] = jnp.zeros((EX - CX, EY), jnp.float32)
    for step_x, ref, other in ((16, xh_ref, xhq_ref), (-16, xl_ref, xlq_ref)):
        for d in range(2):
            rows = spread([ref[16 * a + 8 * d:16 * a + 8 * d + 8, :] for a in range(8)], at_lane(own_c, step_x))
            to = CX + d if step_x > 0 else EX - 1 - d
            for z in range(CZ):
                pc_ref[z, to:to + 1, :CY] = rows[z:z + 1]
        to = CX if step_x > 0 else EX - 1
        last = other[LAST_ROW - FIELD_ROW:LAST_ROW - FIELD_ROW + 8, :] * at_lane(other_c, step_x)
        pc_ref[CZ, to:to + 1, :CY] = jnp.sum(last, axis=0, keepdims=True)

    lane16 = lax.broadcasted_iota(jnp.int32, (CX, 128), 1)
    lane8 = lax.broadcasted_iota(jnp.int32, (8, 128), 1)

    def by_group(index, c, lane):
        total = jnp.zeros(lane.shape, jnp.float32)
        for a in range(8):
            total = jnp.where(index == a, c[a:a + 1, :], total)
        return total

    def columns(ref, c):
        v = ref[...][:CX, 128:] * by_group(lane16 // 16, c, lane16)
        for shift in (64, 32, 16):
            v = v + pltpu.roll(v, shift, 1)
        return v

    def place_columns(z, high, low, layer):
        pc_ref[z, :CX, CY:] = jnp.where(lane16 < 2, pltpu.roll(high, (-2 * layer) % 128, 1), jnp.where(
            lane16 >= 126, pltpu.roll(low, (126 - 2 * layer) % 128, 1), 0.0))

    high, low = columns(yh_ref, at_lane(own_c, 2)), columns(yl_ref, at_lane(own_c, -2))
    for z in range(CZ):
        place_columns(z, high, low, z)
    high, low = columns(yhq_ref, at_lane(other_c, 2)), columns(ylq_ref, at_lane(other_c, -2))
    for j in range(2):
        place_columns(CZ + j, high, low, CZ - 1 - j)

    def corner(ref, side, c):
        v = ref[...][CX:, 128 * side:128 * side + 128] * by_group((lane8 - CORNER_LANE) // 4, c, lane8)
        v = jnp.where((lane8 >= CORNER_LANE) & (lane8 < CORNER_LANE + 32), v, 0.0)
        for shift in (112, 120, 124):
            v = v + pltpu.roll(v, shift, 1)
        return v

    for side, step_x in enumerate((16, -16)):
        high = corner(yh_ref, side, at_lane(own_c, step_x + 2))
        low = corner(yl_ref, side, at_lane(own_c, step_x - 2))
        rows = jnp.where(lane8 < 4, pltpu.roll(high, 128 - CORNER_LANE, 1), jnp.where(
            lane8 >= 124, pltpu.roll(low, 124 - CORNER_LANE, 1), 0.0))
        to = EX - 1 if side else CX
        for z in range(CZ):
            pc_ref[z, to:to + 1, CY:] = rows[z:z + 1]

    def at(z, ref):
        return apply_at(z, ref[z], ref[z + 1], ref[z - 1] if z else None, dg_ref[z], wx_ref[z],
                        wy_ref[z], wz_ref[z], wz_ref[z - 1] if z else None)

    def out_z(z):
        return z + gz * (CZ - 1 - 2 * z)

    def keep(ref, z, value):
        ref[pl.ds(out_z(z), 1)] = value[None, :CX, :CY]

    for z in range(9):
        image = u_ref[z] + at(z, pc_ref)
        residual = r_ref[z] - step * image
        q_ref[z] = iv_ref[z] * residual
        if z < CZ:
            keep(res_ref, z, residual)
            pre = s_ref[z, :CX, :CY] + pc_ref[z, :CX, :CY]
            keep(pre_ref, z, pre)
            keep(sol_ref, z, step * pre)
    own_c2 = pltpu.roll(c2, lax.rem(NDEV - dev, NDEV), 1)
    partial = jnp.zeros((8, 128), jnp.float32)
    for z in range(CZ):
        residual = res_ref[pl.ds(out_z(z), 1)][0]
        second = q_ref[z, :CX, :CY] + iv_ref[z, :CX, :CY] * (residual - at(z, q_ref)[:CX, :CY])
        partial = partial + fold(residual * second)
        for b in range(8):
            second = second + b_ref[b, pl.ds(out_z(z), 1)][0] * own_c2[b:b + 1, 0:1]
        keep(refined_ref, z, second)
    part_ref[...] = jnp.sum(partial, axis=0, keepdims=True)
    spot = lax.broadcasted_iota(jnp.int32, (1, 128), 1)
    scal_ref[...] = jnp.where(spot == 0, g2c2, rz)


def finish_kernel(parts_ref, scal_ref, refined_ref, pre_ref, out_ref):
    growth = (total_of(parts_ref[...]) + scal_ref[:, 0:1]) / scal_ref[:, 1:2]
    for z in range(CZ):
        out_ref[z] = refined_ref[z] + growth * pre_ref[z]


def call(kernel, out_shapes, scratch, n_args, smem_first=False):
    whole = pl.BlockSpec(memory_space=pltpu.VMEM)
    specs = [whole] * n_args
    if smem_first:
        specs[0] = pl.BlockSpec(memory_space=pltpu.SMEM)
    return pl.pallas_call(
        kernel,
        out_shape=[jax.ShapeDtypeStruct(s, jnp.float32) for s in out_shapes],
        in_specs=specs,
        out_specs=[whole] * len(out_shapes),
        scratch_shapes=[pltpu.VMEM(s, jnp.float32) for s in scratch],
        compiler_params=pltpu.CompilerParams(vmem_limit_bytes=VMEM_LIMIT),
    )


def ring(axis, to):
    n = lax.axis_size(axis)
    return [(i, (i + to) % n) for i in range(n)]


def gather_rows(row):
    rows = jnp.broadcast_to(row[None], (NDEV,) + row.shape)
    return lax.all_to_all(rows, AXES, 0, 0, tiled=False)


def local(right_side, conductivity, storage, basis):
    pos = jnp.stack([lax.axis_index(a) for a in AXES]).astype(jnp.int32)
    swap = [(0, 1), (1, 0)]

    def exchange(axis, hi, lo):
        return lax.ppermute(lo, axis, ring(axis, -1)), lax.ppermute(hi, axis, ring(axis, 1))

    box, faces, small = (CZ, CX, CY), (FACE_ROWS, CY), (8, 256)
    fields = jnp.stack([conductivity, storage, right_side])
    b = basis.astype(jnp.float32)
    hi, lo, small_hi, small_lo, layers = call(
        pack_x_kernel, [faces, faces, small, small, (26, CX, CY)], [], 3, True)(pos, fields, b)
    corner_high, corner_low = exchange("gx", small_hi, small_lo)
    main_hi, main_lo = call(pack_y_kernel, [(CX, 256)] * 2, [], 3, True)(pos, fields, b)

    def with_corners(main, half):
        columns = slice(128 * half, 128 * half + 128)
        return jnp.concatenate(
            [main, jnp.concatenate([corner_high[:, columns], corner_low[:, columns]], axis=1)], axis=0)

    y_hi, y_lo = with_corners(main_hi, 1), with_corners(main_lo, 0)
    y_hi, y_lo, hi, lo, layers, gate = lax.optimization_barrier((y_hi, y_lo, hi, lo, layers, pos))
    y_high, y_low = exchange("gy", y_hi, y_lo)
    x_high, x_low = exchange("gx", hi, lo)
    other_layers = lax.ppermute(layers, "gz", swap)
    part, = call(gram_kernel, [(44 * 8, 128)], [], 3, True)(gate, fields, b)
    y_high, y_low, x_high, x_low, other_layers, part = lax.optimization_barrier(
        (y_high, y_low, x_high, x_low, other_layers, part))
    other_yh = lax.ppermute(y_high, "gz", swap)
    other_yl = lax.ppermute(y_low, "gz", swap)
    other_xh = lax.ppermute(x_high[FIELD_ROW:], "gz", swap)
    other_xl = lax.ppermute(x_low[FIELD_ROW:], "gz", swap)

    ext = (EZ, EX, EY)
    pay, r_ext, wx, wy, wz, dg, iv, s, u = call(
        prepare_kernel, [(2, 128)] + [ext] * 8, [ext, ext, ext, (2048, 128)], 17, True,
    )(pos, fields, part, b, other_layers, hi, lo, x_high, x_low, other_xh, other_xl,
      y_hi, y_lo, y_high, y_low, other_yh, other_yl)
    gathered = gather_rows(pay).reshape(NDEV, 256)
    sol, res, pre, refined, total, scal = call(
        coarse_kernel, [box] * 4 + [(1, 128)] * 2,
        [(2, 256, 128), (384, 256), ext, ext], 20, True,
    )(pos, gathered, r_ext, b, other_layers, x_high, x_low, other_xh, other_xl,
      y_high, y_low, other_yh, other_yl, wx, wy, wz, dg, iv, s, u)
    parts = gather_rows(total).reshape(NDEV, 128)
    direction, = call(finish_kernel, [box], [], 4)(parts, scal, refined, pre)
    return sol, res, direction


def solution(mesh):
    spec = P("gz", "gx", "gy")
    return jax.shard_map(
        local,
        mesh=mesh,
        in_specs=(spec, spec, spec, P(None, "gz", "gx", "gy")),
        out_specs=(spec, spec, spec),
        check_vma=False,
    )
```

time: 114 us -> 82 us (0.72)
  waiting for transfers between devices: 35.1 us -> 7.11 us
  blocking collectives: 18.2 us -> 41.4 us
  local copies, waits for them, and re-layouts: 10.9 us -> 0.19 us
  starting transfers between devices: 26.6 us -> 17.7 us
  other arithmetic: 9.8 us -> 1.34 us
    all_to_all x1 -> x2, blocking collectives: 18.2 us -> 41.4 us  [gather_rows(): return lax.all_to_all(rows, AXES, 0, 0, tiled=False)]
    all_to_all x1 -> x0, waiting for transfers between devices: 15.1 us -> none  [gather_rows(): lax.all_to_all(rows, AXES, 0, 0, tiled=False).reshape(NDEV, row.shape[-1])]
    ppermute x10 -> x11, waiting for transfers between devices: 20.1 us -> 7.11 us  [the longest x3 6 us: exchange(): lax.ppermute(hi, axis, ring(axis, 1))]
    all_to_all x1 -> x0, starting transfers between devices: 6.76 us -> none  [gather_rows(): lax.all_to_all(rows, AXES, 0, 0, tiled=False).reshape(NDEV, row.shape[-1])]
    unnamed x28 -> x7, local copies, waits for them, and re-layouts: 6.5 us -> 0.03 us
    convert_element_type x5 -> x1, other arithmetic: 4.93 us -> 1.22 us  [local(): b = basis.astype(jnp.float32)]
    pallas_call x1 -> x4, Pallas kernels: 4.9 us -> 7.25 us  [the longest x1 2.78 us: local(): call(prepare_kernel, [(2, 128)] + [ext] * 8, [ext, ext, ext, (2048, 128)]...]
    ppermute x10 -> x11, starting transfers between devices: 19.8 us -> 17.7 us  [the longest x3 11.4 us: exchange(): lax.ppermute(lo, axis, ring(axis, -1))]
  transfers between devices with their start and end apart: 11 -> 11, of which waited for: 6 -> 4; matrix products, arithmetic and copies ran while one was open for 11% -> 0% of each run, Pallas kernels for 0% -> 4%
where the time goes in v3:
time: 82 us; the launch traced here: 81.9 us
  blocking collectives  41.4 us (50%)
  starting transfers between devices  17.7 us (22%)
  Pallas kernels  13.3 us (16%)
  waiting for transfers between devices  7.11 us (9%)
  other arithmetic  1.34 us (2%)
    all_to_all x2, blocking collectives, gather_rows(): return lax.all_to_all(rows, AXES, 0, 0, tiled=False)  41.4 us
    ppermute x3, starting transfers between devices, exchange(): lax.ppermute(lo, axis, ring(axis, -1))  11.4 us
    ppermute x3, waiting for transfers between devices, exchange(): lax.ppermute(hi, axis, ring(axis, 1))  6 us
    pallas_call x1, Pallas kernels, local(): call(coarse_kernel, [box] * 4 + [(1, 128)] * 2, [(2, 256, 128), (384, 256...  5.19 us
    pallas_call x1, Pallas kernels, local(): call(prepare_kernel, [(2, 128)] + [ext] * 8, [ext, ext, ext, (2048, 128)]...  2.78 us
    pallas_call x1, Pallas kernels, local(): part, = call(gram_kernel, [(44 * 8, 128)], [], 3, True)(gate, fields, b)  2.62 us
    ppermute x1, starting transfers between devices, local(): other_xl = lax.ppermute(x_low[FIELD_ROW:], 'gz', swap)  2.14 us
    ppermute x1, starting transfers between devices, local(): other_layers = lax.ppermute(layers, 'gz', swap)  2.1 us
  transfers between devices with their start and end apart: 11, of which 4 were waited for; matrix products, arithmetic and copies ran while one was open for 0% of the time, Pallas kernels for 4%

profile of v3, /device:TPU:1, one launch (start us, length us, event | category | flops | bytes accessed | tf_op | source)
XLA Modules:
  0.0 81.9 jit_solution(3372354595650745241)
XLA Ops:
  0.7 1.2 %convert_element_type.3.b_ref = f32[8,8,16,256]{3,2,1,0:T(8,128)S(1)} convert(bf16[8,8,16,256]{3,2,1,0:T(8,128)(2,1)} %param.7) | non-fusion elementwise | flops 262144 | bytes 1572864 | tf_op jit(solution)/shard_map/convert_element_type | solution.py:551
  1.9 0.1 pad_add_fusion.pos_ref
  2.0 0.8 shard_map.68
  2.8 5.8 %collective-permute-start = (f32[8,256]{1,0:T(8,128)S(1)}, f32[8,256]{1,0:T(8,128)S(1)}, u32[]{:S(2)}, u32[]{:S(2)}) collective-permute-start(f32[8,256]{1,0:T(8,128)S(1)} %get-tuple-element.38), channel_id=1, source_target_pairs={{0,240},{16,0},{32,16},{48,32},{64,48},{80,64},{96,80},{112,96},{1... | collective-permute-start | bytes 24584 | tf_op jit(solution)/shard_map/ppermute | solution.py:547
  8.7 0.0 collective-permute-start.1
  8.7 1.0 %shard_map.67 = (f32[16,256]{1,0:T(8,128)S(1)}, f32[16,256]{1,0:T(8,128)S(1)}) custom-call(s32[3]{0:T(128)S(1)} %pad_add_fusion.pos_ref, f32[3,8,16,256]{3,2,1,0:T(8,128)S(1)} %pad_maximum_fusion.f_ref.f_in, f32[8,8,16,256]{3,2,1,0:T(8,128)S(1)} %convert_element_type.3.b_ref), custom_call_target="tpu_custom_call" | custom-call | tf_op jit(solution)/shard_map/pallas_call | solution.py:555
  9.7 0.0 collective-permute-done
  9.7 4.8 %collective-permute-done.1 = f32[8,256]{1,0:T(8,128)S(1)} collective-permute-done((f32[8,256]{1,0:T(8,128)S(1)}, f32[8,256]{1,0:T(8,128)S(1)}, u32[]{:S(2)}, u32[]{:S(2)}) %collective-permute-start.1) | collective-permute-done | bytes 8224 | tf_op jit(solution)/shard_map/ppermute | solution.py:547
  14.5 2.1 %collective-permute-start.6 = (f32[26,16,256]{2,1,0:T(8,128)S(1)}, f32[26,16,256]{2,1,0:T(8,128)S(1)}, u32[]{:S(2)}, u32[]{:S(2)}) collective-permute-start(f32[26,16,256]{2,1,0:T(8,128)S(1)} %get-tuple-element.48), channel_id=1, source_target_pairs={{0,1},{1,0},{2,3},{3,2},{4,5},{5,4},{6,7},{7,6},{8,9},{9,8},{10,11... | collective-permute-start | bytes 1277960 | tf_op jit(solution)/shard_map/ppermute | solution.py:566
  16.6 0.0 collective-permute-start.4
  16.6 1.5 %collective-permute-start.5 = (f32[216,256]{1,0:T(8,128)S(1)}, f32[216,256]{1,0:T(8,128)S(1)}, u32[]{:S(2)}, u32[]{:S(2)}) collective-permute-start(f32[216,256]{1,0:T(8,128)S(1)} %get-tuple-element.47.hi_ref), channel_id=1, source_target_pairs={{0,16},{16,32},{32,48},{48,64},{64,80},{80,96},{96,112},{112,128},... | collective-permute-start | bytes 663560 | tf_op jit(solution)/shard_map/ppermute | solution.py:547
  18.1 5.6 %collective-permute-start.2 = (f32[24,256]{1,0:T(8,128)S(1)}, f32[24,256]{1,0:T(8,128)S(1)}, u32[]{:S(2)}, u32[]{:S(2)}) collective-permute-start(f32[24,256]{1,0:T(8,128)S(1)} %get-tuple-element.44.ys_lo_ref), channel_id=1, source_target_pairs={{0,14},{2,0},{4,2},{6,4},{8,6},{10,8},{12,10},{14,12},{1,15},{3,1}... | collective-permute-start | bytes 73736 | tf_op jit(solution)/shard_map/ppermute | solution.py:547
  23.7 0.0 collective-permute-start.3
  23.7 2.6 %shard_map.69.part_ref = f32[352,128]{1,0:T(8,128)S(1)} custom-call(s32[3]{0:T(128)S(1)} %pad_add_fusion.pos_ref, f32[3,8,16,256]{3,2,1,0:T(8,128)S(1)} %pad_maximum_fusion.f_ref.f_in, f32[8,8,16,256]{3,2,1,0:T(8,128)S(1)} %convert_element_type.3.b_ref), custom_call_target="tpu_custom_call" | custom-call | tf_op jit(solution)/shard_map/pallas_call | solution.py:567
  26.3 0.0 collective-permute-done.2.yh_ref
  26.3 1.2 %collective-permute-done.3.yl_ref = f32[24,256]{1,0:T(8,128)S(1)} collective-permute-done((f32[24,256]{1,0:T(8,128)S(1)}, f32[24,256]{1,0:T(8,128)S(1)}, u32[]{:S(2)}, u32[]{:S(2)}) %collective-permute-start.3) | collective-permute-done | bytes 24608 | tf_op jit(solution)/shard_map/ppermute | solution.py:547
  27.5 0.0 collective-permute-done.4.xh_ref
  27.5 0.0 collective-permute-done.5.xl_ref
  27.6 0.0 collective-permute-done.6.q_ref.q_in
  27.6 2.1 %collective-permute-start.8 = (f32[88,256]{1,0:T(8,128)S(1)}, f32[88,256]{1,0:T(8,128)S(1)}, u32[]{:S(2)}, u32[]{:S(2)}) collective-permute-start(f32[88,256]{1,0:T(8,128)S(1)} %slice.23), channel_id=1, source_target_pairs={{0,1},{1,0},{2,3},{3,2},{4,5},{5,4},{6,7},{7,6},{8,9},{9,8},{10,11... | collective-permute-start | bytes 270344 | tf_op jit(solution)/shard_map/ppermute | solution.py:573
  29.7 0.1 collective-permute-start.7
  29.8 0.4 collective-permute-start.9
  30.2 0.1 collective-permute-start.10
  30.3 0.7 collective-permute-done.9.yhq_ref
  31.1 0.3 collective-permute-done.10.ylq_ref
  31.4 2.8 %shard_map.70 = (f32[2,128]{1,0:T(2,128)S(1)}, f32[12,24,384]{2,1,0:T(8,128)S(1)}, f32[12,24,384]{2,1,0:T(8,128)S(1)}, f32[12,24,384]{2,1,0:T(8,128)S(1)}, f32[1...) custom-call(s32[3]{0:T(128)S(1)} %pad_add_fusion.pos_ref, ...), custom_call_target="tpu_custom_call" | custom-call | tf_op jit(solution)/shard_map/pallas_call | solution.py:576
  34.2 0.1 broadcast_in_dim.6
  34.3 23.2 %all_to_all.10 = f32[256,2,128]{2,1,0:T(2,128)S(1)} all-to-all(f32[256,2,128]{2,1,0:T(2,128)S(1)} %broadcast_in_dim.6), channel_id=1, replica_groups=mesh['gx'=16,'gy'=8,'gz'=2] {'gx','gy','gz'}, dimensions={0} | all-to-all | bytes 524288 | tf_op jit(solution)/shard_map/all_to_all | solution.py:539
  57.5 5.2 %shard_map.71 = (f32[8,16,256]{2,1,0:T(8,128)}, f32[8,16,256]{2,1,0:T(8,128)}, f32[8,16,256]{2,1,0:T(8,128)S(1)}, f32[8,16,256]{2,1,0:T(8,128)S(1)}, f32[1,128]{1,0:T(1,128)S(1)}, /*index=5*/f32[1,128]{1,0:T(1,128)S(1)}) custom-call(s32[3]{0:T(128)S(1)} %pad_add_fusion.pos_ref, f32[256,256]{1,0:T(8,128)S(1)} %bitcast.12, ...), custom_call_target="tpu_custom_call" | custom-call | tf_op jit(solution)/shard_map/pallas_call | solution.py:581
  62.7 0.1 broadcast_in_dim.16
  62.8 18.2 %all_to_all.11 = f32[256,1,128]{2,1,0:T(1,128)S(1)} all-to-all(f32[256,1,128]{2,1,0:T(1,128)S(1)} %broadcast_in_dim.16), channel_id=1, replica_groups=mesh['gx'=16,'gy'=8,'gz'=2] {'gx','gy','gz'}, dimensions={0} | all-to-all | bytes 262144 | tf_op jit(solution)/shard_map/all_to_all | solution.py:539
  81.0 0.9 %shard_map.72 = f32[8,16,256]{2,1,0:T(8,128)} custom-call(f32[256,128]{1,0:T(8,128)S(1)} %bitcast.13, f32[1,128]{1,0:T(1,128)S(1)} %get-tuple-element.68.scal_ref, f32[8,16,256]{2,1,0:T(8,128)S(1)} %get-tuple-element.69.refined_ref, f32[8,16,256]{2,1,0:T(8,128)S(1)} %get-tuple-element.70.pre_ref), custom_call_target="tpu_custom_call" | custom-call | tf_op jit(solution)/shard_map/pallas_call | solution.py:587
  (15 shorter events, 0.1 us)
Async XLA Ops:
  0.6 1.3 %copy-start = (f32[8,16,256]{2,1,0:T(8,128)S(1)}, f32[8,16,256]{2,1,0:T(8,128)}, u32[]{:S(2)}) copy-start(f32[8,16,256]{2,1,0:T(8,128)} %param.4) | copy-start | bytes 393220
  0.6 1.3 %copy-start.1 = (f32[8,16,256]{2,1,0:T(8,128)S(1)}, f32[8,16,256]{2,1,0:T(8,128)}, u32[]{:S(2)}) copy-start(f32[8,16,256]{2,1,0:T(8,128)} %param.6) | copy-start | bytes 393220
  0.7 1.3 %copy-start.2 = (f32[8,16,256]{2,1,0:T(8,128)S(1)}, f32[8,16,256]{2,1,0:T(8,128)}, u32[]{:S(2)}) copy-start(f32[8,16,256]{2,1,0:T(8,128)} %param.5) | copy-start | bytes 393220
  2.8 6.9 %collective-permute-start = (f32[8,256]{1,0:T(8,128)S(1)}, f32[8,256]{1,0:T(8,128)S(1)}, u32[]{:S(2)}, u32[]{:S(2)}) collective-permute-start(f32[8,256]{1,0:T(8,128)S(1)} %get-tuple-element.38), channel_id=1, source_target_pairs={{0,240},{16,0},{32,16},{48,32},{64,48},{80,64},{96,80},{112,96},{1... | collective-permute-start | bytes 24584 | tf_op jit(solution)/shard_map/ppermute | solution.py:547
  8.7 5.8 %collective-permute-start.1 = (f32[8,256]{1,0:T(8,128)S(1)}, f32[8,256]{1,0:T(8,128)S(1)}, u32[]{:S(2)}, u32[]{:S(2)}) collective-permute-start(f32[8,256]{1,0:T(8,128)S(1)} %get-tuple-element.39), channel_id=1, source_target_pairs={{0,16},{16,32},{32,48},{48,64},{64,80},{80,96},{96,112},{112,128},... | collective-permute-start | bytes 24584 | tf_op jit(solution)/shard_map/ppermute | solution.py:547
  14.5 13.1 %collective-permute-start.6 = (f32[26,16,256]{2,1,0:T(8,128)S(1)}, f32[26,16,256]{2,1,0:T(8,128)S(1)}, u32[]{:S(2)}, u32[]{:S(2)}) collective-permute-start(f32[26,16,256]{2,1,0:T(8,128)S(1)} %get-tuple-element.48), channel_id=1, source_target_pairs={{0,1},{1,0},{2,3},{3,2},{4,5},{5,4},{6,7},{7,6},{8,9},{9,8},{10,11... | collective-permute-start | bytes 1277960 | tf_op jit(solution)/shard_map/ppermute | solution.py:566
  16.6 10.9 %collective-permute-start.4 = (f32[216,256]{1,0:T(8,128)S(1)}, f32[216,256]{1,0:T(8,128)S(1)}, u32[]{:S(2)}, u32[]{:S(2)}) collective-permute-start(f32[216,256]{1,0:T(8,128)S(1)} %get-tuple-element.46.lo_ref), channel_id=1, source_target_pairs={{0,240},{16,0},{32,16},{48,32},{64,48},{80,64},{96,80},{112,96},{1... | collective-permute-start | bytes 663560 | tf_op jit(solution)/shard_map/ppermute | solution.py:547
  16.6 10.9 %collective-permute-start.5 = (f32[216,256]{1,0:T(8,128)S(1)}, f32[216,256]{1,0:T(8,128)S(1)}, u32[]{:S(2)}, u32[]{:S(2)}) collective-permute-start(f32[216,256]{1,0:T(8,128)S(1)} %get-tuple-element.47.hi_ref), channel_id=1, source_target_pairs={{0,16},{16,32},{32,48},{48,64},{64,80},{80,96},{96,112},{112,128},... | collective-permute-start | bytes 663560 | tf_op jit(solution)/shard_map/ppermute | solution.py:547
  18.1 8.2 %collective-permute-start.2 = (f32[24,256]{1,0:T(8,128)S(1)}, f32[24,256]{1,0:T(8,128)S(1)}, u32[]{:S(2)}, u32[]{:S(2)}) collective-permute-start(f32[24,256]{1,0:T(8,128)S(1)} %get-tuple-element.44.ys_lo_ref), channel_id=1, source_target_pairs={{0,14},{2,0},{4,2},{6,4},{8,6},{10,8},{12,10},{14,12},{1,15},{3,1}... | collective-permute-start | bytes 73736 | tf_op jit(solution)/shard_map/ppermute | solution.py:547
  23.7 3.9 %collective-permute-start.3 = (f32[24,256]{1,0:T(8,128)S(1)}, f32[24,256]{1,0:T(8,128)S(1)}, u32[]{:S(2)}, u32[]{:S(2)}) collective-permute-start(f32[24,256]{1,0:T(8,128)S(1)} %get-tuple-element.45.ys_hi_ref), channel_id=1, source_target_pairs={{0,2},{2,4},{4,6},{6,8},{8,10},{10,12},{12,14},{14,0},{1,3},{3,5},... | collective-permute-start | bytes 73736 | tf_op jit(solution)/shard_map/ppermute | solution.py:547
  27.6 3.9 %collective-permute-start.8 = (f32[88,256]{1,0:T(8,128)S(1)}, f32[88,256]{1,0:T(8,128)S(1)}, u32[]{:S(2)}, u32[]{:S(2)}) collective-permute-start(f32[88,256]{1,0:T(8,128)S(1)} %slice.23), channel_id=1, source_target_pairs={{0,1},{1,0},{2,3},{3,2},{4,5},{5,4},{6,7},{7,6},{8,9},{9,8},{10,11... | collective-permute-start | bytes 270344 | tf_op jit(solution)/shard_map/ppermute | solution.py:573
  29.7 1.7 %collective-permute-start.7 = (f32[88,256]{1,0:T(8,128)S(1)}, f32[88,256]{1,0:T(8,128)S(1)}, u32[]{:S(2)}, u32[]{:S(2)}) collective-permute-start(f32[88,256]{1,0:T(8,128)S(1)} %slice.22), channel_id=1, source_target_pairs={{0,1},{1,0},{2,3},{3,2},{4,5},{5,4},{6,7},{7,6},{8,9},{9,8},{10,11... | collective-permute-start | bytes 270344 | tf_op jit(solution)/shard_map/ppermute | solution.py:572
  29.8 1.3 %collective-permute-start.9 = (f32[24,256]{1,0:T(8,128)S(1)}, f32[24,256]{1,0:T(8,128)S(1)}, u32[]{:S(2)}, u32[]{:S(2)}) collective-permute-start(f32[24,256]{1,0:T(8,128)S(1)} %collective-permute-done.2.yh_ref), channel_id=1, source_target_pairs={{0,1},{1,0},{2,3},{3,2},{4,5},{5,4},{6,7},{7,6},{8,9},{9,8},{10,11... | collective-permute-start | bytes 73736 | tf_op jit(solution)/shard_map/ppermute | solution.py:570
  30.2 1.2 %collective-permute-start.10 = (f32[24,256]{1,0:T(8,128)S(1)}, f32[24,256]{1,0:T(8,128)S(1)}, u32[]{:S(2)}, u32[]{:S(2)}) collective-permute-start(f32[24,256]{1,0:T(8,128)S(1)} %collective-permute-done.3.yl_ref), channel_id=1, source_target_pairs={{0,1},{1,0},{2,3},{3,2},{4,5},{5,4},{6,7},{7,6},{8,9},{9,8},{10,11... | collective-permute-start | bytes 73736 | tf_op jit(solution)/shard_map/ppermute | solution.py:571

commit v4 on v3

--- a/solution.py
+++ b/solution.py
@@ -18,8 +18,8 @@
 ROW_Z, ROW_Y, ROW_X, ROW_OWN, ROW_RS, ROW_SAS, ROW_G, ROW_H = 0, 64, 128, 192, 228, 229, 232, 240
 DEPTHS = (4, 3, 3)
 STEPS = [(f, d) for f in range(3) for d in range(DEPTHS[f])]
-FIELD_ROW, LAST_ROW, FACE_ROWS = 128, 208, 216
-FACE_LANE, CORNER_LANE = 96, 40
+FIELD_ROW, LAST_ROW, CORNER_ROW = 128, 208, 216
+FACE_LANE = 96
 VMEM_LIMIT = 24 * 1024 * 1024
 
 
@@ -64,7 +64,7 @@
     return z + gz * (CZ - 1 - 2 * z)
 
 
-def pack_x_kernel(pos_ref, f_ref, b_ref, hi_ref, lo_ref, small_hi_ref, small_lo_ref, q_ref):
+def pack_x_kernel(pos_ref, f_ref, b_ref, hi_ref, lo_ref, q_ref):
     gz = pos_ref[2]
     for z in range(CZ):
         src, j = source_of(z, gz), CZ - 1 - z
@@ -89,16 +89,6 @@
                 lo_ref[LAST_ROW + a:LAST_ROW + a + 1, :] = v[0:1]
             if j < 2:
                 q_ref[10 + 2 * a + j] = v
-    lane = lax.broadcasted_iota(jnp.int32, (8, 128), 1)
-    rows = [FIELD_ROW + 8 * t for t in range(10)] + [16 * a for a in range(8)]
-    for ref, small_ref in ((hi_ref, small_hi_ref), (lo_ref, small_lo_ref)):
-        first = last = jnp.zeros((8, 128), jnp.float32)
-        for i, row in enumerate(rows):
-            mask = (lane >= 4 * i) & (lane < 4 * i + 4)
-            first = jnp.where(mask, pltpu.roll(ref[row:row + 8, :128], 4 * i, 1), first)
-            last = jnp.where(mask, pltpu.roll(ref[row:row + 8, 128:], 4 * i + 4, 1), last)
-        small_ref[:, :128] = first
-        small_ref[:, 128:] = last
 
 
 def pack_y_kernel(pos_ref, f_ref, b_ref, hi_ref, lo_ref):
@@ -166,34 +156,31 @@
     y_high, y_low = flag(gy < 7), flag(gy > 0)
     lane16 = lax.broadcasted_iota(jnp.int32, (CX, 128), 1)
     lane8 = lax.broadcasted_iota(jnp.int32, (8, 128), 1)
+    lane24 = lax.broadcasted_iota(jnp.int32, (EX, 128), 1)
+    row24 = lax.broadcasted_iota(jnp.int32, (EX, 128), 0)
+    inside_x = jnp.where(row24 < CX, 1.0, jnp.where(row24 < CX + 4, x_high, x_low))
     outs = (k_ref, st_ref, r_ref)
 
-    def beside(lane, high, low, offset, f):
-        high = pltpu.roll(high, -offset % 128, 1)
-        low = pltpu.roll(low, (124 - offset) % 128, 1)
+    def main(f, z, value, high, low, layer):
+        ref, offset = outs[f], 32 * f + 4 * layer
+        high = pltpu.roll(high[:, :128], -offset % 128, 1)
+        low = pltpu.roll(low[:, :128], (124 - offset) % 128, 1)
         if f == 0:
-            high, low = high * y_high, low * y_low
-        return jnp.where(lane < 4, high, jnp.where(lane >= 124, low, 1.0))
-
-    def main(f, z, value, high, low, layer):
-        ref = outs[f]
+            high, low = high * (inside_x * y_high), low * (inside_x * y_low)
         ref[z, :CX, :CY] = value
-        ref[z, :CX, CY:] = beside(lane16, high[:CX, :128], low[:CX, :128], 32 * f + 4 * layer, f)
+        ref[z, :, CY:] = jnp.where(lane24 < 4, high, jnp.where(lane24 >= 124, low, 1.0))
         if f:
-            ref[z, CX:, :] = jnp.ones((EX - CX, EY), jnp.float32)
-
-    def edges(t, sides, high, low, places):
+            ref[z, CX:, :CY] = jnp.ones((EX - CX, CY), jnp.float32)
+
+    def edges(t, sides, places):
         f, d = STEPS[t]
         for side, (ref, inside, row) in enumerate(sides):
             wide = ref[row + 8 * t:row + 8 * t + 8, :]
-            columns = slice(128 * side, 128 * side + 128)
-            corner = beside(lane8, high[CX:, columns], low[CX:, columns], 4 * t, f)
             if f == 0:
-                wide, corner = wide * inside, corner * inside
+                wide = wide * inside
             to = EX - 1 - d if side else CX + d
             for z, layer in places:
                 outs[f][z, to:to + 1, :CY] = wide[layer:layer + 1]
-                outs[f][z, to:to + 1, CY:] = corner[layer:layer + 1]
 
     high, low = yh_ref[...], yl_ref[...]
     for z in range(CZ):
@@ -202,7 +189,7 @@
             main(f, z, f_in[f, pl.ds(src, 1)][0], high, low, z)
     sides = ((xh_ref, x_high, FIELD_ROW), (xl_ref, x_low, FIELD_ROW))
     for t in range(len(STEPS)):
-        edges(t, sides, high, low, [(z, z) for z in range(CZ)])
+        edges(t, sides, [(z, z) for z in range(CZ)])
     high, low = yhq_ref[...], ylq_ref[...]
     first_layer = (0, 4, 7)
     for f in range(3):
@@ -210,7 +197,7 @@
             main(f, CZ + j, q_ref[first_layer[f] + j], high, low, CZ - 1 - j)
     sides = ((xhq_ref, x_high, 0), (xlq_ref, x_low, 0))
     for t, (f, d) in enumerate(STEPS):
-        edges(t, sides, high, low, [(CZ + j, CZ - 1 - j) for j in range(DEPTHS[f])])
+        edges(t, sides, [(CZ + j, CZ - 1 - j) for j in range(DEPTHS[f])])
 
     for z in range(11):
         k = k_ref[z]
@@ -422,7 +409,7 @@
     for j in range(2):
         pc_ref[CZ + j, :CX, :CY] = spread([q_in[10 + 2 * a + j] for a in range(8)], theirs)
     for z in range(10):
-        pc_ref[z, CX:, :] = jnp.zeros((EX - CX, EY), jnp.float32)
+        pc_ref[z, CX:, :CY] = jnp.zeros((EX - CX, CY), jnp.float32)
     for step_x, ref, other in ((16, xh_ref, xhq_ref), (-16, xl_ref, xlq_ref)):
         for d in range(2):
             rows = spread([ref[16 * a + 8 * d:16 * a + 8 * d + 8, :] for a in range(8)], at_lane(own_c, step_x))
@@ -433,47 +420,35 @@
         last = other[LAST_ROW - FIELD_ROW:LAST_ROW - FIELD_ROW + 8, :] * at_lane(other_c, step_x)
         pc_ref[CZ, to:to + 1, :CY] = jnp.sum(last, axis=0, keepdims=True)
 
-    lane16 = lax.broadcasted_iota(jnp.int32, (CX, 128), 1)
-    lane8 = lax.broadcasted_iota(jnp.int32, (8, 128), 1)
-
-    def by_group(index, c, lane):
-        total = jnp.zeros(lane.shape, jnp.float32)
+    lane24 = lax.broadcasted_iota(jnp.int32, (EX, 128), 1)
+    row24 = lax.broadcasted_iota(jnp.int32, (EX, 128), 0)
+
+    def by_group(c):
+        total = jnp.zeros((EX, 128), jnp.float32)
         for a in range(8):
-            total = jnp.where(index == a, c[a:a + 1, :], total)
+            total = jnp.where(lane24 // 16 == a, c[a:a + 1, :], total)
         return total
 
-    def columns(ref, c):
-        v = ref[...][:CX, 128:] * by_group(lane16 // 16, c, lane16)
+    def columns(ref, c, step_y, corners):
+        high_x = low_x = 0.0
+        if corners:
+            high_x, low_x = by_group(at_lane(c, 16 + step_y)), by_group(at_lane(c, step_y - 16))
+        v = jnp.where(row24 < CX, by_group(at_lane(c, step_y)), jnp.where(row24 < CX + 4, high_x, low_x))
+        v = v * ref[...][:, 128:]
         for shift in (64, 32, 16):
             v = v + pltpu.roll(v, shift, 1)
         return v
 
     def place_columns(z, high, low, layer):
-        pc_ref[z, :CX, CY:] = jnp.where(lane16 < 2, pltpu.roll(high, (-2 * layer) % 128, 1), jnp.where(
-            lane16 >= 126, pltpu.roll(low, (126 - 2 * layer) % 128, 1), 0.0))
-
-    high, low = columns(yh_ref, at_lane(own_c, 2)), columns(yl_ref, at_lane(own_c, -2))
+        pc_ref[z, :, CY:] = jnp.where(lane24 < 2, pltpu.roll(high, (-2 * layer) % 128, 1), jnp.where(
+            lane24 >= 126, pltpu.roll(low, (126 - 2 * layer) % 128, 1), 0.0))
+
+    high, low = columns(yh_ref, own_c, 2, True), columns(yl_ref, own_c, -2, True)
     for z in range(CZ):
         place_columns(z, high, low, z)
-    high, low = columns(yhq_ref, at_lane(other_c, 2)), columns(ylq_ref, at_lane(other_c, -2))
+    high, low = columns(yhq_ref, other_c, 2, False), columns(ylq_ref, other_c, -2, False)
     for j in range(2):
         place_columns(CZ + j, high, low, CZ - 1 - j)
-
-    def corner(ref, side, c):
-        v = ref[...][CX:, 128 * side:128 * side + 128] * by_group((lane8 - CORNER_LANE) // 4, c, lane8)
-        v = jnp.where((lane8 >= CORNER_LANE) & (lane8 < CORNER_LANE + 32), v, 0.0)
-        for shift in (112, 120, 124):
-            v = v + pltpu.roll(v, shift, 1)
-        return v
-
-    for side, step_x in enumerate((16, -16)):
-        high = corner(yh_ref, side, at_lane(own_c, step_x + 2))
-        low = corner(yl_ref, side, at_lane(own_c, step_x - 2))
-        rows = jnp.where(lane8 < 4, pltpu.roll(high, 128 - CORNER_LANE, 1), jnp.where(
-            lane8 >= 124, pltpu.roll(low, 124 - CORNER_LANE, 1), 0.0))
-        to = EX - 1 if side else CX
-        for z in range(CZ):
-            pc_ref[z, to:to + 1, CY:] = rows[z:z + 1]
 
     def at(z, ref):
         return apply_at(z, ref[z], ref[z + 1], ref[z - 1] if z else None, dg_ref[z], wx_ref[z],
@@ -546,37 +521,37 @@
     def exchange(axis, hi, lo):
         return lax.ppermute(lo, axis, ring(axis, -1)), lax.ppermute(hi, axis, ring(axis, 1))
 
-    box, faces, small = (CZ, CX, CY), (FACE_ROWS, CY), (8, 256)
+    box, faces = (CZ, CX, CY), (CORNER_ROW, CY)
     fields = jnp.stack([conductivity, storage, right_side])
     b = basis.astype(jnp.float32)
-    hi, lo, small_hi, small_lo, layers = call(
-        pack_x_kernel, [faces, faces, small, small, (26, CX, CY)], [], 3, True)(pos, fields, b)
-    corner_high, corner_low = exchange("gx", small_hi, small_lo)
     main_hi, main_lo = call(pack_y_kernel, [(CX, 256)] * 2, [], 3, True)(pos, fields, b)
-
-    def with_corners(main, half):
-        columns = slice(128 * half, 128 * half + 128)
-        return jnp.concatenate(
-            [main, jnp.concatenate([corner_high[:, columns], corner_low[:, columns]], axis=1)], axis=0)
-
-    y_hi, y_lo = with_corners(main_hi, 1), with_corners(main_lo, 0)
-    y_hi, y_lo, hi, lo, layers, gate = lax.optimization_barrier((y_hi, y_lo, hi, lo, layers, pos))
-    y_high, y_low = exchange("gy", y_hi, y_lo)
+    main_high, main_low = exchange("gy", main_hi, main_lo)
+    hi, lo, layers = call(pack_x_kernel, [faces, faces, (26, CX, CY)], [], 3, True)(pos, fields, b)
+    other_layers = lax.ppermute(layers, "gz", swap)
+    hi = jnp.concatenate([hi, main_high[CX - 4:], main_low[CX - 4:]], axis=0)
+    lo = jnp.concatenate([lo, main_high[:4], main_low[:4]], axis=0)
+    hi, lo, main_high, main_low, gate = lax.optimization_barrier((hi, lo, main_high, main_low, pos))
     x_high, x_low = exchange("gx", hi, lo)
-    other_layers = lax.ppermute(layers, "gz", swap)
+    other_main = lax.ppermute(jnp.concatenate([main_high, main_low], axis=0), "gz", swap)
     part, = call(gram_kernel, [(44 * 8, 128)], [], 3, True)(gate, fields, b)
-    y_high, y_low, x_high, x_low, other_layers, part = lax.optimization_barrier(
-        (y_high, y_low, x_high, x_low, other_layers, part))
-    other_yh = lax.ppermute(y_high, "gz", swap)
-    other_yl = lax.ppermute(y_low, "gz", swap)
+    x_high, x_low, other_layers, other_main, part = lax.optimization_barrier(
+        (x_high, x_low, other_layers, other_main, part))
     other_xh = lax.ppermute(x_high[FIELD_ROW:], "gz", swap)
     other_xl = lax.ppermute(x_low[FIELD_ROW:], "gz", swap)
+
+    def with_corners(main, high, low, row):
+        return jnp.concatenate([main, high[row:row + 4], low[row:row + 4]], axis=0)
+
+    y_high = with_corners(main_high, x_high, x_low, CORNER_ROW)
+    y_low = with_corners(main_low, x_high, x_low, CORNER_ROW + 4)
+    other_yh = with_corners(other_main[:CX], other_xh, other_xl, CORNER_ROW - FIELD_ROW)
+    other_yl = with_corners(other_main[CX:], other_xh, other_xl, CORNER_ROW - FIELD_ROW + 4)
 
     ext = (EZ, EX, EY)
     pay, r_ext, wx, wy, wz, dg, iv, s, u = call(
         prepare_kernel, [(2, 128)] + [ext] * 8, [ext, ext, ext, (2048, 128)], 17, True,
     )(pos, fields, part, b, other_layers, hi, lo, x_high, x_low, other_xh, other_xl,
-      y_hi, y_lo, y_high, y_low, other_yh, other_yl)
+      main_hi, main_lo, y_high, y_low, other_yh, other_yl)
     gathered = gather_rows(pay).reshape(NDEV, 256)
     sol, res, pre, refined, total, scal = call(
         coarse_kernel, [box] * 4 + [(1, 128)] * 2,

time: 82 us -> 79.5 us (0.970)
  blocking collectives: 41.4 us -> 39.2 us
  starting transfers between devices: 17.7 us -> 18.6 us
    all_to_all x2, blocking collectives: 41.4 us -> 39.2 us  [gather_rows(): return lax.all_to_all(rows, AXES, 0, 0, tiled=False)]
    ppermute x2 -> x1, starting transfers between devices: 0.51 us -> 2.38 us  [local(): lax.ppermute(jnp.concatenate([main_high, main_low], axis=0), 'gz', swap)]
    ppermute x3 -> x2, starting transfers between devices: 1.48 us -> 0.01 us  [exchange(): lax.ppermute(hi, axis, ring(axis, 1))]
    ppermute x1, starting transfers between devices: 2.14 us -> 3.62 us  [local(): other_xl = lax.ppermute(x_low[FIELD_ROW:], 'gz', swap)]
    ppermute x2 -> x1, waiting for transfers between devices: 1.09 us -> 0.01 us  [local(): lax.ppermute(jnp.concatenate([main_high, main_low], axis=0), 'gz', swap)]
    ppermute x1, starting transfers between devices: 2.1 us -> 1.04 us  [local(): other_layers = lax.ppermute(layers, 'gz', swap)]
    ppermute x3 -> x2, waiting for transfers between devices: 6 us -> 5.15 us  [exchange(): lax.ppermute(hi, axis, ring(axis, 1))]
    ppermute x1, waiting for transfers between devices: 0.01 us -> 0.83 us  [local(): other_xl = lax.ppermute(x_low[FIELD_ROW:], 'gz', swap)]
  transfers between devices with their start and end apart: 11 -> 8, of which waited for: 4 -> 4; matrix products, arithmetic and copies ran while one was open for 0% -> 0% of each run, Pallas kernels for 4% -> 4%
where the time goes in v4:
time: 79.5 us; the launch traced here: 79.4 us
  blocking collectives  39.2 us (49%)
  starting transfers between devices  18.6 us (23%)
  Pallas kernels  12.8 us (16%)
  waiting for transfers between devices  6.34 us (8%)
  other arithmetic  1.4 us (2%)
    all_to_all x2, blocking collectives, gather_rows(): return lax.all_to_all(rows, AXES, 0, 0, tiled=False)  39.2 us
    ppermute x2, starting transfers between devices, exchange(): lax.ppermute(lo, axis, ring(axis, -1))  11.5 us
    ppermute x2, waiting for transfers between devices, exchange(): lax.ppermute(hi, axis, ring(axis, 1))  5.15 us
    pallas_call x1, Pallas kernels, local(): call(coarse_kernel, [box] * 4 + [(1, 128)] * 2, [(2, 256, 128), (384, 256...  4.81 us
    ppermute x1, starting transfers between devices, local(): other_xl = lax.ppermute(x_low[FIELD_ROW:], 'gz', swap)  3.62 us
    pallas_call x1, Pallas kernels, local(): call(prepare_kernel, [(2, 128)] + [ext] * 8, [ext, ext, ext, (2048, 128)]...  2.73 us
    pallas_call x1, Pallas kernels, local(): part, = call(gram_kernel, [(44 * 8, 128)], [], 3, True)(gate, fields, b)  2.63 us
    ppermute x1, starting transfers between devices, local(): lax.ppermute(jnp.concatenate([main_high, main_low], axis=0), 'gz', swap)  2.38 us
  transfers between devices with their start and end apart: 8, of which 4 were waited for; matrix products, arithmetic and copies ran while one was open for 0% of the time, Pallas kernels for 4%

profile of v4, /device:TPU:1, one launch (start us, length us, event | category | flops | bytes accessed | tf_op | source)
XLA Modules:
  0.0 79.4 jit_solution(13181963832533897083)
XLA Ops:
  0.6 0.0 copy-start
  0.6 0.0 copy-start.1
  0.7 0.0 copy-start.2
  0.7 1.2 %convert_element_type.3.b_ref = f32[8,8,16,256]{3,2,1,0:T(8,128)S(1)} convert(bf16[8,8,16,256]{3,2,1,0:T(8,128)(2,1)} %param.7) | non-fusion elementwise | flops 262144 | bytes 1572864 | tf_op jit(solution)/shard_map/convert_element_type | solution.py:526
  1.9 0.1 pad_add_fusion.pos_ref
  2.0 0.0 copy-done
  2.0 1.0 %shard_map.68 = (f32[16,256]{1,0:T(8,128)S(1)}, f32[16,256]{1,0:T(8,128)S(1)}) custom-call(s32[3]{0:T(128)S(1)} %pad_add_fusion.pos_ref, f32[3,8,16,256]{3,2,1,0:T(8,128)S(1)} %pad_maximum_fusion.f_ref.f_in, f32[8,8,16,256]{3,2,1,0:T(8,128)S(1)} %convert_element_type.3.b_ref), custom_call_target="tpu_custom_call" | custom-call | tf_op jit(solution)/shard_map/pallas_call | solution.py:527
  3.1 6.5 %collective-permute-start = (f32[16,256]{1,0:T(8,128)S(1)}, f32[16,256]{1,0:T(8,128)S(1)}, u32[]{:S(2)}, u32[]{:S(2)}) collective-permute-start(f32[16,256]{1,0:T(8,128)S(1)} %get-tuple-element.34.ys_lo_ref), channel_id=1, source_target_pairs={{0,14},{2,0},{4,2},{6,4},{8,6},{10,8},{12,10},{14,12},{1,15},{3,1}... | collective-permute-start | bytes 49160 | tf_op jit(solution)/shard_map/ppermute | solution.py:522
  9.5 0.0 collective-permute-start.1
  9.6 0.7 shard_map.67
  10.3 1.0 %collective-permute-start.4 = (f32[26,16,256]{2,1,0:T(8,128)S(1)}, f32[26,16,256]{2,1,0:T(8,128)S(1)}, u32[]{:S(2)}, u32[]{:S(2)}) collective-permute-start(f32[26,16,256]{2,1,0:T(8,128)S(1)} %get-tuple-element.39), channel_id=1, source_target_pairs={{0,1},{1,0},{2,3},{3,2},{4,5},{5,4},{6,7},{7,6},{8,9},{9,8},{10,11... | collective-permute-start | bytes 1277960 | tf_op jit(solution)/shard_map/ppermute | solution.py:530
  11.3 0.0 collective-permute-done
  11.3 2.0 %collective-permute-done.1 = f32[16,256]{1,0:T(8,128)S(1)} collective-permute-done((f32[16,256]{1,0:T(8,128)S(1)}, f32[16,256]{1,0:T(8,128)S(1)}, u32[]{:S(2)}, u32[]{:S(2)}) %collective-permute-start.1) | collective-permute-done | bytes 16416 | tf_op jit(solution)/shard_map/ppermute | solution.py:522
  13.4 5.0 %collective-permute-start.2 = (f32[224,256]{1,0:T(8,128)S(1)}, f32[224,256]{1,0:T(8,128)S(1)}, u32[]{:S(2)}, u32[]{:S(2)}) collective-permute-start(f32[224,256]{1,0:T(8,128)S(1)} %get-tuple-element.37.lo_ref), channel_id=1, source_target_pairs={{0,240},{16,0},{32,16},{48,32},{64,48},{80,64},{96,80},{112,96},{1... | collective-permute-start | bytes 688136 | tf_op jit(solution)/shard_map/ppermute | solution.py:522
  18.4 0.0 collective-permute-start.3
  18.4 2.4 %collective-permute-start.5 = (f32[32,256]{1,0:T(8,128)S(1)}, f32[32,256]{1,0:T(8,128)S(1)}, u32[]{:S(2)}, u32[]{:S(2)}) collective-permute-start(f32[32,256]{1,0:T(8,128)S(1)} %pad_maximum_fusion.3), channel_id=1, source_target_pairs={{0,1},{1,0},{2,3},{3,2},{4,5},{5,4},{6,7},{7,6},{8,9},{9,8},{10,11... | collective-permute-start | bytes 98312 | tf_op jit(solution)/shard_map/ppermute | solution.py:535
  20.8 2.6 %shard_map.69.part_ref = f32[352,128]{1,0:T(8,128)S(1)} custom-call(s32[3]{0:T(128)S(1)} %pad_add_fusion.pos_ref, f32[3,8,16,256]{3,2,1,0:T(8,128)S(1)} %pad_maximum_fusion.f_ref.f_in, f32[8,8,16,256]{3,2,1,0:T(8,128)S(1)} %convert_element_type.3.b_ref), custom_call_target="tpu_custom_call" | custom-call | tf_op jit(solution)/shard_map/pallas_call | solution.py:536
  23.4 0.0 collective-permute-done.5
  23.4 0.0 collective-permute-done.2.xh_ref
  23.4 3.1 %collective-permute-done.3.xl_ref = f32[224,256]{1,0:T(8,128)S(1)} collective-permute-done((f32[224,256]{1,0:T(8,128)S(1)}, f32[224,256]{1,0:T(8,128)S(1)}, u32[]{:S(2)}, u32[]{:S(2)}) %collective-permute-start.3) | collective-permute-done | bytes 229408 | tf_op jit(solution)/shard_map/ppermute | solution.py:522
  26.6 0.0 collective-permute-done.4.q_ref.q_in
  26.7 3.6 %collective-permute-start.7 = (f32[96,256]{1,0:T(8,128)S(1)}, f32[96,256]{1,0:T(8,128)S(1)}, u32[]{:S(2)}, u32[]{:S(2)}) collective-permute-start(f32[96,256]{1,0:T(8,128)S(1)} %slice.53), channel_id=1, source_target_pairs={{0,1},{1,0},{2,3},{3,2},{4,5},{5,4},{6,7},{7,6},{8,9},{9,8},{10,11... | collective-permute-start | bytes 294920 | tf_op jit(solution)/shard_map/ppermute | solution.py:540
  30.3 0.1 collective-permute-start.6
  30.4 0.8 %collective-permute-done.7.xlq_ref = f32[96,256]{1,0:T(8,128)S(1)} collective-permute-done((f32[96,256]{1,0:T(8,128)S(1)}, f32[96,256]{1,0:T(8,128)S(1)}, u32[]{:S(2)}, u32[]{:S(2)}) %collective-permute-start.7) | collective-permute-done | bytes 98336 | tf_op jit(solution)/shard_map/ppermute | solution.py:540
  31.2 0.4 collective-permute-done.6.xhq_ref
  31.6 2.7 %shard_map.70 = (f32[2,128]{1,0:T(2,128)S(1)}, f32[12,24,384]{2,1,0:T(8,128)S(1)}, f32[12,24,384]{2,1,0:T(8,128)S(1)}, f32[12,24,384]{2,1,0:T(8,128)S(1)}, f32[1...) custom-call(s32[3]{0:T(128)S(1)} %pad_add_fusion.pos_ref, ...), custom_call_target="tpu_custom_call" | custom-call | tf_op jit(solution)/shard_map/pallas_call | solution.py:551
  34.3 0.1 broadcast_in_dim.6
  34.4 21.0 %all_to_all.10 = f32[256,2,128]{2,1,0:T(2,128)S(1)} all-to-all(f32[256,2,128]{2,1,0:T(2,128)S(1)} %broadcast_in_dim.6), channel_id=1, replica_groups=mesh['gx'=16,'gy'=8,'gz'=2] {'gx','gy','gz'}, dimensions={0} | all-to-all | bytes 524288 | tf_op jit(solution)/shard_map/all_to_all | solution.py:514
  55.4 4.8 %shard_map.71 = (f32[8,16,256]{2,1,0:T(8,128)}, f32[8,16,256]{2,1,0:T(8,128)}, f32[8,16,256]{2,1,0:T(8,128)S(1)}, f32[8,16,256]{2,1,0:T(8,128)S(1)}, f32[1,128]{1,0:T(1,128)S(1)}, /*index=5*/f32[1,128]{1,0:T(1,128)S(1)}) custom-call(s32[3]{0:T(128)S(1)} %pad_add_fusion.pos_ref, f32[256,256]{1,0:T(8,128)S(1)} %bitcast.12, ...), custom_call_target="tpu_custom_call" | custom-call | tf_op jit(solution)/shard_map/pallas_call | solution.py:556
  60.2 0.1 broadcast_in_dim.16
  60.3 18.2 %all_to_all.11 = f32[256,1,128]{2,1,0:T(1,128)S(1)} all-to-all(f32[256,1,128]{2,1,0:T(1,128)S(1)} %broadcast_in_dim.16), channel_id=1, replica_groups=mesh['gx'=16,'gy'=8,'gz'=2] {'gx','gy','gz'}, dimensions={0} | all-to-all | bytes 262144 | tf_op jit(solution)/shard_map/all_to_all | solution.py:514
  78.5 0.9 %shard_map.72 = f32[8,16,256]{2,1,0:T(8,128)} custom-call(f32[256,128]{1,0:T(8,128)S(1)} %bitcast.13, f32[1,128]{1,0:T(1,128)S(1)} %get-tuple-element.60.scal_ref, f32[8,16,256]{2,1,0:T(8,128)S(1)} %get-tuple-element.61.refined_ref, f32[8,16,256]{2,1,0:T(8,128)S(1)} %get-tuple-element.62.pre_ref), custom_call_target="tpu_custom_call" | custom-call | tf_op jit(solution)/shard_map/pallas_call | solution.py:562
  (19 shorter events, 0.2 us)
Async XLA Ops:
  0.6 1.3 %copy-start = (f32[8,16,256]{2,1,0:T(8,128)S(1)}, f32[8,16,256]{2,1,0:T(8,128)}, u32[]{:S(2)}) copy-start(f32[8,16,256]{2,1,0:T(8,128)} %param.4) | copy-start | bytes 393220
  0.6 1.3 %copy-start.1 = (f32[8,16,256]{2,1,0:T(8,128)S(1)}, f32[8,16,256]{2,1,0:T(8,128)}, u32[]{:S(2)}) copy-start(f32[8,16,256]{2,1,0:T(8,128)} %param.6) | copy-start | bytes 393220
  0.7 1.3 %copy-start.2 = (f32[8,16,256]{2,1,0:T(8,128)S(1)}, f32[8,16,256]{2,1,0:T(8,128)}, u32[]{:S(2)}) copy-start(f32[8,16,256]{2,1,0:T(8,128)} %param.5) | copy-start | bytes 393220
  3.1 8.3 %collective-permute-start = (f32[16,256]{1,0:T(8,128)S(1)}, f32[16,256]{1,0:T(8,128)S(1)}, u32[]{:S(2)}, u32[]{:S(2)}) collective-permute-start(f32[16,256]{1,0:T(8,128)S(1)} %get-tuple-element.34.ys_lo_ref), channel_id=1, source_target_pairs={{0,14},{2,0},{4,2},{6,4},{8,6},{10,8},{12,10},{14,12},{1,15},{3,1}... | collective-permute-start | bytes 49160 | tf_op jit(solution)/shard_map/ppermute | solution.py:522
  9.5 3.8 %collective-permute-start.1 = (f32[16,256]{1,0:T(8,128)S(1)}, f32[16,256]{1,0:T(8,128)S(1)}, u32[]{:S(2)}, u32[]{:S(2)}) collective-permute-start(f32[16,256]{1,0:T(8,128)S(1)} %get-tuple-element.35.ys_hi_ref), channel_id=1, source_target_pairs={{0,2},{2,4},{4,6},{6,8},{8,10},{10,12},{12,14},{14,0},{1,3},{3,5},... | collective-permute-start | bytes 49160 | tf_op jit(solution)/shard_map/ppermute | solution.py:522
  10.3 16.3 %collective-permute-start.4 = (f32[26,16,256]{2,1,0:T(8,128)S(1)}, f32[26,16,256]{2,1,0:T(8,128)S(1)}, u32[]{:S(2)}, u32[]{:S(2)}) collective-permute-start(f32[26,16,256]{2,1,0:T(8,128)S(1)} %get-tuple-element.39), channel_id=1, source_target_pairs={{0,1},{1,0},{2,3},{3,2},{4,5},{5,4},{6,7},{7,6},{8,9},{9,8},{10,11... | collective-permute-start | bytes 1277960 | tf_op jit(solution)/shard_map/ppermute | solution.py:530
  13.4 10.0 %collective-permute-start.2 = (f32[224,256]{1,0:T(8,128)S(1)}, f32[224,256]{1,0:T(8,128)S(1)}, u32[]{:S(2)}, u32[]{:S(2)}) collective-permute-start(f32[224,256]{1,0:T(8,128)S(1)} %get-tuple-element.37.lo_ref), channel_id=1, source_target_pairs={{0,240},{16,0},{32,16},{48,32},{64,48},{80,64},{96,80},{112,96},{1... | collective-permute-start | bytes 688136 | tf_op jit(solution)/shard_map/ppermute | solution.py:522
  18.4 8.2 %collective-permute-start.3 = (f32[224,256]{1,0:T(8,128)S(1)}, f32[224,256]{1,0:T(8,128)S(1)}, u32[]{:S(2)}, u32[]{:S(2)}) collective-permute-start(f32[224,256]{1,0:T(8,128)S(1)} %get-tuple-element.38.hi_ref), channel_id=1, source_target_pairs={{0,16},{16,32},{32,48},{48,64},{64,80},{80,96},{96,112},{112,128},... | collective-permute-start | bytes 688136 | tf_op jit(solution)/shard_map/ppermute | solution.py:522
  18.4 5.0 %collective-permute-start.5 = (f32[32,256]{1,0:T(8,128)S(1)}, f32[32,256]{1,0:T(8,128)S(1)}, u32[]{:S(2)}, u32[]{:S(2)}) collective-permute-start(f32[32,256]{1,0:T(8,128)S(1)} %pad_maximum_fusion.3), channel_id=1, source_target_pairs={{0,1},{1,0},{2,3},{3,2},{4,5},{5,4},{6,7},{7,6},{8,9},{9,8},{10,11... | collective-permute-start | bytes 98312 | tf_op jit(solution)/shard_map/ppermute | solution.py:535
  26.7 4.6 %collective-permute-start.7 = (f32[96,256]{1,0:T(8,128)S(1)}, f32[96,256]{1,0:T(8,128)S(1)}, u32[]{:S(2)}, u32[]{:S(2)}) collective-permute-start(f32[96,256]{1,0:T(8,128)S(1)} %slice.53), channel_id=1, source_target_pairs={{0,1},{1,0},{2,3},{3,2},{4,5},{5,4},{6,7},{7,6},{8,9},{9,8},{10,11... | collective-permute-start | bytes 294920 | tf_op jit(solution)/shard_map/ppermute | solution.py:540
  30.3 1.3 %collective-permute-start.6 = (f32[96,256]{1,0:T(8,128)S(1)}, f32[96,256]{1,0:T(8,128)S(1)}, u32[]{:S(2)}, u32[]{:S(2)}) collective-permute-start(f32[96,256]{1,0:T(8,128)S(1)} %slice.52), channel_id=1, source_target_pairs={{0,1},{1,0},{2,3},{3,2},{4,5},{5,4},{6,7},{7,6},{8,9},{9,8},{10,11... | collective-permute-start | bytes 294920 | tf_op jit(solution)/shard_map/ppermute | solution.py:539

commit v5 on v4

--- a/solution.py
+++ b/solution.py
@@ -483,12 +483,6 @@
     scal_ref[...] = jnp.where(spot == 0, g2c2, rz)
 
 
-def finish_kernel(parts_ref, scal_ref, refined_ref, pre_ref, out_ref):
-    growth = (total_of(parts_ref[...]) + scal_ref[:, 0:1]) / scal_ref[:, 1:2]
-    for z in range(CZ):
-        out_ref[z] = refined_ref[z] + growth * pre_ref[z]
-
-
 def call(kernel, out_shapes, scratch, n_args, smem_first=False):
     whole = pl.BlockSpec(memory_space=pltpu.VMEM)
     specs = [whole] * n_args
@@ -558,8 +552,8 @@
         [(2, 256, 128), (384, 256), ext, ext], 20, True,
     )(pos, gathered, r_ext, b, other_layers, x_high, x_low, other_xh, other_xl,
       y_high, y_low, other_yh, other_yl, wx, wy, wz, dg, iv, s, u)
-    parts = gather_rows(total).reshape(NDEV, 128)
-    direction, = call(finish_kernel, [box], [], 4)(parts, scal, refined, pre)
+    growth = (jnp.sum(gather_rows(total)) + scal[0, 0]) / scal[0, 1]
+    direction = refined + growth * pre
     return sol, res, direction
 
 

time: 79.5 us -> 82.8 us (1.042)
  blocking collectives: 39.2 us -> 21 us
  waiting for transfers between devices: 6.34 us -> 18.7 us
  starting transfers between devices: 18.6 us -> 24.1 us
  between operations: 0.79 us -> 2.73 us
  other arithmetic: 1.4 us -> 2.71 us
  local copies, waits for them, and re-layouts: 0.22 us -> 1.52 us
  Pallas kernels: 12.8 us -> 11.9 us
    all_to_all x2 -> x1, blocking collectives: 39.2 us -> 21 us  [gather_rows(): return lax.all_to_all(rows, AXES, 0, 0, tiled=False)]
    all_to_all x0 -> x1, waiting for transfers between devices: none -> 12.4 us  [gather_rows(): return lax.all_to_all(rows, AXES, 0, 0, tiled=False)]
    all_to_all x0 -> x1, starting transfers between devices: none -> 5.46 us  [gather_rows(): return lax.all_to_all(rows, AXES, 0, 0, tiled=False)]
    pallas_call x1 -> x0, Pallas kernels: 0.85 us -> none  [local(): direction, = call(finish_kernel, [box], [], 4)(parts, scal, refined, pre)]
  transfers between devices with their start and end apart: 8 -> 9, of which waited for: 4 -> 5; matrix products, arithmetic and copies ran while one was open for 0% -> 1% of each run, Pallas kernels for 4% -> 4%
where the time goes in v5:
time: 82.8 us; the launch traced here: 82.6 us
  starting transfers between devices  24.1 us (29%)
  blocking collectives  21 us (25%)
  waiting for transfers between devices  18.7 us (23%)
  Pallas kernels  11.9 us (14%)
  between operations  2.73 us (3%)
  other arithmetic  2.71 us (3%)
  local copies, waits for them, and re-layouts  1.52 us (2%)
    all_to_all x1, blocking collectives, gather_rows(): return lax.all_to_all(rows, AXES, 0, 0, tiled=False)  21 us
    all_to_all x1, waiting for transfers between devices, gather_rows(): return lax.all_to_all(rows, AXES, 0, 0, tiled=False)  12.4 us
    ppermute x2, starting transfers between devices, exchange(): lax.ppermute(lo, axis, ring(axis, -1))  11.5 us
    all_to_all x1, starting transfers between devices, gather_rows(): return lax.all_to_all(rows, AXES, 0, 0, tiled=False)  5.46 us
    ppermute x2, waiting for transfers between devices, exchange(): lax.ppermute(hi, axis, ring(axis, 1))  5.15 us
    pallas_call x1, Pallas kernels, local(): call(coarse_kernel, [box] * 4 + [(1, 128)] * 2, [(2, 256, 128), (384, 256...  4.81 us
    ppermute x1, starting transfers between devices, local(): other_xl = lax.ppermute(x_low[FIELD_ROW:], 'gz', swap)  3.62 us
    pallas_call x1, Pallas kernels, local(): call(prepare_kernel, [(2, 128)] + [ext] * 8, [ext, ext, ext, (2048, 128)]...  2.73 us
  transfers between devices with their start and end apart: 9, of which 5 were waited for; matrix products, arithmetic and copies ran while one was open for 1% of the time, Pallas kernels for 4%

profile of v5, /device:TPU:1, one launch (start us, length us, event | category | flops | bytes accessed | tf_op | source)
XLA Modules:
  0.0 82.6 jit_solution(1609182508127560982)
XLA Ops:
  0.6 0.0 copy-start
  0.7 1.2 %convert_element_type.3.b_ref = f32[8,8,16,256]{3,2,1,0:T(8,128)S(1)} convert(bf16[8,8,16,256]{3,2,1,0:T(8,128)(2,1)} %param.7) | non-fusion elementwise | flops 262144 | bytes 1572864 | tf_op jit(solution)/shard_map/convert_element_type | solution.py:520
  1.9 0.1 pad_add_fusion.pos_ref
  2.0 1.0 %shard_map.68 = (f32[16,256]{1,0:T(8,128)S(1)}, f32[16,256]{1,0:T(8,128)S(1)}) custom-call(s32[3]{0:T(128)S(1)} %pad_add_fusion.pos_ref, f32[3,8,16,256]{3,2,1,0:T(8,128)S(1)} %pad_maximum_fusion.f_ref.f_in, f32[8,8,16,256]{3,2,1,0:T(8,128)S(1)} %convert_element_type.3.b_ref), custom_call_target="tpu_custom_call" | custom-call | tf_op jit(solution)/shard_map/pallas_call | solution.py:521
  3.1 6.5 %collective-permute-start = (f32[16,256]{1,0:T(8,128)S(1)}, f32[16,256]{1,0:T(8,128)S(1)}, u32[]{:S(2)}, u32[]{:S(2)}) collective-permute-start(f32[16,256]{1,0:T(8,128)S(1)} %get-tuple-element.34.ys_lo_ref), channel_id=1, source_target_pairs={{0,14},{2,0},{4,2},{6,4},{8,6},{10,8},{12,10},{14,12},{1,15},{3,1}... | collective-permute-start | bytes 49160 | tf_op jit(solution)/shard_map/ppermute | solution.py:516
  9.5 0.0 collective-permute-start.1
  9.6 0.7 shard_map.67
  10.3 1.0 %collective-permute-start.4 = (f32[26,16,256]{2,1,0:T(8,128)S(1)}, f32[26,16,256]{2,1,0:T(8,128)S(1)}, u32[]{:S(2)}, u32[]{:S(2)}) collective-permute-start(f32[26,16,256]{2,1,0:T(8,128)S(1)} %get-tuple-element.39), channel_id=1, source_target_pairs={{0,1},{1,0},{2,3},{3,2},{4,5},{5,4},{6,7},{7,6},{8,9},{9,8},{10,11... | collective-permute-start | bytes 1277960 | tf_op jit(solution)/shard_map/ppermute | solution.py:524
  11.3 0.0 collective-permute-done
  11.3 2.0 %collective-permute-done.1 = f32[16,256]{1,0:T(8,128)S(1)} collective-permute-done((f32[16,256]{1,0:T(8,128)S(1)}, f32[16,256]{1,0:T(8,128)S(1)}, u32[]{:S(2)}, u32[]{:S(2)}) %collective-permute-start.1) | collective-permute-done | bytes 16416 | tf_op jit(solution)/shard_map/ppermute | solution.py:516
  13.4 5.0 %collective-permute-start.2 = (f32[224,256]{1,0:T(8,128)S(1)}, f32[224,256]{1,0:T(8,128)S(1)}, u32[]{:S(2)}, u32[]{:S(2)}) collective-permute-start(f32[224,256]{1,0:T(8,128)S(1)} %get-tuple-element.37.lo_ref), channel_id=1, source_target_pairs={{0,240},{16,0},{32,16},{48,32},{64,48},{80,64},{96,80},{112,96},{1... | collective-permute-start | bytes 688136 | tf_op jit(solution)/shard_map/ppermute | solution.py:516
  18.4 0.0 collective-permute-start.3
  18.4 2.4 %collective-permute-start.5 = (f32[32,256]{1,0:T(8,128)S(1)}, f32[32,256]{1,0:T(8,128)S(1)}, u32[]{:S(2)}, u32[]{:S(2)}) collective-permute-start(f32[32,256]{1,0:T(8,128)S(1)} %pad_maximum_fusion.3), channel_id=1, source_target_pairs={{0,1},{1,0},{2,3},{3,2},{4,5},{5,4},{6,7},{7,6},{8,9},{9,8},{10,11... | collective-permute-start | bytes 98312 | tf_op jit(solution)/shard_map/ppermute | solution.py:529
  20.8 2.6 %shard_map.69.part_ref = f32[352,128]{1,0:T(8,128)S(1)} custom-call(s32[3]{0:T(128)S(1)} %pad_add_fusion.pos_ref, f32[3,8,16,256]{3,2,1,0:T(8,128)S(1)} %pad_maximum_fusion.f_ref.f_in, f32[8,8,16,256]{3,2,1,0:T(8,128)S(1)} %convert_element_type.3.b_ref), custom_call_target="tpu_custom_call" | custom-call | tf_op jit(solution)/shard_map/pallas_call | solution.py:530
  23.4 0.0 collective-permute-done.5
  23.4 0.0 collective-permute-done.2.xh_ref
  23.4 3.1 %collective-permute-done.3.xl_ref = f32[224,256]{1,0:T(8,128)S(1)} collective-permute-done((f32[224,256]{1,0:T(8,128)S(1)}, f32[224,256]{1,0:T(8,128)S(1)}, u32[]{:S(2)}, u32[]{:S(2)}) %collective-permute-start.3) | collective-permute-done | bytes 229408 | tf_op jit(solution)/shard_map/ppermute | solution.py:516
  26.6 0.0 collective-permute-done.4.q_ref.q_in
  26.7 3.6 %collective-permute-start.7 = (f32[96,256]{1,0:T(8,128)S(1)}, f32[96,256]{1,0:T(8,128)S(1)}, u32[]{:S(2)}, u32[]{:S(2)}) collective-permute-start(f32[96,256]{1,0:T(8,128)S(1)} %slice.59), channel_id=1, source_target_pairs={{0,1},{1,0},{2,3},{3,2},{4,5},{5,4},{6,7},{7,6},{8,9},{9,8},{10,11... | collective-permute-start | bytes 294920 | tf_op jit(solution)/shard_map/ppermute | solution.py:534
  30.3 0.1 collective-permute-start.6
  30.4 0.8 %collective-permute-done.7.xlq_ref = f32[96,256]{1,0:T(8,128)S(1)} collective-permute-done((f32[96,256]{1,0:T(8,128)S(1)}, f32[96,256]{1,0:T(8,128)S(1)}, u32[]{:S(2)}, u32[]{:S(2)}) %collective-permute-start.7) | collective-permute-done | bytes 98336 | tf_op jit(solution)/shard_map/ppermute | solution.py:534
  31.2 0.4 collective-permute-done.6.xhq_ref
  31.6 2.7 %shard_map.70 = (f32[2,128]{1,0:T(2,128)S(1)}, f32[12,24,384]{2,1,0:T(8,128)S(1)}, f32[12,24,384]{2,1,0:T(8,128)S(1)}, f32[12,24,384]{2,1,0:T(8,128)S(1)}, f32[1...) custom-call(s32[3]{0:T(128)S(1)} %pad_add_fusion.pos_ref, ...), custom_call_target="tpu_custom_call" | custom-call | tf_op jit(solution)/shard_map/pallas_call | solution.py:545
  34.3 0.1 broadcast_in_dim.6
  34.4 21.0 %all_to_all.10 = f32[256,2,128]{2,1,0:T(2,128)S(1)} all-to-all(f32[256,2,128]{2,1,0:T(2,128)S(1)} %broadcast_in_dim.6), channel_id=1, replica_groups=mesh['gx'=16,'gy'=8,'gz'=2] {'gx','gy','gz'}, dimensions={0} | all-to-all | bytes 524288 | tf_op jit(solution)/shard_map/all_to_all | solution.py:508
  55.4 4.8 %shard_map.71 = (f32[8,16,256]{2,1,0:T(8,128)}, f32[8,16,256]{2,1,0:T(8,128)}, f32[8,16,256]{2,1,0:T(8,128)S(1)}, f32[8,16,256]{2,1,0:T(8,128)S(1)}, f32[1,128]{1,0:T(1,128)S(1)}, /*index=5*/f32[1,128]{1,0:T(1,128)S(1)}) custom-call(s32[3]{0:T(128)S(1)} %pad_add_fusion.pos_ref, f32[256,256]{1,0:T(8,128)S(1)} %bitcast.14, ...), custom_call_target="tpu_custom_call" | custom-call | tf_op jit(solution)/shard_map/pallas_call | solution.py:550
  60.2 0.7 broadcast_in_dim.16
  60.9 5.5 %all-to-all-start.1 = ((f32[256,1,128]{2,1,0:T(1,128)}), f32[256,1,128]{2,1,0:T(1,128)S(1)}, u32[]{:S(2)}, u32[]{:S(2)}) async-start(f32[256,1,128]{2,1,0:T(1,128)} %broadcast_in_dim.16), calls=%async_computation.1 | async-start | bytes 262144 | tf_op jit(solution)/shard_map/all_to_all | solution.py:508
  66.4 0.6 fusion.7
  67.1 12.4 %all-to-all-done.1 = f32[256,1,128]{2,1,0:T(1,128)S(1)} async-done(((f32[256,1,128]{2,1,0:T(1,128)}), f32[256,1,128]{2,1,0:T(1,128)S(1)}, u32[]{:S(2)}, u32[]{:S(2)}) %all-to-all-start.1) | async-done | bytes 131104 | tf_op jit(solution)/shard_map/all_to_all | solution.py:508
  79.4 0.6 reduce_sum.9
  82.0 0.7 multiply_add_fusion
  (22 shorter events, 0.2 us)
Async XLA Ops:
  0.6 1.3 %copy-start = (f32[8,16,256]{2,1,0:T(8,128)S(1)}, f32[8,16,256]{2,1,0:T(8,128)}, u32[]{:S(2)}) copy-start(f32[8,16,256]{2,1,0:T(8,128)} %param.4) | copy-start | bytes 393220
  0.6 1.3 %copy-start.1 = (f32[8,16,256]{2,1,0:T(8,128)S(1)}, f32[8,16,256]{2,1,0:T(8,128)}, u32[]{:S(2)}) copy-start(f32[8,16,256]{2,1,0:T(8,128)} %param.6) | copy-start | bytes 393220
  0.7 1.3 %copy-start.2 = (f32[8,16,256]{2,1,0:T(8,128)S(1)}, f32[8,16,256]{2,1,0:T(8,128)}, u32[]{:S(2)}) copy-start(f32[8,16,256]{2,1,0:T(8,128)} %param.5) | copy-start | bytes 393220
  3.1 8.3 %collective-permute-start = (f32[16,256]{1,0:T(8,128)S(1)}, f32[16,256]{1,0:T(8,128)S(1)}, u32[]{:S(2)}, u32[]{:S(2)}) collective-permute-start(f32[16,256]{1,0:T(8,128)S(1)} %get-tuple-element.34.ys_lo_ref), channel_id=1, source_target_pairs={{0,14},{2,0},{4,2},{6,4},{8,6},{10,8},{12,10},{14,12},{1,15},{3,1}... | collective-permute-start | bytes 49160 | tf_op jit(solution)/shard_map/ppermute | solution.py:516
  9.5 3.8 %collective-permute-start.1 = (f32[16,256]{1,0:T(8,128)S(1)}, f32[16,256]{1,0:T(8,128)S(1)}, u32[]{:S(2)}, u32[]{:S(2)}) collective-permute-start(f32[16,256]{1,0:T(8,128)S(1)} %get-tuple-element.35.ys_hi_ref), channel_id=1, source_target_pairs={{0,2},{2,4},{4,6},{6,8},{8,10},{10,12},{12,14},{14,0},{1,3},{3,5},... | collective-permute-start | bytes 49160 | tf_op jit(solution)/shard_map/ppermute | solution.py:516
  10.3 16.3 %collective-permute-start.4 = (f32[26,16,256]{2,1,0:T(8,128)S(1)}, f32[26,16,256]{2,1,0:T(8,128)S(1)}, u32[]{:S(2)}, u32[]{:S(2)}) collective-permute-start(f32[26,16,256]{2,1,0:T(8,128)S(1)} %get-tuple-element.39), channel_id=1, source_target_pairs={{0,1},{1,0},{2,3},{3,2},{4,5},{5,4},{6,7},{7,6},{8,9},{9,8},{10,11... | collective-permute-start | bytes 1277960 | tf_op jit(solution)/shard_map/ppermute | solution.py:524
  13.4 10.0 %collective-permute-start.2 = (f32[224,256]{1,0:T(8,128)S(1)}, f32[224,256]{1,0:T(8,128)S(1)}, u32[]{:S(2)}, u32[]{:S(2)}) collective-permute-start(f32[224,256]{1,0:T(8,128)S(1)} %get-tuple-element.37.lo_ref), channel_id=1, source_target_pairs={{0,240},{16,0},{32,16},{48,32},{64,48},{80,64},{96,80},{112,96},{1... | collective-permute-start | bytes 688136 | tf_op jit(solution)/shard_map/ppermute | solution.py:516
  18.4 8.2 %collective-permute-start.3 = (f32[224,256]{1,0:T(8,128)S(1)}, f32[224,256]{1,0:T(8,128)S(1)}, u32[]{:S(2)}, u32[]{:S(2)}) collective-permute-start(f32[224,256]{1,0:T(8,128)S(1)} %get-tuple-element.38.hi_ref), channel_id=1, source_target_pairs={{0,16},{16,32},{32,48},{48,64},{64,80},{80,96},{96,112},{112,128},... | collective-permute-start | bytes 688136 | tf_op jit(solution)/shard_map/ppermute | solution.py:516
  18.4 5.0 %collective-permute-start.5 = (f32[32,256]{1,0:T(8,128)S(1)}, f32[32,256]{1,0:T(8,128)S(1)}, u32[]{:S(2)}, u32[]{:S(2)}) collective-permute-start(f32[32,256]{1,0:T(8,128)S(1)} %pad_maximum_fusion.3), channel_id=1, source_target_pairs={{0,1},{1,0},{2,3},{3,2},{4,5},{5,4},{6,7},{7,6},{8,9},{9,8},{10,11... | collective-permute-start | bytes 98312 | tf_op jit(solution)/shard_map/ppermute | solution.py:529
  26.7 4.6 %collective-permute-start.7 = (f32[96,256]{1,0:T(8,128)S(1)}, f32[96,256]{1,0:T(8,128)S(1)}, u32[]{:S(2)}, u32[]{:S(2)}) collective-permute-start(f32[96,256]{1,0:T(8,128)S(1)} %slice.59), channel_id=1, source_target_pairs={{0,1},{1,0},{2,3},{3,2},{4,5},{5,4},{6,7},{7,6},{8,9},{9,8},{10,11... | collective-permute-start | bytes 294920 | tf_op jit(solution)/shard_map/ppermute | solution.py:534
  30.3 1.3 %collective-permute-start.6 = (f32[96,256]{1,0:T(8,128)S(1)}, f32[96,256]{1,0:T(8,128)S(1)}, u32[]{:S(2)}, u32[]{:S(2)}) collective-permute-start(f32[96,256]{1,0:T(8,128)S(1)} %slice.58), channel_id=1, source_target_pairs={{0,1},{1,0},{2,3},{3,2},{4,5},{5,4},{6,7},{7,6},{8,9},{9,8},{10,11... | collective-permute-start | bytes 294920 | tf_op jit(solution)/shard_map/ppermute | solution.py:533
  60.9 18.5 %all-to-all-start.1 = ((f32[256,1,128]{2,1,0:T(1,128)}), f32[256,1,128]{2,1,0:T(1,128)S(1)}, u32[]{:S(2)}, u32[]{:S(2)}) async-start(f32[256,1,128]{2,1,0:T(1,128)} %broadcast_in_dim.16), calls=%async_computation.1 | async-start | bytes 262144 | tf_op jit(solution)/shard_map/all_to_all | solution.py:508

commit v6 on v4

--- a/solution.py
+++ b/solution.py
@@ -536,8 +536,8 @@
     part, = call(gram_kernel, [(44 * 8, 128)], [], 3, True)(gate, fields, b)
     x_high, x_low, other_layers, other_main, part = lax.optimization_barrier(
         (x_high, x_low, other_layers, other_main, part))
-    other_xh = lax.ppermute(x_high[FIELD_ROW:], "gz", swap)
-    other_xl = lax.ppermute(x_low[FIELD_ROW:], "gz", swap)
+    other_x = lax.ppermute(jnp.concatenate([x_high[FIELD_ROW:], x_low[FIELD_ROW:]], axis=0), "gz", swap)
+    other_xh, other_xl = other_x[:CORNER_ROW + 8 - FIELD_ROW], other_x[CORNER_ROW + 8 - FIELD_ROW:]
 
     def with_corners(main, high, low, row):
         return jnp.concatenate([main, high[row:row + 4], low[row:row + 4]], axis=0)

time: 79.5 us -> 79.6 us (level)
    ppermute x2 -> x1, starting transfers between devices: 3.72 us -> 3.62 us  [local(): lax.ppermute(jnp.concatenate([x_high[FIELD_ROW:], x_low[FIELD_ROW:]], axi...]
  transfers between devices with their start and end apart: 8 -> 7, of which waited for: 4 -> 3; matrix products, arithmetic and copies ran while one was open for 0% -> 0% of each run, Pallas kernels for 4% -> 4%
where the time goes in v6:
time: 79.6 us; the launch traced here: 79.4 us
  blocking collectives  39.4 us (49%)
  starting transfers between devices  18.5 us (23%)
  Pallas kernels  12.8 us (16%)
  waiting for transfers between devices  6.2 us (8%)
  other arithmetic  1.42 us (2%)
  between operations  0.8 us (1%)
    all_to_all x2, blocking collectives, gather_rows(): return lax.all_to_all(rows, AXES, 0, 0, tiled=False)  39.4 us
    ppermute x2, starting transfers between devices, exchange(): lax.ppermute(lo, axis, ring(axis, -1))  11.5 us
    ppermute x2, waiting for transfers between devices, exchange(): lax.ppermute(hi, axis, ring(axis, 1))  5.15 us
    pallas_call x1, Pallas kernels, local(): call(coarse_kernel, [box] * 4 + [(1, 128)] * 2, [(2, 256, 128), (384, 256...  4.81 us
    ppermute x1, starting transfers between devices, local(): lax.ppermute(jnp.concatenate([x_high[FIELD_ROW:], x_low[FIELD_ROW:]], axi...  3.62 us
    pallas_call x1, Pallas kernels, local(): call(prepare_kernel, [(2, 128)] + [ext] * 8, [ext, ext, ext, (2048, 128)]...  2.73 us
    pallas_call x1, Pallas kernels, local(): part, = call(gram_kernel, [(44 * 8, 128)], [], 3, True)(gate, fields, b)  2.63 us
    ppermute x1, starting transfers between devices, local(): lax.ppermute(jnp.concatenate([main_high, main_low], axis=0), 'gz', swap)  2.38 us
  transfers between devices with their start and end apart: 7, of which 3 were waited for; matrix products, arithmetic and copies ran while one was open for 0% of the time, Pallas kernels for 4%

profile of v6, /device:TPU:1, one launch (start us, length us, event | category | flops | bytes accessed | tf_op | source)
XLA Modules:
  0.0 79.4 jit_solution(13998769772868571183)
XLA Ops:
  0.6 0.0 copy-start
  0.6 0.0 copy-start.1
  0.7 0.0 copy-start.2
  0.7 1.2 %convert_element_type.3.b_ref = f32[8,8,16,256]{3,2,1,0:T(8,128)S(1)} convert(bf16[8,8,16,256]{3,2,1,0:T(8,128)(2,1)} %param.7) | non-fusion elementwise | flops 262144 | bytes 1572864 | tf_op jit(solution)/shard_map/convert_element_type | solution.py:526
  1.9 0.1 pad_add_fusion.pos_ref
  2.0 0.0 copy-done
  2.0 0.0 copy-done.1
  2.0 0.0 copy-done.2
  2.0 1.0 %shard_map.68 = (f32[16,256]{1,0:T(8,128)S(1)}, f32[16,256]{1,0:T(8,128)S(1)}) custom-call(s32[3]{0:T(128)S(1)} %pad_add_fusion.pos_ref, f32[3,8,16,256]{3,2,1,0:T(8,128)S(1)} %pad_maximum_fusion.f_ref.f_in, f32[8,8,16,256]{3,2,1,0:T(8,128)S(1)} %convert_element_type.3.b_ref), custom_call_target="tpu_custom_call" | custom-call | tf_op jit(solution)/shard_map/pallas_call | solution.py:527
  3.1 6.5 %collective-permute-start = (f32[16,256]{1,0:T(8,128)S(1)}, f32[16,256]{1,0:T(8,128)S(1)}, u32[]{:S(2)}, u32[]{:S(2)}) collective-permute-start(f32[16,256]{1,0:T(8,128)S(1)} %get-tuple-element.34.ys_lo_ref), channel_id=1, source_target_pairs={{0,14},{2,0},{4,2},{6,4},{8,6},{10,8},{12,10},{14,12},{1,15},{3,1}... | collective-permute-start | bytes 49160 | tf_op jit(solution)/shard_map/ppermute | solution.py:522
  9.5 0.0 collective-permute-start.1
  9.6 0.7 shard_map.67
  10.3 1.0 %collective-permute-start.4 = (f32[26,16,256]{2,1,0:T(8,128)S(1)}, f32[26,16,256]{2,1,0:T(8,128)S(1)}, u32[]{:S(2)}, u32[]{:S(2)}) collective-permute-start(f32[26,16,256]{2,1,0:T(8,128)S(1)} %get-tuple-element.39), channel_id=1, source_target_pairs={{0,1},{1,0},{2,3},{3,2},{4,5},{5,4},{6,7},{7,6},{8,9},{9,8},{10,11... | collective-permute-start | bytes 1277960 | tf_op jit(solution)/shard_map/ppermute | solution.py:530
  11.3 0.0 collective-permute-done
  11.3 2.0 %collective-permute-done.1 = f32[16,256]{1,0:T(8,128)S(1)} collective-permute-done((f32[16,256]{1,0:T(8,128)S(1)}, f32[16,256]{1,0:T(8,128)S(1)}, u32[]{:S(2)}, u32[]{:S(2)}) %collective-permute-start.1) | collective-permute-done | bytes 16416 | tf_op jit(solution)/shard_map/ppermute | solution.py:522
  13.4 5.0 %collective-permute-start.2 = (f32[224,256]{1,0:T(8,128)S(1)}, f32[224,256]{1,0:T(8,128)S(1)}, u32[]{:S(2)}, u32[]{:S(2)}) collective-permute-start(f32[224,256]{1,0:T(8,128)S(1)} %get-tuple-element.37.lo_ref), channel_id=1, source_target_pairs={{0,240},{16,0},{32,16},{48,32},{64,48},{80,64},{96,80},{112,96},{1... | collective-permute-start | bytes 688136 | tf_op jit(solution)/shard_map/ppermute | solution.py:522
  18.4 0.0 collective-permute-start.3
  18.4 2.4 %collective-permute-start.5 = (f32[32,256]{1,0:T(8,128)S(1)}, f32[32,256]{1,0:T(8,128)S(1)}, u32[]{:S(2)}, u32[]{:S(2)}) collective-permute-start(f32[32,256]{1,0:T(8,128)S(1)} %pad_maximum_fusion.4), channel_id=1, source_target_pairs={{0,1},{1,0},{2,3},{3,2},{4,5},{5,4},{6,7},{7,6},{8,9},{9,8},{10,11... | collective-permute-start | bytes 98312 | tf_op jit(solution)/shard_map/ppermute | solution.py:535
  20.8 2.6 %shard_map.69.part_ref = f32[352,128]{1,0:T(8,128)S(1)} custom-call(s32[3]{0:T(128)S(1)} %pad_add_fusion.pos_ref, f32[3,8,16,256]{3,2,1,0:T(8,128)S(1)} %pad_maximum_fusion.f_ref.f_in, f32[8,8,16,256]{3,2,1,0:T(8,128)S(1)} %convert_element_type.3.b_ref), custom_call_target="tpu_custom_call" | custom-call | tf_op jit(solution)/shard_map/pallas_call | solution.py:536
  23.4 0.0 collective-permute-done.5
  23.4 0.0 collective-permute-done.2.xh_ref
  23.4 3.1 %collective-permute-done.3.xl_ref = f32[224,256]{1,0:T(8,128)S(1)} collective-permute-done((f32[224,256]{1,0:T(8,128)S(1)}, f32[224,256]{1,0:T(8,128)S(1)}, u32[]{:S(2)}, u32[]{:S(2)}) %collective-permute-start.3) | collective-permute-done | bytes 229408 | tf_op jit(solution)/shard_map/ppermute | solution.py:522
  26.6 0.0 collective-permute-done.4.q_ref.q_in
  26.7 3.6 %collective-permute-start.6 = (f32[192,256]{1,0:T(8,128)S(1)}, f32[192,256]{1,0:T(8,128)S(1)}, u32[]{:S(2)}, u32[]{:S(2)}) collective-permute-start(f32[192,256]{1,0:T(8,128)S(1)} %pad_maximum_fusion.3), channel_id=1, source_target_pairs={{0,1},{1,0},{2,3},{3,2},{4,5},{5,4},{6,7},{7,6},{8,9},{9,8},{10,11... | collective-permute-start | bytes 589832 | tf_op jit(solution)/shard_map/ppermute | solution.py:539
  30.3 1.0 %collective-permute-done.6 = f32[192,256]{1,0:T(8,128)S(1)} collective-permute-done((f32[192,256]{1,0:T(8,128)S(1)}, f32[192,256]{1,0:T(8,128)S(1)}, u32[]{:S(2)}, u32[]{:S(2)}) %collective-permute-start.6) | collective-permute-done | bytes 196640 | tf_op jit(solution)/shard_map/ppermute | solution.py:539
  31.4 2.7 %shard_map.70 = (f32[2,128]{1,0:T(2,128)S(1)}, f32[12,24,384]{2,1,0:T(8,128)S(1)}, f32[12,24,384]{2,1,0:T(8,128)S(1)}, f32[12,24,384]{2,1,0:T(8,128)S(1)}, f32[1...) custom-call(s32[3]{0:T(128)S(1)} %pad_add_fusion.pos_ref, ...), custom_call_target="tpu_custom_call" | custom-call | tf_op jit(solution)/shard_map/pallas_call | solution.py:551
  34.1 0.1 broadcast_in_dim.6
  34.2 21.2 %all_to_all.10 = f32[256,2,128]{2,1,0:T(2,128)S(1)} all-to-all(f32[256,2,128]{2,1,0:T(2,128)S(1)} %broadcast_in_dim.6), channel_id=1, replica_groups=mesh['gx'=16,'gy'=8,'gz'=2] {'gx','gy','gz'}, dimensions={0} | all-to-all | bytes 524288 | tf_op jit(solution)/shard_map/all_to_all | solution.py:514
  55.4 4.8 %shard_map.71 = (f32[8,16,256]{2,1,0:T(8,128)}, f32[8,16,256]{2,1,0:T(8,128)}, f32[8,16,256]{2,1,0:T(8,128)S(1)}, f32[8,16,256]{2,1,0:T(8,128)S(1)}, f32[1,128]{1,0:T(1,128)S(1)}, /*index=5*/f32[1,128]{1,0:T(1,128)S(1)}) custom-call(s32[3]{0:T(128)S(1)} %pad_add_fusion.pos_ref, f32[256,256]{1,0:T(8,128)S(1)} %bitcast.12, ...), custom_call_target="tpu_custom_call" | custom-call | tf_op jit(solution)/shard_map/pallas_call | solution.py:556
  60.2 0.1 broadcast_in_dim.16
  60.3 18.2 %all_to_all.11 = f32[256,1,128]{2,1,0:T(1,128)S(1)} all-to-all(f32[256,1,128]{2,1,0:T(1,128)S(1)} %broadcast_in_dim.16), channel_id=1, replica_groups=mesh['gx'=16,'gy'=8,'gz'=2] {'gx','gy','gz'}, dimensions={0} | all-to-all | bytes 262144 | tf_op jit(solution)/shard_map/all_to_all | solution.py:514
  78.5 0.9 %shard_map.72 = f32[8,16,256]{2,1,0:T(8,128)} custom-call(f32[256,128]{1,0:T(8,128)S(1)} %bitcast.13, f32[1,128]{1,0:T(1,128)S(1)} %get-tuple-element.60.scal_ref, f32[8,16,256]{2,1,0:T(8,128)S(1)} %get-tuple-element.61.refined_ref, f32[8,16,256]{2,1,0:T(8,128)S(1)} %get-tuple-element.62.pre_ref), custom_call_target="tpu_custom_call" | custom-call | tf_op jit(solution)/shard_map/pallas_call | solution.py:562
  (18 shorter events, 0.2 us)
Async XLA Ops:
  0.6 1.3 %copy-start = (f32[8,16,256]{2,1,0:T(8,128)S(1)}, f32[8,16,256]{2,1,0:T(8,128)}, u32[]{:S(2)}) copy-start(f32[8,16,256]{2,1,0:T(8,128)} %param.4) | copy-start | bytes 393220
  0.6 1.3 %copy-start.1 = (f32[8,16,256]{2,1,0:T(8,128)S(1)}, f32[8,16,256]{2,1,0:T(8,128)}, u32[]{:S(2)}) copy-start(f32[8,16,256]{2,1,0:T(8,128)} %param.6) | copy-start | bytes 393220
  0.7 1.3 %copy-start.2 = (f32[8,16,256]{2,1,0:T(8,128)S(1)}, f32[8,16,256]{2,1,0:T(8,128)}, u32[]{:S(2)}) copy-start(f32[8,16,256]{2,1,0:T(8,128)} %param.5) | copy-start | bytes 393220
  3.1 8.3 %collective-permute-start = (f32[16,256]{1,0:T(8,128)S(1)}, f32[16,256]{1,0:T(8,128)S(1)}, u32[]{:S(2)}, u32[]{:S(2)}) collective-permute-start(f32[16,256]{1,0:T(8,128)S(1)} %get-tuple-element.34.ys_lo_ref), channel_id=1, source_target_pairs={{0,14},{2,0},{4,2},{6,4},{8,6},{10,8},{12,10},{14,12},{1,15},{3,1}... | collective-permute-start | bytes 49160 | tf_op jit(solution)/shard_map/ppermute | solution.py:522
  9.5 3.8 %collective-permute-start.1 = (f32[16,256]{1,0:T(8,128)S(1)}, f32[16,256]{1,0:T(8,128)S(1)}, u32[]{:S(2)}, u32[]{:S(2)}) collective-permute-start(f32[16,256]{1,0:T(8,128)S(1)} %get-tuple-element.35.ys_hi_ref), channel_id=1, source_target_pairs={{0,2},{2,4},{4,6},{6,8},{8,10},{10,12},{12,14},{14,0},{1,3},{3,5},... | collective-permute-start | bytes 49160 | tf_op jit(solution)/shard_map/ppermute | solution.py:522
  10.3 16.3 %collective-permute-start.4 = (f32[26,16,256]{2,1,0:T(8,128)S(1)}, f32[26,16,256]{2,1,0:T(8,128)S(1)}, u32[]{:S(2)}, u32[]{:S(2)}) collective-permute-start(f32[26,16,256]{2,1,0:T(8,128)S(1)} %get-tuple-element.39), channel_id=1, source_target_pairs={{0,1},{1,0},{2,3},{3,2},{4,5},{5,4},{6,7},{7,6},{8,9},{9,8},{10,11... | collective-permute-start | bytes 1277960 | tf_op jit(solution)/shard_map/ppermute | solution.py:530
  13.4 10.0 %collective-permute-start.2 = (f32[224,256]{1,0:T(8,128)S(1)}, f32[224,256]{1,0:T(8,128)S(1)}, u32[]{:S(2)}, u32[]{:S(2)}) collective-permute-start(f32[224,256]{1,0:T(8,128)S(1)} %get-tuple-element.37.lo_ref), channel_id=1, source_target_pairs={{0,240},{16,0},{32,16},{48,32},{64,48},{80,64},{96,80},{112,96},{1... | collective-permute-start | bytes 688136 | tf_op jit(solution)/shard_map/ppermute | solution.py:522
  18.4 8.2 %collective-permute-start.3 = (f32[224,256]{1,0:T(8,128)S(1)}, f32[224,256]{1,0:T(8,128)S(1)}, u32[]{:S(2)}, u32[]{:S(2)}) collective-permute-start(f32[224,256]{1,0:T(8,128)S(1)} %get-tuple-element.38.hi_ref), channel_id=1, source_target_pairs={{0,16},{16,32},{32,48},{48,64},{64,80},{80,96},{96,112},{112,128},... | collective-permute-start | bytes 688136 | tf_op jit(solution)/shard_map/ppermute | solution.py:522
  18.4 5.0 %collective-permute-start.5 = (f32[32,256]{1,0:T(8,128)S(1)}, f32[32,256]{1,0:T(8,128)S(1)}, u32[]{:S(2)}, u32[]{:S(2)}) collective-permute-start(f32[32,256]{1,0:T(8,128)S(1)} %pad_maximum_fusion.4), channel_id=1, source_target_pairs={{0,1},{1,0},{2,3},{3,2},{4,5},{5,4},{6,7},{7,6},{8,9},{9,8},{10,11... | collective-permute-start | bytes 98312 | tf_op jit(solution)/shard_map/ppermute | solution.py:535
  26.7 4.7 %collective-permute-start.6 = (f32[192,256]{1,0:T(8,128)S(1)}, f32[192,256]{1,0:T(8,128)S(1)}, u32[]{:S(2)}, u32[]{:S(2)}) collective-permute-start(f32[192,256]{1,0:T(8,128)S(1)} %pad_maximum_fusion.3), channel_id=1, source_target_pairs={{0,1},{1,0},{2,3},{3,2},{4,5},{5,4},{6,7},{7,6},{8,9},{9,8},{10,11... | collective-permute-start | bytes 589832 | tf_op jit(solution)/shard_map/ppermute | solution.py:539
